TPU v7x, 256 devices: a whole 4x4x8 slice. The times are simulated.
256 devices in a mesh: row: 16 (over x, z_lo), col: 4 (over z_hi, core), hid: 4 (over y).
Axes of the slice: x: 4, y: 4, z: 8 (z_hi: 2, z_lo: 4; z = z_hi * 4 + z_lo), core: 2. Of those that a mesh axis runs over, the one named last changes fastest.
Arguments:
- features: bfloat16 [1024, 256, 512], P('hid', 'row', 'col'), may hold values from -6 to 6
- dw_kernel: float32 [1024, 7, 7], P('hid'), may hold values from -0.875 to 0.875
- dw_bias: float32 [1024], P('hid'), may hold values from -3 to 3
- norm_gain: float32 [1024], P('hid'), may hold values from 0.5 to 1.5
- norm_bias: float32 [1024], P('hid'), may hold values from -3 to 3
- w_in: bfloat16 [4096, 1024], P('hid'), may hold values from -0.1875 to 0.1875
- b_in: float32 [4096], P('hid'), may hold values from -3 to 3
- w_out: bfloat16 [4096, 1024], P('hid'), may hold values from -0.125 to 0.125
- b_out: float32 [1024], P('hid'), may hold values from -3 to 3
- layer_scale: float32 [1024], P('hid'), may hold values from 0.3 to 1.5
Outputs:
- block_out: bfloat16 [1024, 256, 512], P('hid', 'row', 'col')
All inputs are finite; a program needn't handle non-finite values.
Results may differ from a plain program's by a relative error of at most 0.013.
Values may be sent and summed in bfloat16 or wider, within the bound.
No kernel may reach another device: no remote copies, remote signals or barrier semaphores. Data moves between devices by JAX's collectives and lax.ppermute only.
A program may use at most 128 MiB of HBM per device.

v0:
```python
import jax
import jax.numpy as jnp
from jax import lax
from jax.sharding import PartitionSpec as P


def padded_2(block, sides, width):
    for axis, dim in sides:
        count = lax.axis_size(axis)
        forward = [(i, i + 1) for i in range(count - 1)]
        backward = [(target, source) for source, target in forward]
        low = lax.ppermute(
            lax.slice_in_dim(block, block.shape[dim] - width, None, axis=dim), axis, forward
        )
        high = lax.ppermute(lax.slice_in_dim(block, 0, width, axis=dim), axis, backward)
        block = jnp.concatenate([low, block, high], axis=dim)
    return block


def on_device(
    features, dw_kernel, dw_bias, norm_gain, norm_bias, w_in, b_in, w_out, b_out, layer_scale
):
    local_ch, rows, cols = features.shape
    chans = w_in.shape[1]
    padded = padded_2(features, (("row", 1), ("col", 2)), 3)
    padded = padded.astype(jnp.float32)
    mixed = jnp.zeros((local_ch, rows, cols), jnp.float32) + dw_bias[:, None, None]
    for a in range(7):
        for b in range(7):
            mixed = (
                mixed + dw_kernel[:, a, b][:, None, None] * padded[:, a : a + rows, b : b + cols]
            )
    mixed = mixed.reshape(local_ch, rows * cols)
    total, squares = lax.psum((jnp.sum(mixed, axis=0), jnp.sum(mixed * mixed, axis=0)), "hid")
    mean = total / chans
    var = squares / chans - mean * mean
    normed = (
        (mixed - mean) * lax.rsqrt(var + 1e-06) * norm_gain[:, None] + norm_bias[:, None]
    ).astype(jnp.bfloat16)
    gathered = lax.all_gather(normed, "hid", axis=0, tiled=True)
    pre = lax.dot_general(
        w_in, gathered, (((1,), (0,)), ((), ())), preferred_element_type=jnp.float32
    )
    hidden = jax.nn.gelu(pre + b_in[:, None], approximate=False).astype(jnp.bfloat16)
    mlp = lax.psum_scatter(
        lax.dot_general(
            w_out, hidden, (((0,), (0,)), ((), ())), preferred_element_type=jnp.float32
        ).astype(jnp.bfloat16),
        "hid",
        scatter_dimension=0,
        tiled=True,
    ).astype(jnp.float32)
    mlp = mlp.reshape(local_ch, rows, cols)
    result = features.astype(jnp.float32) + layer_scale[:, None, None] * (
        mlp + b_out[:, None, None]
    )
    return result.astype(jnp.bfloat16)


def solution(mesh):
    return jax.shard_map(
        on_device,
        mesh=mesh,
        in_specs=(
            P("hid", "row", "col"),
            P("hid", None, None),
            P("hid"),
            P("hid"),
            P("hid"),
            P("hid", None),
            P("hid"),
            P("hid", None),
            P("hid"),
            P("hid"),
        ),
        out_specs=P("hid", "row", "col"),
        check_vma=False,
    )
```

profile of v0, /device:TPU:1, one launch (start us, length us, event | category | flops | bytes accessed | tf_op | source)
XLA Modules:
  0.0 258.1 jit_solution(3622994337401183470)
XLA Ops:
  6.5 0.0 copy-start
  6.5 0.0 copy-start.2
  6.5 0.0 all-gather.2.cloned.1.call-start
  6.5 2.4 copy.12
  8.9 0.2 fusion.110
  9.1 4.4 %collective-permute-start = (bf16[256,3,128]{0,1,2:T(4,128)(2,1)S(1)}, bf16[256,3,128]{0,1,2:T(4,128)(2,1)S(1)}, u32[]{:S(2)}, u32[]{:S(2)}) collective-permute-start(bf16[256,3,128]{0,1,2:T(4,128)(2,1)S(1)} %get-tuple-element.12), channel_id=1, source_target_pairs={{0,16},{16,32},{32,48},{48,64},{64,80},{80,96},{96,112},{112,128},... | collective-permute-start | bytes 589832 | tf_op jit(solution)/shard_map/ppermute | solution.py:12
  13.5 1.3 collective-permute-start.1
  14.8 0.0 copy-done.2
  14.9 3.6 %collective-permute-done = bf16[256,3,128]{0,1,2:T(4,128)(2,1)S(1)} collective-permute-done((bf16[256,3,128]{0,1,2:T(4,128)(2,1)S(1)}, bf16[256,3,128]{0,1,2:T(4,128)(2,1)S(1)}, u32[]{:S(2)}, u32[]{:S(2)}) %collective-permute-start) | collective-permute-done | bytes 196640 | tf_op jit(solution)/shard_map/ppermute | solution.py:12
  18.5 10.1 %collective-permute-done.1 = bf16[256,3,128]{0,1,2:T(4,128)(2,1)S(1)} collective-permute-done((bf16[256,3,128]{0,1,2:T(4,128)(2,1)S(1)}, bf16[256,3,128]{0,1,2:T(4,128)(2,1)S(1)}, u32[]{:S(2)}, u32[]{:S(2)}) %collective-permute-start.1) | collective-permute-done | bytes 196640 | tf_op jit(solution)/shard_map/ppermute | solution.py:15
  28.6 1.0 pad_maximum_fusion
  29.6 9.0 %collective-permute-start.2 = (bf16[256,22,3]{0,1,2:T(8,128)(2,1)S(1)}, bf16[256,22,3]{0,1,2:T(8,128)(2,1)S(1)}, u32[]{:S(2)}, u32[]{:S(2)}) collective-permute-start(bf16[256,22,3]{0,1,2:T(8,128)(2,1)S(1)} %get-tuple-element.10), channel_id=1, source_target_pairs={{0,4},{4,8},{8,12},{1,5},{5,9},{9,13},{2,6},{6,10},{10,14},{3,7},{... | collective-permute-start | bytes 101384 | tf_op jit(solution)/shard_map/ppermute | solution.py:12
  38.6 1.9 collective-permute-start.3
  40.5 0.3 copy.16
  40.8 0.0 collective-permute-done.2
  40.9 6.9 %collective-permute-done.3 = bf16[256,22,3]{0,1,2:T(8,128)(2,1)S(1)} collective-permute-done((bf16[256,22,3]{0,1,2:T(8,128)(2,1)S(1)}, bf16[256,22,3]{0,1,2:T(8,128)(2,1)S(1)}, u32[]{:S(2)}, u32[]{:S(2)}) %collective-permute-start.3) | collective-permute-done | bytes 33824 | tf_op jit(solution)/shard_map/ppermute | solution.py:15
  47.8 0.0 copy-start.3
  47.8 2.0 maximum_convert_fusion
  49.8 0.0 copy-done.3
  49.8 0.0 copy-start.4
  49.8 0.0 copy-start.5
  49.8 48.6 %fusion.107 = (f32[16,128]{1,0:T(8,128)S(1)}, f32[16,128]{1,0:T(8,128)S(1)}, f32[256,16,128]{0,2,1:T(8,128)}) fusion(f32[256,22,134]{0,2,1:T(8,128)} %maximum_convert_fusion, f32[256]{0:T(256)S(1)} %bitcast.187, f32[256]{0:T(256)S(1)} %bitcast.188, f32[256]{0:T(256)S(1)} %bitcast.141, f32[256]{0:T(256)S(1)} %bitcast.142, f32[256]{0:T(256)S(1)} %bitcast.143, ...), kind=kLoop, calls=%fused_computation.166 | loop fusion | flops 52948992 | bytes 104925184 | tf_op jit(solution)/shard_map/reduce_sum | solution.py:34
  98.4 13.4 %all-reduce = (f32[2048]{0:T(1024)S(1)}, f32[2048]{0:T(1024)S(1)}) all-reduce(f32[2048]{0:T(1024)S(1)} %bitcast.139, f32[2048]{0:T(1024)S(1)} %bitcast.138), channel_id=1, replica_groups=mesh['row'=16,'col'=4,'hid'=4] {'hid'}, use_global_device_ids=true, to_apply=%region_3.0 | all-reduce | flops 4096 | bytes 32768 | tf_op jit(solution)/shard_map/psum | solution.py:34
  111.8 0.0 copy-done.4
  111.8 0.0 copy-done.5
  111.9 0.0 copy-start.8
  111.9 2.7 %fusion.76 = bf16[256,2048]{0,1:T(8,128)(2,1)} fusion(f32[256,16,128]{0,2,1:T(8,128)} %get-tuple-element.9, f32[256]{0:T(256)S(1)} %copy-done.4, f32[256]{0:T(256)S(1)} %copy-done.5, f32[2048]{0:T(1024)S(1)} %get-tuple-element.64, f32[2048]{0:T(1024)S(1)} %get-tuple-element.63), kind=kLoop, calls=%fused_computation.129 | loop fusion | flops 2621440 | bytes 3164160 | tf_op jit(solution)/shard_map/convert_element_type | solution.py:39
  114.6 0.0 all-gather.2.cloned.1.call-update
  114.6 0.0 reduce-scatter.2.cloned.1.call-start
  114.7 50.5 %all-gather.2.cloned.1.call-done = bf16[1024,2048]{0,1:T(8,128)(2,1)} async-done(((bf16[256,2048]{0,1:T(8,128)(2,1)}), bf16[1024,2048]{0,1:T(8,128)(2,1)}) %all-gather.2.cloned.1.call-update) | async-done | bytes 4194320 | tf_op jit(solution)/shard_map/all_gather | solution.py:40
  165.2 0.0 copy-done
  165.2 0.0 copy-done.8
  165.2 28.6 %convert_bitcast_fusion = bf16[1024,2048]{0,1:T(8,128)(2,1)} fusion(bf16[1024,1024]{1,0:T(8,128)(2,1)S(1)} %copy-done, f32[1024]{0:T(1024)S(1)} %copy-done.8, bf16[1024,2048]{0,1:T(8,128)(2,1)} %all-gather.2.cloned.1.call-done, bf16[1024,1024]{1,0:T(8,128)(2,1)} %param.15), kind=kOutput, calls=%fused_computation.24 | convolution fusion | flops 8730443776 | bytes 12587008 | tf_op jit(solution)/shard_map/dot_general | solution.py:46
  193.8 0.0 reduce-scatter.2.cloned.1.call-update
  193.8 0.0 copy-start.1
  193.9 0.0 copy-start.6
  193.9 0.0 copy-start.7
  193.9 51.4 %reduce-scatter.2.cloned.1.call-done = bf16[256,2048]{0,1:T(8,128)(2,1)} async-done(((bf16[1024,2048]{0,1:T(8,128)(2,1)}), bf16[256,2048]{0,1:T(8,128)(2,1)}) %reduce-scatter.2.cloned.1.call-update) | async-done | bytes 1048592 | tf_op jit(solution)/shard_map/reduce_scatter | solution.py:45
  245.2 2.7 %copy.18 = f32[256,16,128]{2,1,0:T(8,128)} copy(bf16[256,16,128]{0,2,1:T(8,128)(2,1)} %bitcast.137) | data formatting | bytes 3145728 | tf_op jit(solution)/shard_map/reshape | solution.py:53
  248.0 0.0 copy-done.1
  248.0 0.0 copy-done.6
  248.0 0.0 copy-done.7
  248.0 3.3 %add_convert_fusion = bf16[256,16,128]{2,1,0:T(8,128)(2,1)} fusion(f32[256,16,128]{2,1,0:T(8,128)} %copy.18, bf16[256,16,128]{2,1,0:T(8,128)(2,1)S(1)} %copy-done.1, f32[256]{0:T(256)S(1)} %copy-done.6, f32[256]{0:T(256)S(1)} %copy-done.7), kind=kLoop, calls=%fused_computation.130 | loop fusion | flops 2621440 | bytes 4196352 | tf_op jit(solution)/shard_map/convert_element_type | solution.py:57
  (7 shorter events, 0.1 us)
Async XLA Ops:
  6.5 158.6 %copy-start = (bf16[1024,1024]{1,0:T(8,128)(2,1)S(1)}, bf16[1024,1024]{1,0:T(8,128)(2,1)}, u32[]{:S(2)}) copy-start(bf16[1024,1024]{1,0:T(8,128)(2,1)} %param.17) | copy-start | bytes 6291460
  6.5 8.3 %copy-start.2 = (f32[256,7,7]{0,2,1:T(8,128)S(1)}, f32[256,7,7]{0,2,1:T(8,128)}, u32[]{:S(2)}) copy-start(f32[256,7,7]{0,2,1:T(8,128)} %param.11) | copy-start | bytes 150532
  6.5 158.6 %all-gather.2.cloned.1.call-start = ((), (), s32[]{:S(2)}) async-start(), calls=%async_computation.1 | async-start | bytes 5242880 | tf_op jit(solution)/shard_map/all_gather | solution.py:40
  9.1 9.3 %collective-permute-start = (bf16[256,3,128]{0,1,2:T(4,128)(2,1)S(1)}, bf16[256,3,128]{0,1,2:T(4,128)(2,1)S(1)}, u32[]{:S(2)}, u32[]{:S(2)}) collective-permute-start(bf16[256,3,128]{0,1,2:T(4,128)(2,1)S(1)} %get-tuple-element.12), channel_id=1, source_target_pairs={{0,16},{16,32},{32,48},{48,64},{64,80},{80,96},{96,112},{112,128},... | collective-permute-start | bytes 589832 | tf_op jit(solution)/shard_map/ppermute | solution.py:12
  13.5 15.1 %collective-permute-start.1 = (bf16[256,3,128]{0,1,2:T(4,128)(2,1)S(1)}, bf16[256,3,128]{0,1,2:T(4,128)(2,1)S(1)}, u32[]{:S(2)}, u32[]{:S(2)}) collective-permute-start(bf16[256,3,128]{0,1,2:T(4,128)(2,1)S(1)} %get-tuple-element.13), channel_id=1, source_target_pairs={{16,0},{32,16},{48,32},{64,48},{80,64},{96,80},{112,96},{128,112},... | collective-permute-start | bytes 589832 | tf_op jit(solution)/shard_map/ppermute | solution.py:15
  29.6 11.3 %collective-permute-start.2 = (bf16[256,22,3]{0,1,2:T(8,128)(2,1)S(1)}, bf16[256,22,3]{0,1,2:T(8,128)(2,1)S(1)}, u32[]{:S(2)}, u32[]{:S(2)}) collective-permute-start(bf16[256,22,3]{0,1,2:T(8,128)(2,1)S(1)} %get-tuple-element.10), channel_id=1, source_target_pairs={{0,4},{4,8},{8,12},{1,5},{5,9},{9,13},{2,6},{6,10},{10,14},{3,7},{... | collective-permute-start | bytes 101384 | tf_op jit(solution)/shard_map/ppermute | solution.py:12
  38.6 9.2 %collective-permute-start.3 = (bf16[256,22,3]{0,1,2:T(8,128)(2,1)S(1)}, bf16[256,22,3]{0,1,2:T(8,128)(2,1)S(1)}, u32[]{:S(2)}, u32[]{:S(2)}) collective-permute-start(bf16[256,22,3]{0,1,2:T(8,128)(2,1)S(1)} %get-tuple-element.11), channel_id=1, source_target_pairs={{4,0},{8,4},{12,8},{5,1},{9,5},{13,9},{6,2},{10,6},{14,10},{7,3},{... | collective-permute-start | bytes 101384 | tf_op jit(solution)/shard_map/ppermute | solution.py:15
  47.8 2.1 copy-start.3
  49.8 62.0 %copy-start.4 = (f32[256]{0:T(256)S(1)}, f32[256]{0:T(256)}, u32[]{:S(2)}) copy-start(f32[256]{0:T(256)} %param.14) | copy-start | bytes 3076
  49.8 62.0 %copy-start.5 = (f32[256]{0:T(256)S(1)}, f32[256]{0:T(256)}, u32[]{:S(2)}) copy-start(f32[256]{0:T(256)} %param.13) | copy-start | bytes 3076
  111.9 53.3 %copy-start.8 = (f32[1024]{0:T(1024)S(1)}, f32[1024]{0:T(1024)}, u32[]{:S(2)}) copy-start(f32[1024]{0:T(1024)} %param.16) | copy-start | bytes 12292
  114.6 130.6 %reduce-scatter.2.cloned.1.call-start = ((), (), s32[]{:S(2)}) async-start(), calls=%async_computation.2 | async-start | bytes 5242880 | tf_op jit(solution)/shard_map/reduce_scatter | solution.py:45
  193.8 54.1 %copy-start.1 = (bf16[256,16,128]{2,1,0:T(8,128)(2,1)S(1)}, bf16[256,16,128]{2,1,0:T(8,128)(2,1)}, u32[]{:S(2)}) copy-start(bf16[256,16,128]{2,1,0:T(8,128)(2,1)} %param.10) | copy-start | bytes 3145732
  193.9 54.1 %copy-start.6 = (f32[256]{0:T(256)S(1)}, f32[256]{0:T(256)}, u32[]{:S(2)}) copy-start(f32[256]{0:T(256)} %param.18) | copy-start | bytes 3076
  193.9 54.1 %copy-start.7 = (f32[256]{0:T(256)S(1)}, f32[256]{0:T(256)}, u32[]{:S(2)}) copy-start(f32[256]{0:T(256)} %param.19) | copy-start | bytes 3076
Sparse Core Ops, SparseCore 0:
  114.7 50.3 all-gather.1
  194.0 51.2 reduce-scatter.1
where the time goes:
time: 258 us
  waiting for transfers between devices  122 us (47%)
  other arithmetic  57.6 us (22%)
  matrix products  28.6 us (11%)
  starting transfers between devices  16.6 us (6%)
  between operations  13.6 us (5%)
  blocking collectives  13.4 us (5%)
  local copies, waits for them, and re-layouts  5.77 us (2%)
    reduce_scatter x1, waiting for transfers between devices, on_device(): lax.psum_scatter(lax.dot_general(w_out, hidden, (((0,), (0,)), ((), ())),...  51.4 us
    all_gather x1, waiting for transfers between devices, on_device(): gathered = lax.all_gather(normed, 'hid', axis=0, tiled=True)  50.5 us
    reduce_sum x1, other arithmetic, on_device(): jnp.sum(mixed, axis=0)  48.6 us
    dot_general x1, matrix products, on_device(): lax.dot_general(w_out, hidden, (((0,), (0,)), ((), ())), preferred_elemen...  28.6 us
    ppermute x2, waiting for transfers between devices, padded_2(): lax.ppermute(lax.slice_in_dim(block, 0, width, axis=dim), axis, backward)  17 us
    psum x1, blocking collectives, on_device(): lax.psum((jnp.sum(mixed, axis=0), jnp.sum(mixed * mixed, axis=0)), 'hid')  13.4 us
    ppermute x2, starting transfers between devices, padded_2(): lax.ppermute(lax.slice_in_dim(block, block.shape[dim] - width, None, axis...  13.4 us
  transfers between devices with their start and end apart: 6, of which 5 were waited for; matrix products, arithmetic and copies ran while one was open for 0% of the time, Pallas kernels for 0%

commit v1 on v0

v1 whole, which is shorter than its diff:
```python
import functools
import jax
import jax.numpy as jnp
from jax import lax
from jax.experimental import pallas as pl
from jax.experimental.pallas import tpu as pltpu
from jax.sharding import PartitionSpec as P

F32 = jnp.float32
BF = jnp.bfloat16
VM = pl.BlockSpec(memory_space=pltpu.VMEM)
SM = pl.BlockSpec(memory_space=pltpu.SMEM)
HB = pl.BlockSpec(memory_space=pl.ANY)
NT = (((1,), (1,)), ((), ()))
CB = 32


def params(mib):
    return pltpu.CompilerParams(vmem_limit_bytes=mib << 20)


def turn_kernel(x_ref, xt_ref, l_ref, r_ref, xf):
    xf[...] = x_ref[...].astype(F32).reshape(4096, 128)
    for r in range(16):
        for h in range(2):
            t = xf[pl.ds(h * 2048 + r, 128, stride=16), :]
            xt_ref[r, :, h * 128 : (h + 1) * 128] = t.T.astype(BF)
    for j in range(3):
        l_ref[:, j * 256 : (j + 1) * 256] = xt_ref[:, j, :]
        r_ref[:, j * 256 : (j + 1) * 256] = xt_ref[:, 125 + j, :]


def turn(x):
    edge = jax.ShapeDtypeStruct((16, 768), BF)
    return pl.pallas_call(
        turn_kernel,
        out_shape=(jax.ShapeDtypeStruct((16, 128, 256), BF), edge, edge),
        in_specs=[VM],
        out_specs=(VM, VM, VM),
        scratch_shapes=[pltpu.VMEM((4096, 128), F32)],
        compiler_params=params(16),
        cost_estimate=pl.CostEstimate(flops=0, bytes_accessed=4 << 20, transcendentals=0),
        name="turn",
    )(x)


def conv_kernel(
    sc, xt_ref, l_ref, r_ref, top_ref, bot_ref, ct_ref, cb_ref, kw_ref, o0, o1, o2, o3, xs
):
    for h in range(2):
        hs = slice(h * 128, (h + 1) * 128)
        for r in range(16):
            xs[h, 3 + r, 8:136, :] = xt_ref[r, :, hs].astype(F32)
        for r in range(3):
            xs[h, r, 8:136, :] = top_ref[r, :, hs].astype(F32)
            xs[h, 19 + r, 8:136, :] = bot_ref[r, :, hs].astype(F32)
        for j in range(3):
            js = slice(j * 256 + h * 128, j * 256 + (h + 1) * 128)
            ks = slice(768 + j * 256 + h * 128, 768 + j * 256 + (h + 1) * 128)
            xs[h, 3:19, 5 + j, :] = l_ref[:, js].astype(F32)
            xs[h, 3:19, 136 + j, :] = r_ref[:, js].astype(F32)
            xs[h, 0:3, 5 + j, :] = ct_ref[:, js].astype(F32)
            xs[h, 0:3, 136 + j, :] = ct_ref[:, ks].astype(F32)
            xs[h, 19:22, 5 + j, :] = cb_ref[:, js].astype(F32)
            xs[h, 19:22, 136 + j, :] = cb_ref[:, ks].astype(F32)
    for k, o in enumerate((o0, o1, o2, o3)):
        row0 = 4 * lax.rem(sc[0] + k, 4)
        for h in range(2):
            hs = slice(h * 128, (h + 1) * 128)
            for c0 in range(0, 128, CB):
                acc = [jnp.zeros((CB, 128), F32) for _ in range(4)]
                for b in range(7):
                    for ri in range(10):
                        xv = xs[h, row0 + ri, c0 + 5 + b : c0 + 5 + b + CB, :]
                        for ro in range(4):
                            a = ri - ro
                            if 0 <= a < 7:
                                acc[ro] = acc[ro] + kw_ref[a * 7 + b : a * 7 + b + 1, hs] * xv
                for ro in range(4):
                    o[ro, c0 : c0 + CB, hs] = acc[ro].astype(BF)


def conv(sc, *args):
    o = jax.ShapeDtypeStruct((4, 128, 256), BF)
    return pl.pallas_call(
        conv_kernel,
        out_shape=(o,) * 4,
        in_specs=[SM] + [VM] * 8,
        out_specs=(VM,) * 4,
        scratch_shapes=[pltpu.VMEM((2, 22, 144, 128), F32)],
        compiler_params=params(16),
        cost_estimate=pl.CostEstimate(flops=60_000_000, bytes_accessed=4 << 20, transcendentals=0),
        name="conv",
    )(sc, *args)


def gelu(p):
    return 0.5 * p * (1.0 + lax.erf(p * 0.7071067811865476))


def mlp_kernel(sc, *refs):
    m = refs[0:4]
    pp = refs[4]
    w_in, w_out = refs[5:7]
    mine, other = refs[7:12], refs[12:17]
    outs = refs[17:21]
    n_ref, acc, win, wout, bv, sems = refs[21:27]
    y, core, c0, c1 = sc[0], sc[1], sc[2], sc[3]
    color_mine = jnp.where(core == 0, c0, c1)
    color_other = jnp.where(core == 0, c1, c0)
    copies = [[] for _ in range(5)]

    def load(chunk, src, dst):
        copy = pltpu.make_async_copy(src, dst, sems.at[sum(len(c) for c in copies)])
        copy.start()
        copies[chunk].append(copy)

    load(0, w_in, win.at[0:1024])
    load(0, w_out, wout.at[0:1024])
    for s, side in enumerate((mine, other)):
        for a in range(4):
            for k in range(3):
                base = 1024 + a * 768 + k * 256 + s * 128
                for w, dst in ((0, win), (1, wout)):
                    start = k * 256 + w * 128
                    if a < 3:
                        src = side[a].at[start : start + 128]
                    elif start < 384:
                        src = side[3].at[start : start + 128]
                    else:
                        src = side[4].at[start - 384 : start - 256]
                    load(1 + a, src, dst.at[base : base + 128])

    def wide(q, first, count):
        return jnp.concatenate([pp[q, first + i] for i in range(count)], axis=1)

    total = jnp.zeros((512, 1), F32)
    squares = jnp.zeros((512, 1), F32)
    for k in range(4):
        q = lax.rem(y + 4 - k, 4)
        v = m[k][...].astype(F32) + wide(q, 0, 2)
        total = total + jnp.sum(v, axis=1, keepdims=True)
        squares = squares + jnp.sum(v * v, axis=1, keepdims=True)
    mean = total * (1.0 / 1024)
    rstd = lax.rsqrt(squares * (1.0 / 1024) - mean * mean + 1e-06)
    for k in range(4):
        q = lax.rem(y + 4 - k, 4)
        v = m[k][...].astype(F32) + wide(q, 0, 2)
        v = (v - mean) * rstd * wide(q, 2, 2) + wide(q, 4, 2)
        n_ref[:, pl.ds(pl.multiple_of(q * 256, 256), 256)] = v.astype(BF)

    def block(first, size, bias, fresh):
        pre = lax.dot_general(
            n_ref[...], win[first : first + size], NT, preferred_element_type=F32
        )
        h = gelu(pre + bias).astype(BF)
        for q in range(4):
            part = jnp.dot(
                h,
                wout[first : first + size, q * 256 : (q + 1) * 256],
                preferred_element_type=F32,
            )
            acc[q] = part if fresh else acc[q] + part

    for copy in copies[0]:
        copy.wait()
    block(0, 1024, wide(y, 6, 8), True)
    for a, shift in enumerate((0, 1, 3, 2)):
        for k in range(3):
            row = lax.rem(y + 1 + k, 4)
            for s in range(2):
                color = lax.rem((color_other if s else color_mine) + shift, 4)
                half = (1 - core) if s else core
                bv[a, :, k * 256 + s * 128 : k * 256 + s * 128 + 128] = pp[
                    row, 6 + half * 4 + color
                ]
        for copy in copies[1 + a]:
            copy.wait()
        block(1024 + a * 768, 768, bv[a], False)
    for k in range(4):
        outs[k][...] = acc[lax.rem(y + k, 4)].astype(BF)


def mlp(sc, mixed, pp, w_in, w_out, mine, other):
    o = jax.ShapeDtypeStruct((512, 256), BF)
    return pl.pallas_call(
        mlp_kernel,
        out_shape=(o,) * 4,
        in_specs=[SM] + [VM] * 5 + [HB] * 12,
        out_specs=(VM,) * 4,
        scratch_shapes=[
            pltpu.VMEM((512, 1024), BF),
            pltpu.VMEM((4, 512, 256), F32),
            pltpu.VMEM((4096, 1024), BF),
            pltpu.VMEM((4096, 1024), BF),
            pltpu.VMEM((4, 1, 768), F32),
            pltpu.SemaphoreType.DMA((50,)),
        ],
        compiler_params=params(48),
        cost_estimate=pl.CostEstimate(
            flops=8_600_000_000, bytes_accessed=20 << 20, transcendentals=2 << 20
        ),
        name="mlp",
    )(sc, *mixed, pp, w_in, w_out, *mine, *other)


def final_kernel(sc, x_ref, ls_ref, bo_ref, f0, f1, f2, f3, o_ref, t):
    for k, f in enumerate((f0, f1, f2, f3)):
        row0 = 4 * lax.rem(sc[0] + 4 - k, 4)
        for i in range(4):
            v = f[i * 128 : (i + 1) * 128, :].astype(F32)
            v = ls_ref[...] * (v + bo_ref[...])
            for h in range(2):
                t[pl.ds(h * 2048 + row0 + i, 128, stride=16), :] = v[
                    :, h * 128 : (h + 1) * 128
                ].T
    o_ref[...] = (x_ref[...].astype(F32) + t[...].reshape(256, 16, 128)).astype(BF)


def final(sc, x, ls, bo, parts):
    return pl.pallas_call(
        final_kernel,
        out_shape=jax.ShapeDtypeStruct((256, 16, 128), BF),
        in_specs=[SM] + [VM] * 7,
        out_specs=VM,
        scratch_shapes=[pltpu.VMEM((4096, 128), F32)],
        compiler_params=params(16),
        cost_estimate=pl.CostEstimate(flops=1 << 20, bytes_accessed=4 << 20, transcendentals=0),
        name="final",
    )(sc, x, ls, bo, *parts)


def from_hid(x, k):
    return lax.ppermute(x, "hid", [((i + k) % 4, i) for i in range(4)])


def to_hid(x, k):
    return lax.ppermute(x, "hid", [(i, (i + k) % 4) for i in range(4)])


def place(x, z, core):
    return (x * 4 + z % 4) * 4 + (z // 4) * 2 + core


def from_plane(v, step, major):
    pairs = []
    for x in range(4):
        for z in range(8):
            for core in range(2):
                along_x = (core == 0) == major
                sx, sz = ((x + step) % 4, z) if along_x else (x, (z + step) % 8)
                pairs.append((place(sx, sz, core), place(x, z, core)))
    return lax.ppermute(v, ("row", "col"), pairs)


def from_core(v):
    return lax.ppermute(v, "col", [(0, 1), (1, 0), (2, 3), (3, 2)])


def shift(v, axis, up):
    n = lax.axis_size(axis)
    pairs = [(i, i + 1) for i in range(n - 1)]
    return lax.ppermute(v, axis, pairs if up else [(b, a) for a, b in pairs])


def on_device(
    features, dw_kernel, dw_bias, norm_gain, norm_bias, w_in, b_in, w_out, b_out, layer_scale
):
    row, col, y = lax.axis_index("row"), lax.axis_index("col"), lax.axis_index("hid")
    x, zl, core = row // 4, row % 4, col % 2
    c0, c1 = (x + 2 * zl) % 4, (2 * x + zl) % 4
    color = jnp.where(core == 0, c0, c1)
    sc = jnp.stack([y, core, c0, c1]).astype(jnp.int32)

    pp = lax.all_gather(
        jnp.concatenate([dw_bias, norm_gain, norm_bias, b_in]).reshape(14, 1, 128), "hid"
    )

    xt, left, right = turn(features)
    halo_l = shift(right, "col", True)
    halo_r = shift(left, "col", False)
    top = shift(xt[13:16], "row", True)
    bot = shift(xt[0:3], "row", False)
    corner_t = shift(jnp.concatenate([halo_l[13:16], halo_r[13:16]], 1), "row", True)
    corner_b = shift(jnp.concatenate([halo_l[0:3], halo_r[0:3]], 1), "row", False)

    start = 512 * core + 128 * color
    piece = jnp.concatenate(
        [
            lax.dynamic_slice_in_dim(w_in, start, 128, 0),
            lax.dynamic_slice_in_dim(w_out, start, 128, 0),
        ]
    )
    held = jnp.concatenate([from_hid(piece, k) for k in (1, 2, 3)])
    mine = [
        held,
        from_plane(held, 1, True),
        from_plane(held, -1, True),
        from_plane(held[:384], 1, False),
        from_plane(held[384:], -1, False),
    ]
    other = [from_core(v) for v in mine]

    kw = jnp.transpose(dw_kernel.reshape(256, 49))
    mixed = conv(sc, xt, halo_l, halo_r, top, bot, corner_t, corner_b, kw)
    mixed = [mixed[0]] + [to_hid(mixed[k], k) for k in (1, 2, 3)]
    mixed = [v.reshape(512, 256) for v in mixed]
    parts = mlp(sc, mixed, pp, w_in, w_out, mine, other)
    parts = [parts[0]] + [to_hid(parts[k], k) for k in (1, 2, 3)]
    return final(sc, features, layer_scale[None, :], b_out[None, :], parts)


def solution(mesh):
    return jax.shard_map(
        on_device,
        mesh=mesh,
        in_specs=(
            P("hid", "row", "col"),
            P("hid", None, None),
            P("hid"),
            P("hid"),
            P("hid"),
            P("hid", None),
            P("hid"),
            P("hid", None),
            P("hid"),
            P("hid"),
        ),
        out_specs=P("hid", "row", "col"),
        check_vma=False,
    )
```

time: 258 us -> 155 us (0.60)
  waiting for transfers between devices: 122 us -> 52.2 us
  other arithmetic: 57.6 us -> 0.27 us
  starting transfers between devices: 16.6 us -> 57.7 us
  matrix products: 28.6 us -> 0 us
  Pallas kernels: 0 us -> 25.4 us
  between operations: 13.6 us -> 0.27 us
  blocking collectives: 13.4 us -> 9.13 us
  local copies, waits for them, and re-layouts: 5.77 us -> 8.74 us
    reduce_scatter x1 -> x0, waiting for transfers between devices: 51.4 us -> none  [on_device(): lax.psum_scatter(lax.dot_general(w_out, hidden, (((0,), (0,)), ((), ())),...]
    all_gather x1 -> x0, waiting for transfers between devices: 50.5 us -> none  [on_device(): gathered = lax.all_gather(normed, 'hid', axis=0, tiled=True)]
    reduce_sum x1 -> x0, other arithmetic: 48.6 us -> none  [on_device(): jnp.sum(mixed, axis=0)]
    ppermute x4 -> x24, starting transfers between devices: 16.6 us -> 57.7 us  [the longest x6 18.5 us: shift(): return lax.ppermute(v, axis, pairs if up else [(b, a) for a, b in pairs])]
    ppermute x4 -> x24, waiting for transfers between devices: 20.6 us -> 52.2 us  [the longest x3 23.7 us: from_hid(): return lax.ppermute(x, 'hid', [((i + k) % 4, i) for i in range(4)])]
    dot_general x1 -> x0, matrix products: 28.6 us -> none  [on_device(): lax.dot_general(w_out, hidden, (((0,), (0,)), ((), ())), preferred_elemen...]
    pallas_call x0 -> x4, Pallas kernels: none -> 25.4 us  [the longest x1 14.4 us: mlp(): pl.pallas_call(mlp_kernel, out_shape=(o,) * 4, in_specs=[SM] + [VM] * 5 +...]
    psum x1 -> x0, blocking collectives: 13.4 us -> none  [on_device(): lax.psum((jnp.sum(mixed, axis=0), jnp.sum(mixed * mixed, axis=0)), 'hid')]
  transfers between devices with their start and end apart: 6 -> 24, of which waited for: 5 -> 9; matrix products, arithmetic and copies ran while one was open for 0% -> 2% of each run, Pallas kernels for 0% -> 5%
where the time goes in v1:
time: 155 us; the launch traced here: 154 us
  starting transfers between devices  57.7 us (37%)
  waiting for transfers between devices  52.2 us (34%)
  Pallas kernels  25.4 us (16%)
  blocking collectives  9.13 us (6%)
  local copies, waits for them, and re-layouts  8.74 us (6%)
    ppermute x3, waiting for transfers between devices, from_hid(): return lax.ppermute(x, 'hid', [((i + k) % 4, i) for i in range(4)])  23.7 us
    ppermute x6, starting transfers between devices, shift(): return lax.ppermute(v, axis, pairs if up else [(b, a) for a, b in pairs])  18.5 us
    ppermute x5, starting transfers between devices, from_core(): return lax.ppermute(v, 'col', [(0, 1), (1, 0), (2, 3), (3, 2)])  18 us
    ppermute x6, waiting for transfers between devices, to_hid(): return lax.ppermute(x, 'hid', [(i, (i + k) % 4) for i in range(4)])  16.5 us
    pallas_call x1, Pallas kernels, mlp(): pl.pallas_call(mlp_kernel, out_shape=(o,) * 4, in_specs=[SM] + [VM] * 5 +...  14.4 us
    ppermute x6, waiting for transfers between devices, shift(): return lax.ppermute(v, axis, pairs if up else [(b, a) for a, b in pairs])  11.9 us
    ppermute x4, starting transfers between devices, from_plane(): return lax.ppermute(v, ('row', 'col'), pairs)  10 us
    all_gather x1, blocking collectives, on_device(): lax.all_gather(jnp.concatenate([dw_bias, norm_gain, norm_bias, b_in]).res...  9.13 us
  transfers between devices with their start and end apart: 24, of which 9 were waited for; matrix products, arithmetic and copies ran while one was open for 2% of the time, Pallas kernels for 5%

profile of v1, /device:TPU:1, one launch (start us, length us, event | category | flops | bytes accessed | tf_op | source)
XLA Modules:
  0.0 153.7 jit_solution(12457811486155565648)
XLA Ops:
  0.0 1.1 constant_dynamic-slice_fusion
  1.1 0.0 copy-start
  1.1 3.6 %collective-permute-start.9 = (bf16[256,1024]{1,0:T(8,128)(2,1)S(1)}, bf16[256,1024]{1,0:T(8,128)(2,1)S(1)}, u32[]{:S(2)}, u32[]{:S(2)}) collective-permute-start(bf16[256,1024]{1,0:T(8,128)(2,1)S(1)} %pad_maximum_fusion.2), channel_id=1, source_target_pairs={{1,0},{2,1},{3,2},{0,3},{5,4},{6,5},{7,6},{4,7},{9,8},{10,9},{11,1... | collective-permute-start | bytes 1572872 | tf_op jit(solution)/shard_map/ppermute | solution.py:234
  4.8 0.3 collective-permute-start.10
  5.1 0.7 collective-permute-start.11
  5.8 20.6 %collective-permute-done.9 = bf16[256,1024]{1,0:T(8,128)(2,1)S(1)} collective-permute-done((bf16[256,1024]{1,0:T(8,128)(2,1)S(1)}, bf16[256,1024]{1,0:T(8,128)(2,1)S(1)}, u32[]{:S(2)}, u32[]{:S(2)}) %collective-permute-start.9) | collective-permute-done | bytes 524320 | tf_op jit(solution)/shard_map/ppermute | solution.py:234
  26.4 0.9 constant_dynamic-update-slice_fusion.2
  27.3 0.9 constant_dynamic-update-slice_fusion.1
  28.3 3.1 %collective-permute-done.11 = bf16[256,1024]{1,0:T(8,128)(2,1)S(1)} collective-permute-done((bf16[256,1024]{1,0:T(8,128)(2,1)S(1)}, bf16[256,1024]{1,0:T(8,128)(2,1)S(1)}, u32[]{:S(2)}, u32[]{:S(2)}) %collective-permute-start.11) | collective-permute-done | bytes 524320 | tf_op jit(solution)/shard_map/ppermute | solution.py:234
  31.4 0.9 constant_dynamic-update-slice_fusion.refs_7_
  32.3 1.6 %collective-permute-start.13 = (bf16[768,1024]{1,0:T(8,128)(2,1)}, bf16[768,1024]{1,0:T(8,128)(2,1)}, u32[]{:S(2)}, u32[]{:S(2)}) collective-permute-start(bf16[768,1024]{1,0:T(8,128)(2,1)} %constant_dynamic-update-slice_fusion.refs_7_), channel_id=1, source_target_pairs={{192,0},{60,4},{208,16},{4,20},{224,32},{20,36},{240,48},{36,52},{... | collective-permute-start | bytes 4718600 | tf_op jit(solution)/shard_map/ppermute | solution.py:253
  33.9 4.0 %collective-permute-start.12 = (bf16[768,1024]{1,0:T(8,128)(2,1)}, bf16[768,1024]{1,0:T(8,128)(2,1)}, u32[]{:S(2)}, u32[]{:S(2)}) collective-permute-start(bf16[768,1024]{1,0:T(8,128)(2,1)} %constant_dynamic-update-slice_fusion.refs_7_), channel_id=1, source_target_pairs={{64,0},{20,4},{80,16},{36,20},{96,32},{52,36},{112,48},{12,52},{72... | collective-permute-start | bytes 4718600 | tf_op jit(solution)/shard_map/ppermute | solution.py:253
  38.0 0.9 turn.1
  38.8 6.8 %collective-permute-start = (bf16[16,768]{1,0:T(8,128)(2,1)S(1)}, bf16[16,768]{1,0:T(8,128)(2,1)S(1)}, u32[]{:S(2)}, u32[]{:S(2)}) collective-permute-start(bf16[16,768]{1,0:T(8,128)(2,1)S(1)} %get-tuple-element.17), channel_id=1, source_target_pairs={{0,4},{4,8},{8,12},{1,5},{5,9},{9,13},{2,6},{6,10},{10,14},{3,7},{... | collective-permute-start | bytes 73736 | tf_op jit(solution)/shard_map/ppermute | solution.py:263
  45.6 1.9 %collective-permute-start.1 = (bf16[16,768]{1,0:T(8,128)(2,1)S(1)}, bf16[16,768]{1,0:T(8,128)(2,1)S(1)}, u32[]{:S(2)}, u32[]{:S(2)}) collective-permute-start(bf16[16,768]{1,0:T(8,128)(2,1)S(1)} %get-tuple-element.18), channel_id=1, source_target_pairs={{4,0},{8,4},{12,8},{5,1},{9,5},{13,9},{6,2},{10,6},{14,10},{7,3},{... | collective-permute-start | bytes 73736 | tf_op jit(solution)/shard_map/ppermute | solution.py:263
  47.6 1.3 collective-permute-start.3
  48.9 5.4 %collective-permute-done.l_ref = bf16[16,768]{1,0:T(8,128)(2,1)S(1)} collective-permute-done((bf16[16,768]{1,0:T(8,128)(2,1)S(1)}, bf16[16,768]{1,0:T(8,128)(2,1)S(1)}, u32[]{:S(2)}, u32[]{:S(2)}) %collective-permute-start) | collective-permute-done | bytes 24608 | tf_op jit(solution)/shard_map/ppermute | solution.py:263
  54.3 4.9 %collective-permute-start.2 = (bf16[3,128,256]{2,1,0:T(8,128)(2,1)S(1)}, bf16[3,128,256]{2,1,0:T(8,128)(2,1)S(1)}, u32[]{:S(2)}, u32[]{:S(2)}) collective-permute-start(bf16[3,128,256]{2,1,0:T(8,128)(2,1)S(1)} %get-tuple-element.28), channel_id=1, source_target_pairs={{0,16},{16,32},{32,48},{48,64},{64,80},{80,96},{96,112},{112,128},... | collective-permute-start | bytes 589832 | tf_op jit(solution)/shard_map/ppermute | solution.py:263
  59.2 2.2 %collective-permute-start.4 = (bf16[3,1536]{1,0:T(4,128)(2,1)S(1)}, bf16[3,1536]{1,0:T(4,128)(2,1)S(1)}, u32[]{:S(2)}, u32[]{:S(2)}) collective-permute-start(bf16[3,1536]{1,0:T(4,128)(2,1)S(1)} %pad_maximum_fusion.3), channel_id=1, source_target_pairs={{0,16},{16,32},{32,48},{48,64},{64,80},{80,96},{96,112},{112,128},... | collective-permute-start | bytes 27656 | tf_op jit(solution)/shard_map/ppermute | solution.py:263
  61.4 0.8 collective-permute-done.4.ct_ref
  62.2 1.5 collective-permute-start.5
  63.7 0.1 pad_add_fusion.sc
  63.8 0.8 reshape.15
  64.6 5.7 %collective-permute-done.5.cb_ref = bf16[3,1536]{1,0:T(4,128)(2,1)S(1)} collective-permute-done((bf16[3,1536]{1,0:T(4,128)(2,1)S(1)}, bf16[3,1536]{1,0:T(4,128)(2,1)S(1)}, u32[]{:S(2)}, u32[]{:S(2)}) %collective-permute-start.5) | collective-permute-done | bytes 9248 | tf_op jit(solution)/shard_map/ppermute | solution.py:263
  70.3 7.4 %conv.1 = (bf16[4,128,256]{2,1,0:T(8,128)(2,1)S(1)}, bf16[4,128,256]{2,1,0:T(8,128)(2,1)S(1)}, bf16[4,128,256]{2,1,0:T(8,128)(2,1)S(1)}, bf16[4,128,256]{2,1,0:T(8,128)(2,1)S(1)}) custom-call(s32[4]{0:T(128)S(1)} %pad_add_fusion.sc, bf16[16,128,256]{2,1,0:T(8,128)(2,1)S(1)} %get-tuple-element.16.xt_ref, bf16[16,768]{1,0:T(8,128)(2,1)S(1)} %collective-permute-done.l_ref, ...), custom_call_target="tpu_custom_call" | custom-call | flops 60000000 | bytes 4194304 | tf_op jit(solution)/shard_map/conv/pallas_call | solution.py:85
  77.8 0.7 copy-done.3
  78.5 1.5 collective-permute-start.7
  80.0 1.2 collective-permute-start.8
  81.3 0.1 pad_maximum_fusion
  81.4 6.3 %collective-permute-done.6 = bf16[4,128,256]{2,1,0:T(8,128)(2,1)S(1)} collective-permute-done((bf16[4,128,256]{2,1,0:T(8,128)(2,1)S(1)}, bf16[4,128,256]{2,1,0:T(8,128)(2,1)S(1)}, u32[]{:S(2)}, u32[]{:S(2)}) %collective-permute-start.6) | collective-permute-done | bytes 262176 | tf_op jit(solution)/shard_map/ppermute | solution.py:238
  87.8 0.7 copy-done.5
  88.5 4.3 %collective-permute-start.15 = (bf16[384,1024]{1,0:T(8,128)(2,1)S(1)}, bf16[384,1024]{1,0:T(8,128)(2,1)S(1)}, u32[]{:S(2)}, u32[]{:S(2)}) collective-permute-start(bf16[384,1024]{1,0:T(8,128)(2,1)S(1)} %get-tuple-element.29), channel_id=1, source_target_pairs={{56,0},{196,4},{0,16},{212,20},{16,32},{228,36},{32,48},{244,52},{... | collective-permute-start | bytes 2359304 | tf_op jit(solution)/shard_map/ppermute | solution.py:253
  92.8 0.7 copy-done.7
  93.5 8.5 %collective-permute-start.18 = (bf16[768,1024]{1,0:T(8,128)(2,1)}, bf16[768,1024]{1,0:T(8,128)(2,1)}, u32[]{:S(2)}, u32[]{:S(2)}) collective-permute-start(bf16[768,1024]{1,0:T(8,128)(2,1)} %collective-permute-done.13.refs_9_), channel_id=1, source_target_pairs={{0,4},{4,0},{8,12},{12,8},{1,5},{5,1},{9,13},{13,9},{2,6},{6,2},{1... | collective-permute-start | bytes 4718600 | tf_op jit(solution)/shard_map/ppermute | solution.py:257
  102.0 0.1 collective-permute-start.17
  102.1 9.0 %collective-permute-start.20 = (bf16[384,1024]{1,0:T(8,128)(2,1)S(1)}, bf16[384,1024]{1,0:T(8,128)(2,1)}, u32[]{:S(2)}, u32[]{:S(2)}) collective-permute-start(bf16[384,1024]{1,0:T(8,128)(2,1)S(1)} %collective-permute-done.15.refs_11_), channel_id=1, source_target_pairs={{0,4},{4,0},{8,12},{12,8},{1,5},{5,1},{9,13},{13,9},{2,6},{6,2},{1... | collective-permute-start | bytes 2359304 | tf_op jit(solution)/shard_map/ppermute | solution.py:257
  111.1 0.4 collective-permute-start.19
  111.6 9.1 %all_gather.3.refs_4_ = f32[4,14,1,128]{3,2,1,0:T(1,128)S(1)} all-gather(f32[1,14,1,128]{3,2,1,0:T(1,128)S(1)} %all_gather_reshape.3), channel_id=1, replica_groups=mesh['row'=16,'col'=4,'hid'=4] {'hid'}, dimensions={0}, use_global_device_ids=true | all-gather | bytes 35840 | tf_op jit(solution)/shard_map/all_gather | solution.py:275
  120.8 0.9 copy-done.6
  121.7 0.9 copy-done.8
  122.7 14.4 %mlp.1 = (bf16[512,256]{1,0:T(8,128)(2,1)S(1)}, bf16[512,256]{1,0:T(8,128)(2,1)S(1)}, bf16[512,256]{1,0:T(8,128)(2,1)S(1)}, bf16[512,256]{1,0:T(8,128)(2,1)S(1)}) custom-call(s32[4]{0:T(128)S(1)} %pad_add_fusion.sc, bf16[512,256]{1,0:T(8,128)(2,1)S(1)} %bitcast.16, bf16[512,256]{1,0:T(8,128)(2,1)S(1)} %bitcast.17, bf16[512,256]{1,0:T(8,128)(2,1)S(1)} %bitcast.18, ...), custom_call_target="tpu_custom_call" | custom-call | flops 8600000512 | bytes 20971520 | tf_op jit(solution)/shard_map/mlp/pallas_call | solution.py:186
  137.1 1.2 collective-permute-start.21
  138.3 2.4 %collective-permute-start.22 = (bf16[512,256]{1,0:T(8,128)(2,1)S(1)}, bf16[512,256]{1,0:T(8,128)(2,1)S(1)}, u32[]{:S(2)}, u32[]{:S(2)}) collective-permute-start(bf16[512,256]{1,0:T(8,128)(2,1)S(1)} %get-tuple-element.25), channel_id=1, source_target_pairs={{0,2},{1,3},{2,0},{3,1},{4,6},{5,7},{6,4},{7,5},{8,10},{9,11},{10,... | collective-permute-start | bytes 786440 | tf_op jit(solution)/shard_map/ppermute | solution.py:238
  140.7 0.1 collective-permute-start.23
  140.8 3.1 %collective-permute-done.21.f1 = bf16[512,256]{1,0:T(8,128)(2,1)S(1)} collective-permute-done((bf16[512,256]{1,0:T(8,128)(2,1)S(1)}, bf16[512,256]{1,0:T(8,128)(2,1)S(1)}, u32[]{:S(2)}, u32[]{:S(2)}) %collective-permute-start.21) | collective-permute-done | bytes 262176 | tf_op jit(solution)/shard_map/ppermute | solution.py:238
  143.9 5.6 %collective-permute-done.22.f2 = bf16[512,256]{1,0:T(8,128)(2,1)S(1)} collective-permute-done((bf16[512,256]{1,0:T(8,128)(2,1)S(1)}, bf16[512,256]{1,0:T(8,128)(2,1)S(1)}, u32[]{:S(2)}, u32[]{:S(2)}) %collective-permute-start.22) | collective-permute-done | bytes 262176 | tf_op jit(solution)/shard_map/ppermute | solution.py:238
  149.5 1.5 collective-permute-done.23.f3
  151.0 2.7 %final.1 = bf16[256,16,128]{2,1,0:T(8,128)(2,1)} custom-call(s32[4]{0:T(128)S(1)} %pad_add_fusion.sc, bf16[256,16,128]{2,1,0:T(8,128)(2,1)S(1)} %copy-done, f32[1,256]{1,0:T(1,128)S(1)} %bitcast.14, f32[1,256]{1,0:T(1,128)S(1)} %bitcast.15, bf16[512,256]{1,0:T(8,128)(2,1)S(1)} %get-tuple-element.23.f0, bf16[512,256]{1,0:T(8,128)(2,1)S(1)} %collective-permute-done.21.f1, ...), custom_call_target="tpu_custom_call" | custom-call | flops 1048576 | bytes 4194304 | tf_op jit(solution)/shard_map/final/pallas_call | solution.py:221
  (54 shorter events, 0.2 us)
Async XLA Ops:
  1.1 36.9 %copy-start = (bf16[256,16,128]{2,1,0:T(8,128)(2,1)S(1)}, bf16[256,16,128]{2,1,0:T(8,128)(2,1)}, u32[]{:S(2)}) copy-start(bf16[256,16,128]{2,1,0:T(8,128)(2,1)} %x_ref.3) | copy-start | bytes 3145732
  1.1 25.3 %collective-permute-start.9 = (bf16[256,1024]{1,0:T(8,128)(2,1)S(1)}, bf16[256,1024]{1,0:T(8,128)(2,1)S(1)}, u32[]{:S(2)}, u32[]{:S(2)}) collective-permute-start(bf16[256,1024]{1,0:T(8,128)(2,1)S(1)} %pad_maximum_fusion.2), channel_id=1, source_target_pairs={{1,0},{2,1},{3,2},{0,3},{5,4},{6,5},{7,6},{4,7},{9,8},{10,9},{11,1... | collective-permute-start | bytes 1572872 | tf_op jit(solution)/shard_map/ppermute | solution.py:234
  4.8 22.6 %collective-permute-start.10 = (bf16[256,1024]{1,0:T(8,128)(2,1)S(1)}, bf16[256,1024]{1,0:T(8,128)(2,1)S(1)}, u32[]{:S(2)}, u32[]{:S(2)}) collective-permute-start(bf16[256,1024]{1,0:T(8,128)(2,1)S(1)} %pad_maximum_fusion.2), channel_id=1, source_target_pairs={{2,0},{3,1},{0,2},{1,3},{6,4},{7,5},{4,6},{5,7},{10,8},{11,9},{8,1... | collective-permute-start | bytes 1572872 | tf_op jit(solution)/shard_map/ppermute | solution.py:234
  5.1 26.2 %collective-permute-start.11 = (bf16[256,1024]{1,0:T(8,128)(2,1)S(1)}, bf16[256,1024]{1,0:T(8,128)(2,1)S(1)}, u32[]{:S(2)}, u32[]{:S(2)}) collective-permute-start(bf16[256,1024]{1,0:T(8,128)(2,1)S(1)} %pad_maximum_fusion.2), channel_id=1, source_target_pairs={{3,0},{0,1},{1,2},{2,3},{7,4},{4,5},{5,6},{6,7},{11,8},{8,9},{9,10... | collective-permute-start | bytes 1572872 | tf_op jit(solution)/shard_map/ppermute | solution.py:234
  27.3 6.6 %copy-start.9 = (bf16[256,1024]{1,0:T(8,128)(2,1)}, bf16[256,1024]{1,0:T(8,128)(2,1)S(1)}, u32[]{:S(2)}) copy-start(bf16[256,1024]{1,0:T(8,128)(2,1)S(1)} %collective-permute-done.10) | copy-start | bytes 1572868
  31.4 2.6 %copy-start.11 = (bf16[256,1024]{1,0:T(8,128)(2,1)}, bf16[256,1024]{1,0:T(8,128)(2,1)S(1)}, u32[]{:S(2)}) copy-start(bf16[256,1024]{1,0:T(8,128)(2,1)S(1)} %collective-permute-done.11) | copy-start | bytes 1572868
  32.3 61.2 %collective-permute-start.13 = (bf16[768,1024]{1,0:T(8,128)(2,1)}, bf16[768,1024]{1,0:T(8,128)(2,1)}, u32[]{:S(2)}, u32[]{:S(2)}) collective-permute-start(bf16[768,1024]{1,0:T(8,128)(2,1)} %constant_dynamic-update-slice_fusion.refs_7_), channel_id=1, source_target_pairs={{192,0},{60,4},{208,16},{4,20},{224,32},{20,36},{240,48},{36,52},{... | collective-permute-start | bytes 4718600 | tf_op jit(solution)/shard_map/ppermute | solution.py:253
  33.9 68.1 %collective-permute-start.12 = (bf16[768,1024]{1,0:T(8,128)(2,1)}, bf16[768,1024]{1,0:T(8,128)(2,1)}, u32[]{:S(2)}, u32[]{:S(2)}) collective-permute-start(bf16[768,1024]{1,0:T(8,128)(2,1)} %constant_dynamic-update-slice_fusion.refs_7_), channel_id=1, source_target_pairs={{64,0},{20,4},{80,16},{36,20},{96,32},{52,36},{112,48},{12,52},{72... | collective-permute-start | bytes 4718600 | tf_op jit(solution)/shard_map/ppermute | solution.py:253
  38.8 15.4 %collective-permute-start = (bf16[16,768]{1,0:T(8,128)(2,1)S(1)}, bf16[16,768]{1,0:T(8,128)(2,1)S(1)}, u32[]{:S(2)}, u32[]{:S(2)}) collective-permute-start(bf16[16,768]{1,0:T(8,128)(2,1)S(1)} %get-tuple-element.17), channel_id=1, source_target_pairs={{0,4},{4,8},{8,12},{1,5},{5,9},{9,13},{2,6},{6,10},{10,14},{3,7},{... | collective-permute-start | bytes 73736 | tf_op jit(solution)/shard_map/ppermute | solution.py:263
  45.6 13.5 %collective-permute-start.1 = (bf16[16,768]{1,0:T(8,128)(2,1)S(1)}, bf16[16,768]{1,0:T(8,128)(2,1)S(1)}, u32[]{:S(2)}, u32[]{:S(2)}) collective-permute-start(bf16[16,768]{1,0:T(8,128)(2,1)S(1)} %get-tuple-element.18), channel_id=1, source_target_pairs={{4,0},{8,4},{12,8},{5,1},{9,5},{13,9},{6,2},{10,6},{14,10},{7,3},{... | collective-permute-start | bytes 73736 | tf_op jit(solution)/shard_map/ppermute | solution.py:263
  47.6 22.8 %collective-permute-start.3 = (bf16[3,128,256]{2,1,0:T(8,128)(2,1)S(1)}, bf16[3,128,256]{2,1,0:T(8,128)(2,1)S(1)}, u32[]{:S(2)}, u32[]{:S(2)}) collective-permute-start(bf16[3,128,256]{2,1,0:T(8,128)(2,1)S(1)} %get-tuple-element.27), channel_id=1, source_target_pairs={{16,0},{32,16},{48,32},{64,48},{80,64},{96,80},{112,96},{128,112},... | collective-permute-start | bytes 589832 | tf_op jit(solution)/shard_map/ppermute | solution.py:263
  54.3 16.1 %collective-permute-start.2 = (bf16[3,128,256]{2,1,0:T(8,128)(2,1)S(1)}, bf16[3,128,256]{2,1,0:T(8,128)(2,1)S(1)}, u32[]{:S(2)}, u32[]{:S(2)}) collective-permute-start(bf16[3,128,256]{2,1,0:T(8,128)(2,1)S(1)} %get-tuple-element.28), channel_id=1, source_target_pairs={{0,16},{16,32},{32,48},{48,64},{64,80},{80,96},{96,112},{112,128},... | collective-permute-start | bytes 589832 | tf_op jit(solution)/shard_map/ppermute | solution.py:263
  59.2 3.0 %collective-permute-start.4 = (bf16[3,1536]{1,0:T(4,128)(2,1)S(1)}, bf16[3,1536]{1,0:T(4,128)(2,1)S(1)}, u32[]{:S(2)}, u32[]{:S(2)}) collective-permute-start(bf16[3,1536]{1,0:T(4,128)(2,1)S(1)} %pad_maximum_fusion.3), channel_id=1, source_target_pairs={{0,16},{16,32},{32,48},{48,64},{64,80},{80,96},{96,112},{112,128},... | collective-permute-start | bytes 27656 | tf_op jit(solution)/shard_map/ppermute | solution.py:263
  62.2 8.1 %collective-permute-start.5 = (bf16[3,1536]{1,0:T(4,128)(2,1)S(1)}, bf16[3,1536]{1,0:T(4,128)(2,1)S(1)}, u32[]{:S(2)}, u32[]{:S(2)}) collective-permute-start(bf16[3,1536]{1,0:T(4,128)(2,1)S(1)} %pad_maximum_fusion.4), channel_id=1, source_target_pairs={{16,0},{32,16},{48,32},{64,48},{80,64},{96,80},{112,96},{128,112},... | collective-permute-start | bytes 27656 | tf_op jit(solution)/shard_map/ppermute | solution.py:263
  64.6 16.7 %copy-start.10 = (bf16[256,1024]{1,0:T(8,128)(2,1)S(1)}, bf16[256,1024]{1,0:T(8,128)(2,1)}, u32[]{:S(2)}) copy-start(bf16[256,1024]{1,0:T(8,128)(2,1)} %copy-done.9) | copy-start | bytes 1572868
  64.6 16.7 %copy-start.12 = (bf16[256,1024]{1,0:T(8,128)(2,1)S(1)}, bf16[256,1024]{1,0:T(8,128)(2,1)}, u32[]{:S(2)}) copy-start(bf16[256,1024]{1,0:T(8,128)(2,1)} %copy-done.11) | copy-start | bytes 1572868
  77.8 0.7 copy-start.3
  78.5 9.2 %collective-permute-start.6 = (bf16[4,128,256]{2,1,0:T(8,128)(2,1)S(1)}, bf16[4,128,256]{2,1,0:T(8,128)(2,1)S(1)}, u32[]{:S(2)}, u32[]{:S(2)}) collective-permute-start(bf16[4,128,256]{2,1,0:T(8,128)(2,1)S(1)} %get-tuple-element.20), channel_id=1, source_target_pairs={{0,1},{1,2},{2,3},{3,0},{4,5},{5,6},{6,7},{7,4},{8,9},{9,10},{10,1... | collective-permute-start | bytes 786440 | tf_op jit(solution)/shard_map/ppermute | solution.py:238
  78.5 9.2 %collective-permute-start.7 = (bf16[4,128,256]{2,1,0:T(8,128)(2,1)S(1)}, bf16[4,128,256]{2,1,0:T(8,128)(2,1)S(1)}, u32[]{:S(2)}, u32[]{:S(2)}) collective-permute-start(bf16[4,128,256]{2,1,0:T(8,128)(2,1)S(1)} %get-tuple-element.21), channel_id=1, source_target_pairs={{0,2},{1,3},{2,0},{3,1},{4,6},{5,7},{6,4},{7,5},{8,10},{9,11},{10,... | collective-permute-start | bytes 786440 | tf_op jit(solution)/shard_map/ppermute | solution.py:238
  80.0 31.5 %copy-start.13 = (f32[1024]{0:T(1024)S(1)}, f32[1024]{0:T(1024)}, u32[]{:S(2)}) copy-start(f32[1024]{0:T(1024)} %param.16) | copy-start | bytes 12292
  80.0 31.5 %copy-start.14 = (f32[256]{0:T(256)S(1)}, f32[256]{0:T(256)}, u32[]{:S(2)}) copy-start(f32[256]{0:T(256)} %param.14) | copy-start | bytes 3076
  80.0 31.5 %copy-start.15 = (f32[256]{0:T(256)S(1)}, f32[256]{0:T(256)}, u32[]{:S(2)}) copy-start(f32[256]{0:T(256)} %param.13) | copy-start | bytes 3076
  80.0 31.5 %copy-start.16 = (f32[256]{0:T(256)S(1)}, f32[256]{0:T(256)}, u32[]{:S(2)}) copy-start(f32[256]{0:T(256)} %param.12) | copy-start | bytes 3076
  80.0 40.7 %copy-start.4 = (bf16[4,128,256]{2,1,0:T(8,128)(2,1)S(1)}, bf16[4,128,256]{2,1,0:T(8,128)(2,1)}, u32[]{:S(2)}) copy-start(bf16[4,128,256]{2,1,0:T(8,128)(2,1)} %copy-done.3) | copy-start | bytes 786436
  80.0 12.8 %collective-permute-start.8 = (bf16[4,128,256]{2,1,0:T(8,128)(2,1)S(1)}, bf16[4,128,256]{2,1,0:T(8,128)(2,1)S(1)}, u32[]{:S(2)}, u32[]{:S(2)}) collective-permute-start(bf16[4,128,256]{2,1,0:T(8,128)(2,1)S(1)} %get-tuple-element.22), channel_id=1, source_target_pairs={{0,3},{1,0},{2,1},{3,2},{4,7},{5,4},{6,5},{7,6},{8,11},{9,8},{10,9... | collective-permute-start | bytes 786440 | tf_op jit(solution)/shard_map/ppermute | solution.py:238
  87.7 33.0 %collective-permute-start.16 = (bf16[768,1024]{1,0:T(8,128)(2,1)}, bf16[768,1024]{1,0:T(8,128)(2,1)}, u32[]{:S(2)}, u32[]{:S(2)}) collective-permute-start(bf16[768,1024]{1,0:T(8,128)(2,1)} %constant_dynamic-update-slice_fusion.refs_7_), channel_id=1, source_target_pairs={{0,4},{4,0},{8,12},{12,8},{1,5},{5,1},{9,13},{13,9},{2,6},{6,2},{1... | collective-permute-start | bytes 4718600 | tf_op jit(solution)/shard_map/ppermute | solution.py:257
  87.8 0.7 copy-start.5
  88.5 13.7 %collective-permute-start.15 = (bf16[384,1024]{1,0:T(8,128)(2,1)S(1)}, bf16[384,1024]{1,0:T(8,128)(2,1)S(1)}, u32[]{:S(2)}, u32[]{:S(2)}) collective-permute-start(bf16[384,1024]{1,0:T(8,128)(2,1)S(1)} %get-tuple-element.29), channel_id=1, source_target_pairs={{56,0},{196,4},{0,16},{212,20},{16,32},{228,36},{32,48},{244,52},{... | collective-permute-start | bytes 2359304 | tf_op jit(solution)/shard_map/ppermute | solution.py:253
  92.8 0.7 copy-start.7
  93.5 17.6 %collective-permute-start.14 = (bf16[384,1024]{1,0:T(8,128)(2,1)S(1)}, bf16[384,1024]{1,0:T(8,128)(2,1)S(1)}, u32[]{:S(2)}, u32[]{:S(2)}) collective-permute-start(bf16[384,1024]{1,0:T(8,128)(2,1)S(1)} %get-tuple-element.30), channel_id=1, source_target_pairs={{16,0},{68,4},{32,16},{84,20},{48,32},{100,36},{8,48},{116,52},{24... | collective-permute-start | bytes 2359304 | tf_op jit(solution)/shard_map/ppermute | solution.py:253
  93.5 27.2 %collective-permute-start.18 = (bf16[768,1024]{1,0:T(8,128)(2,1)}, bf16[768,1024]{1,0:T(8,128)(2,1)}, u32[]{:S(2)}, u32[]{:S(2)}) collective-permute-start(bf16[768,1024]{1,0:T(8,128)(2,1)} %collective-permute-done.13.refs_9_), channel_id=1, source_target_pairs={{0,4},{4,0},{8,12},{12,8},{1,5},{5,1},{9,13},{13,9},{2,6},{6,2},{1... | collective-permute-start | bytes 4718600 | tf_op jit(solution)/shard_map/ppermute | solution.py:257
  102.0 18.7 %collective-permute-start.17 = (bf16[768,1024]{1,0:T(8,128)(2,1)}, bf16[768,1024]{1,0:T(8,128)(2,1)}, u32[]{:S(2)}, u32[]{:S(2)}) collective-permute-start(bf16[768,1024]{1,0:T(8,128)(2,1)} %collective-permute-done.12.refs_8_), channel_id=1, source_target_pairs={{0,4},{4,0},{8,12},{12,8},{1,5},{5,1},{9,13},{13,9},{2,6},{6,2},{1... | collective-permute-start | bytes 4718600 | tf_op jit(solution)/shard_map/ppermute | solution.py:257
  102.1 18.6 %collective-permute-start.20 = (bf16[384,1024]{1,0:T(8,128)(2,1)S(1)}, bf16[384,1024]{1,0:T(8,128)(2,1)}, u32[]{:S(2)}, u32[]{:S(2)}) collective-permute-start(bf16[384,1024]{1,0:T(8,128)(2,1)S(1)} %collective-permute-done.15.refs_11_), channel_id=1, source_target_pairs={{0,4},{4,0},{8,12},{12,8},{1,5},{5,1},{9,13},{13,9},{2,6},{6,2},{1... | collective-permute-start | bytes 2359304 | tf_op jit(solution)/shard_map/ppermute | solution.py:257
  111.1 9.6 %collective-permute-start.19 = (bf16[384,1024]{1,0:T(8,128)(2,1)S(1)}, bf16[384,1024]{1,0:T(8,128)(2,1)}, u32[]{:S(2)}, u32[]{:S(2)}) collective-permute-start(bf16[384,1024]{1,0:T(8,128)(2,1)S(1)} %collective-permute-done.14.refs_10_), channel_id=1, source_target_pairs={{0,4},{4,0},{8,12},{12,8},{1,5},{5,1},{9,13},{13,9},{2,6},{6,2},{1... | collective-permute-start | bytes 2359304 | tf_op jit(solution)/shard_map/ppermute | solution.py:257
  120.8 1.0 copy-start.6
  121.7 0.9 copy-start.8
  122.7 28.3 %copy-start.1 = (f32[256]{0:T(256)S(1)}, f32[256]{0:T(256)}, u32[]{:S(2)}) copy-start(f32[256]{0:T(256)} %param.19) | copy-start | bytes 3076
  122.7 28.3 %copy-start.2 = (f32[256]{0:T(256)S(1)}, f32[256]{0:T(256)}, u32[]{:S(2)}) copy-start(f32[256]{0:T(256)} %param.18) | copy-start | bytes 3076
  137.1 6.8 %collective-permute-start.21 = (bf16[512,256]{1,0:T(8,128)(2,1)S(1)}, bf16[512,256]{1,0:T(8,128)(2,1)S(1)}, u32[]{:S(2)}, u32[]{:S(2)}) collective-permute-start(bf16[512,256]{1,0:T(8,128)(2,1)S(1)} %get-tuple-element.24), channel_id=1, source_target_pairs={{0,1},{1,2},{2,3},{3,0},{4,5},{5,6},{6,7},{7,4},{8,9},{9,10},{10,1... | collective-permute-start | bytes 786440 | tf_op jit(solution)/shard_map/ppermute | solution.py:238
  138.3 11.2 %collective-permute-start.22 = (bf16[512,256]{1,0:T(8,128)(2,1)S(1)}, bf16[512,256]{1,0:T(8,128)(2,1)S(1)}, u32[]{:S(2)}, u32[]{:S(2)}) collective-permute-start(bf16[512,256]{1,0:T(8,128)(2,1)S(1)} %get-tuple-element.25), channel_id=1, source_target_pairs={{0,2},{1,3},{2,0},{3,1},{4,6},{5,7},{6,4},{7,5},{8,10},{9,11},{10,... | collective-permute-start | bytes 786440 | tf_op jit(solution)/shard_map/ppermute | solution.py:238
  140.7 10.3 %collective-permute-start.23 = (bf16[512,256]{1,0:T(8,128)(2,1)S(1)}, bf16[512,256]{1,0:T(8,128)(2,1)S(1)}, u32[]{:S(2)}, u32[]{:S(2)}) collective-permute-start(bf16[512,256]{1,0:T(8,128)(2,1)S(1)} %get-tuple-element.26), channel_id=1, source_target_pairs={{0,3},{1,0},{2,1},{3,2},{4,7},{5,4},{6,5},{7,6},{8,11},{9,8},{10,9... | collective-permute-start | bytes 786440 | tf_op jit(solution)/shard_map/ppermute | solution.py:238

commit v2 on v0

v2 whole, which is shorter than its diff:
```python
import functools
import jax
import jax.numpy as jnp
from jax import lax
from jax.experimental import pallas as pl
from jax.experimental.pallas import tpu as pltpu
from jax.sharding import PartitionSpec as P

F32 = jnp.float32
BF = jnp.bfloat16
VM = pl.BlockSpec(memory_space=pltpu.VMEM)
SM = pl.BlockSpec(memory_space=pltpu.SMEM)
HB = pl.BlockSpec(memory_space=pl.ANY)
NT = (((1,), (1,)), ((), ()))
CB = 32


def params(mib):
    return pltpu.CompilerParams(vmem_limit_bytes=mib << 20)


def turn_kernel(sc, x_ref, xt_ref, a_ref, b_ref, xf):
    xf[...] = x_ref[...].astype(F32).reshape(4096, 128)
    for r in range(16):
        for h in range(2):
            t = xf[pl.ds(h * 2048 + r, 128, stride=16), :]
            xt_ref[r, :, h * 128 : (h + 1) * 128] = t.T.astype(BF)
    for j in range(3):
        js = slice(j * 256, (j + 1) * 256)
        low, high = xt_ref[:, j, :].astype(F32), xt_ref[:, 125 + j, :].astype(F32)
        a_ref[:, js] = jnp.where(sc[1] == 0, high, low).astype(BF)
        b_ref[:, js] = jnp.where(sc[1] == 0, low, high).astype(BF)


def turn(sc, x):
    edge = jax.ShapeDtypeStruct((16, 768), BF)
    return pl.pallas_call(
        turn_kernel,
        out_shape=(jax.ShapeDtypeStruct((16, 128, 256), BF), edge, edge),
        in_specs=[SM, VM],
        out_specs=(VM, VM, VM),
        scratch_shapes=[pltpu.VMEM((4096, 128), F32)],
        compiler_params=params(16),
        cost_estimate=pl.CostEstimate(flops=0, bytes_accessed=4 << 20, transcendentals=0),
        name="turn",
    )(sc, x)


def pack_kernel(xt_ref, a_ref, b_ref, r1_ref, r3_ref, down_ref, up_ref, relay_up, relay_down):
    for r in range(3):
        down_ref[r * 128 : (r + 1) * 128, :] = xt_ref[13 + r]
        up_ref[r * 128 : (r + 1) * 128, :] = xt_ref[r]
    edges = [
        edge[:, j * 256 : (j + 1) * 256].astype(F32) for edge in (a_ref, b_ref) for j in range(3)
    ]
    none = jnp.zeros((8, 256), F32)
    down_ref[384:416, :] = jnp.concatenate([v[12:16] for v in edges] + [none]).astype(BF)
    up_ref[384:416, :] = jnp.concatenate([v[0:4] for v in edges] + [none]).astype(BF)
    relay_up[...] = r1_ref[0:128, :]
    relay_down[...] = r3_ref[128:256, :]


def pack(xt, a, b, r1, r3):
    o = jax.ShapeDtypeStruct((416, 256), BF)
    w = jax.ShapeDtypeStruct((128, 1024), BF)
    return pl.pallas_call(
        pack_kernel,
        out_shape=(o, o, w, w),
        in_specs=[VM] * 5,
        out_specs=(VM,) * 4,
        compiler_params=params(16),
        cost_estimate=pl.CostEstimate(flops=0, bytes_accessed=2 << 20, transcendentals=0),
        name="pack",
    )(xt, a, b, r1, r3)


def cut_kernel(sc, w_in, w_out, piece, sems):
    start = pl.multiple_of(sc[8], 128)
    copies = [
        pltpu.make_async_copy(w.at[pl.ds(start, 128)], piece.at[128 * i : 128 * i + 128], sems.at[i])
        for i, w in enumerate((w_in, w_out))
    ]
    for copy in copies:
        copy.start()
    for copy in copies:
        copy.wait()


def cut(sc, w_in, w_out):
    return pl.pallas_call(
        cut_kernel,
        out_shape=jax.ShapeDtypeStruct((256, 1024), BF),
        in_specs=[SM, HB, HB],
        out_specs=VM,
        scratch_shapes=[pltpu.SemaphoreType.DMA((2,))],
        compiler_params=params(60),
        cost_estimate=pl.CostEstimate(flops=0, bytes_accessed=1 << 20, transcendentals=0),
        name="cut",
    )(sc, w_in, w_out)


def taps(sc, xs, kw_ref, edge, sums, outs):
    @pl.loop(0, 8)
    def _(step):
        h, k = lax.rem(step, 2), step // 2
        q = lax.rem(sc[0] + k, 4)
        row0 = 2 * q + 6 * (q // 2) if edge else 2 * q
        for c0 in range(0, 128, CB):
            acc = [jnp.zeros((CB, 128), F32) for _ in range(2)]
            for b in range(7):
                for ri in range(8):
                    xv = xs[h, row0 + ri, c0 + 5 + b : c0 + 5 + b + CB, :]
                    for ro in range(2):
                        a = ri - ro
                        if 0 <= a < 7:
                            acc[ro] = acc[ro] + kw_ref[h, a * 7 + b : a * 7 + b + 1, :] * xv
            for ro in range(2):
                sums[k, h, ro * 128 + c0 : ro * 128 + c0 + CB, :] = acc[ro].astype(BF)

    for k, o in enumerate(outs):
        for h in range(2):
            o[0:256, h * 128 : (h + 1) * 128] = sums[k, h]


def columns(sc, a, b):
    a, b, first = a.astype(F32), b.astype(F32), sc[1] == 0
    low = jnp.where(sc[6] > 0, jnp.where(first, b, a), 0.0)
    high = jnp.where(sc[7] > 0, jnp.where(first, a, b), 0.0)
    return low, high


def inner_kernel(sc, xt_ref, a_ref, b_ref, kw_ref, o0, o1, o2, o3, xs, sums):
    for h in range(2):
        hs = slice(h * 128, (h + 1) * 128)
        for r in range(14):
            xs[h, r, 8:136, :] = xt_ref[1 + r, :, hs].astype(F32)
        for j in range(3):
            js = slice(j * 256 + h * 128, j * 256 + (h + 1) * 128)
            low, high = columns(sc, a_ref[:, js], b_ref[:, js])
            xs[h, :, 5 + j, :] = low[1:15]
            xs[h, :, 136 + j, :] = high[1:15]
    taps(sc, xs, kw_ref, False, sums, (o0, o1, o2, o3))


def edge_kernel(
    sc, xt_ref, a_ref, b_ref, top_ref, bot_ref, kw_ref, p_ref, o0, o1, o2, o3, xs, sums
):
    up, down = sc[4] > 0, sc[5] > 0
    for h in range(2):
        hs = slice(h * 128, (h + 1) * 128)
        for r in range(7):
            xs[h, 3 + r, 8:136, :] = xt_ref[r, :, hs].astype(F32)
            xs[h, 10 + r, 8:136, :] = xt_ref[9 + r, :, hs].astype(F32)
        for r in range(3):
            rs = slice(r * 128, (r + 1) * 128)
            xs[h, r, 8:136, :] = jnp.where(up, top_ref[rs, hs].astype(F32), 0.0)
            xs[h, 17 + r, 8:136, :] = jnp.where(down, bot_ref[rs, hs].astype(F32), 0.0)
        tc, bc = top_ref[384:416, hs].astype(F32), bot_ref[384:416, hs].astype(F32)
        for j in range(3):
            js = slice(j * 256 + h * 128, j * 256 + (h + 1) * 128)
            sides = columns(sc, a_ref[:, js], b_ref[:, js])
            ra, rb = slice(4 * j, 4 * j + 4), slice(12 + 4 * j, 16 + 4 * j)
            tops = columns(sc, tc[ra], tc[rb])
            bots = columns(sc, bc[ra], bc[rb])
            for at, v, t, d in zip((5 + j, 136 + j), sides, tops, bots):
                xs[h, 3:10, at, :] = v[0:7]
                xs[h, 10:17, at, :] = v[9:16]
                xs[h, 0:3, at, :] = jnp.where(up, t, 0.0)[1:4]
                xs[h, 17:20, at, :] = jnp.where(down, d, 0.0)[0:3]
    for o in (o0, o1, o2, o3):
        o[256:288] = p_ref[...]
    taps(sc, xs, kw_ref, True, sums, (o0, o1, o2, o3))


def conv_inner(sc, *args):
    o = jax.ShapeDtypeStruct((256, 256), BF)
    return pl.pallas_call(
        inner_kernel,
        out_shape=(o,) * 4,
        in_specs=[SM] + [VM] * 4,
        out_specs=(VM,) * 4,
        scratch_shapes=[pltpu.VMEM((2, 14, 144, 128), F32), pltpu.VMEM((4, 2, 256, 128), BF)],
        compiler_params=params(16),
        cost_estimate=pl.CostEstimate(flops=30_000_000, bytes_accessed=4 << 20, transcendentals=0),
        name="conv_inner",
    )(sc, *args)


def conv_edge(sc, *args):
    o = jax.ShapeDtypeStruct((288, 256), BF)
    return pl.pallas_call(
        edge_kernel,
        out_shape=(o,) * 4,
        in_specs=[SM] + [VM] * 7,
        out_specs=(VM,) * 4,
        scratch_shapes=[pltpu.VMEM((2, 20, 144, 128), F32), pltpu.VMEM((4, 2, 256, 128), BF)],
        compiler_params=params(16),
        cost_estimate=pl.CostEstimate(flops=30_000_000, bytes_accessed=4 << 20, transcendentals=0),
        name="conv_edge",
    )(sc, *args)


def gelu(p):
    return 0.5 * p * (1.0 + lax.erf(p * 0.7071067811865476))


def norm_kernel(sc, i0, i1, i2, i3, e0, e1, e2, e3, n_ref, bias):
    sides = []
    for k, (inner, edge) in enumerate(((i0, e0), (i1, e1), (i2, e2), (i3, e3))):
        p = sum(edge[256 + 8 * t : 264 + 8 * t, :].astype(F32) for t in (2, 1, 0))
        for i in range(8):
            bias[(4 - k) % 4, i] = p[3 + i // 2 : 4 + i // 2, i % 2 * 128 : i % 2 * 128 + 128]
        sides.append((inner, edge, p))
    for part in range(2):
        @pl.loop(0, 2)
        def _(step):
            rows = pl.ds(pl.multiple_of(step * 128, 128), 128)
            total = jnp.zeros((128, 1), F32)
            squares = jnp.zeros((128, 1), F32)
            for *m, p in sides:
                v = m[part][rows, :].astype(F32) + p[0:1]
                total = total + jnp.sum(v, axis=1, keepdims=True)
                squares = squares + jnp.sum(v * v, axis=1, keepdims=True)
            mean = total * (1.0 / 1024)
            rstd = lax.rsqrt(squares * (1.0 / 1024) - mean * mean + 1e-06)
            at = pl.ds(pl.multiple_of(256 * part + step * 128, 128), 128)
            for k, (*m, p) in enumerate(sides):
                q = lax.rem(sc[0] + 4 - k, 4)
                v = m[part][rows, :].astype(F32) + p[0:1]
                v = (v - mean) * rstd * p[1:2] + p[2:3]
                n_ref[at, pl.ds(pl.multiple_of(q * 256, 256), 256)] = v.astype(BF)


def norm(sc, inner, edge):
    return pl.pallas_call(
        norm_kernel,
        out_shape=(
            jax.ShapeDtypeStruct((512, 1024), BF),
            jax.ShapeDtypeStruct((4, 8, 1, 128), F32),
        ),
        in_specs=[SM] + [VM] * 8,
        out_specs=(VM, VM),
        compiler_params=params(16),
        cost_estimate=pl.CostEstimate(flops=1 << 23, bytes_accessed=2 << 20, transcendentals=0),
        name="norm",
    )(sc, *inner, *edge)


def blocks(pixels, acc, at, items, out):
    items = [(win, wout, jnp.concatenate(bias, axis=1)) for win, wout, bias in items]

    @pl.loop(0, 2 * len(pixels))
    def _(step):
        rows = pl.ds(pl.multiple_of(lax.rem(step, 2) * 256, 256), 256)
        n = pixels[0][rows, :]
        if len(pixels) > 1:
            n = jnp.where(step < 2, n, pixels[1][rows, :])
        total = None
        for win, wout, bias in items:
            pre = lax.dot_general(n, win[...], NT, preferred_element_type=F32)
            h = gelu(pre + bias).astype(BF)
            part = jnp.dot(h, wout[...], preferred_element_type=F32)
            total = part if total is None else total + part
        here = pl.ds(pl.multiple_of(step * 256, 256), 256)
        there = pl.ds(pl.multiple_of(at + step * 256, 256), 256)
        for q in range(4):
            part = total[:, q * 256 : (q + 1) * 256]
            if acc is not None:
                part = part + acc[q, there, :]
            out[q, here, :] = part.astype(out.dtype)


def shards_bias(sc, bias, shift):
    color = jnp.where(sc[1] == 0, sc[2], sc[3])
    return [bias[k, sc[1] * 4 + lax.rem(color + shift, 4)] for k in (1, 2, 3)]


def first_kernel(sc, n_ref, n_other, bias, w_in, w_out, held, out):
    own = pl.ds(pl.multiple_of(sc[1] * 512, 512), 512)
    values = [bias[0, sc[1] * 4 + c] for c in range(4)]
    items = [(w_in.at[own], w_out.at[own], values)]
    items += [(held.at[0:384], held.at[384:768], shards_bias(sc, bias, 0))]
    blocks((n_ref, n_other), None, 0, items, out)


def middle_kernel(sc, n_ref, n_other, bias, acc, plus, minus, out):
    items = [
        (w.at[0:384], w.at[384:768], shards_bias(sc, bias, shift))
        for w, shift in ((plus, 1), (minus, 3))
    ]
    blocks((n_ref, n_other), acc, 0, items, out)


def last_kernel(at, sc, n_ref, bias, acc, low, high, out):
    blocks((n_ref,), acc, at, [(low, high, shards_bias(sc, bias, 2))], out)


def mlp(kernel, sc, arrays, size, rows, out, name):
    return pl.pallas_call(
        kernel,
        out_shape=jax.ShapeDtypeStruct((4, rows, 256), out),
        in_specs=[SM] + [VM] * len(arrays),
        out_specs=VM,
        compiler_params=params(20),
        cost_estimate=pl.CostEstimate(
            flops=4_000 * size * rows, bytes_accessed=6 << 20, transcendentals=size * rows
        ),
        name=name,
    )(sc, *arrays)


def add_kernel(sc, acc, other, o0, o1, o2, o3):
    for k, o in enumerate((o0, o1, o2, o3)):
        q = lax.rem(sc[0] + k, 4)
        o[...] = (acc[q] + other[q].astype(F32)).astype(BF)


def add(sc, acc, other):
    return pl.pallas_call(
        add_kernel,
        out_shape=(jax.ShapeDtypeStruct((512, 256), BF),) * 4,
        in_specs=[SM, VM, VM],
        out_specs=(VM,) * 4,
        compiler_params=params(16),
        cost_estimate=pl.CostEstimate(flops=1 << 20, bytes_accessed=4 << 20, transcendentals=0),
        name="add",
    )(sc, acc, other)


def join_kernel(r1, ra, rb, r3, held, low, high, sems):
    moves = [(r1.at[0:128], 0), (ra, 128), (r3.at[0:128], 256)]
    moves += [(r1.at[128:256], 384), (rb, 512), (r3.at[128:256], 640)]
    copies = []
    for i, (src, at) in enumerate(moves):
        half, base = (low, at) if at < 384 else (high, at - 384)
        copies.append(pltpu.make_async_copy(src, held.at[at : at + 128], sems.at[2 * i]))
        copies.append(pltpu.make_async_copy(src, half.at[base : base + 128], sems.at[2 * i + 1]))
    for copy in copies:
        copy.start()
    for copy in copies:
        copy.wait()


def join(*pieces):
    half = jax.ShapeDtypeStruct((384, 1024), BF)
    return pl.pallas_call(
        join_kernel,
        out_shape=(jax.ShapeDtypeStruct((768, 1024), BF), half, half),
        in_specs=[HB] * 4,
        out_specs=(HB,) * 3,
        scratch_shapes=[pltpu.SemaphoreType.DMA((12,))],
        compiler_params=params(16),
        cost_estimate=pl.CostEstimate(flops=0, bytes_accessed=6 << 20, transcendentals=0),
        name="join",
    )(*pieces)


def final_kernel(sc, x_ref, ls_ref, bo_ref, f0, f1, f2, f3, o_ref, t):
    for k, f in enumerate((f0, f1, f2, f3)):
        q = lax.rem(sc[0] + 4 - k, 4)
        inner, edge = 4 + 2 * q, 2 * q + 8 * (q // 2)
        for i in range(4):
            row = inner + i if i < 2 else edge + i - 2
            v = f[i * 128 : (i + 1) * 128, :].astype(F32)
            v = ls_ref[...] * (v + bo_ref[...])
            for h in range(2):
                t[pl.ds(h * 2048 + row, 128, stride=16), :] = v[
                    :, h * 128 : (h + 1) * 128
                ].T
    o_ref[...] = (x_ref[...].astype(F32) + t[...].reshape(256, 16, 128)).astype(BF)


def final(sc, x, ls, bo, parts):
    return pl.pallas_call(
        final_kernel,
        out_shape=jax.ShapeDtypeStruct((256, 16, 128), BF),
        in_specs=[SM] + [VM] * 7,
        out_specs=VM,
        scratch_shapes=[pltpu.VMEM((4096, 128), F32)],
        compiler_params=params(16),
        cost_estimate=pl.CostEstimate(flops=1 << 20, bytes_accessed=4 << 20, transcendentals=0),
        name="final",
    )(sc, x, ls, bo, *parts)


def from_hid(x, k):
    return lax.ppermute(x, "hid", [((i + k) % 4, i) for i in range(4)])


def to_hid(x, k):
    return lax.ppermute(x, "hid", [(i, (i + k) % 4) for i in range(4)])


def place(x, z, core):
    return (x * 4 + z % 4) * 4 + (z // 4) * 2 + core


def from_plane(v, step, major):
    pairs = []
    for x in range(4):
        for z in range(8):
            for core in range(2):
                along_x = (core == 0) == major
                sx, sz = ((x + step) % 4, z) if along_x else (x, (z + step) % 8)
                pairs.append((place(sx, sz, core), place(x, z, core)))
    return lax.ppermute(v, ("row", "col"), pairs)


def from_core(v):
    return lax.ppermute(v, "col", [(0, 1), (1, 0), (2, 3), (3, 2)])


def around(v, up):
    return lax.ppermute(v, "row", [(i, (i + (1 if up else -1)) % 16) for i in range(16)])


def from_chip(v):
    return lax.ppermute(v, "col", [(1, 2), (2, 1), (0, 3), (3, 0)])


def after(values, *others):
    values = tuple(values)
    return lax.optimization_barrier(values + others)[: len(values)]


def on_device(
    features, dw_kernel, dw_bias, norm_gain, norm_bias, w_in, b_in, w_out, b_out, layer_scale
):
    row, col, y = lax.axis_index("row"), lax.axis_index("col"), lax.axis_index("hid")
    x, zl, core = row // 4, row % 4, col % 2
    c0, c1 = (x + 2 * zl) % 4, (2 * x + zl) % 4
    color = jnp.where(core == 0, c0, c1)
    start = 512 * core + 128 * color
    sc = jnp.stack([y, core, c0, c1, row, 15 - row, col, 3 - col, start]).astype(jnp.int32)

    piece = cut(sc, w_in, w_out)
    r1, r3 = from_hid(piece, 1), from_hid(piece, 3)

    xt, send_a, send_b = turn(sc, features)
    a, b = from_core(send_a), from_chip(send_b)
    kw = jnp.transpose(dw_kernel.reshape(2, 128, 49), (0, 2, 1))
    small = jnp.concatenate([dw_bias, norm_gain, norm_bias, b_in]).reshape(7, 256)
    small = jnp.pad(small, ((0, 1), (0, 0)))
    high = lax.reduce_precision(small, 8, 7)
    middle = lax.reduce_precision(small - high, 8, 7)
    lowest = small - high - middle
    small = jnp.concatenate([high, middle, lowest, jnp.zeros_like(high)]).astype(BF)
    b, kw, small = after([b, kw, small])
    down, up, ra, rb = pack(xt, a, b, r1, r3)
    top, bot = around(down, True), around(up, False)
    ra, rb = from_hid(ra, 1), from_hid(rb, 3)

    inner = conv_inner(sc, xt, a, b, kw)
    inner = [inner[0]] + [to_hid(inner[k], k) for k in (1, 2, 3)]
    held, low, high = join(r1, ra, rb, r3)
    plane = [
        from_plane(held, 1, True),
        from_plane(held, -1, True),
        from_plane(low, 1, False),
        from_plane(high, -1, False),
    ]
    top, bot = after([top, bot], held)
    edge = conv_edge(sc, xt, a, b, top, bot, kw, small)
    edge = [edge[0]] + [to_hid(edge[k], k) for k in (1, 2, 3)]

    n, bias = norm(sc, inner, edge)
    n_other = from_core(n)
    plus, minus, low, high = plane
    acc = mlp(first_kernel, sc, [n, n_other, bias, w_in, w_out, held], 896, 1024, F32, "mlp_first")
    plus, minus, acc = after([plus, minus, acc])
    acc = mlp(middle_kernel, sc, [n, n_other, bias, acc, plus, minus], 768, 1024, F32, "mlp_mid")
    low, high, acc = after([low, high, acc])
    last = functools.partial(last_kernel, 512)
    other = mlp(last, sc, [n_other, bias, acc, low, high], 384, 512, BF, "mlp_last_other")
    back = from_core(other)
    (acc,) = after([acc], other)
    last = functools.partial(last_kernel, 0)
    acc = mlp(last, sc, [n, bias, acc, low, high], 384, 512, F32, "mlp_last")
    parts = add(sc, acc, back)
    parts = [parts[0]] + [to_hid(parts[k], k) for k in (1, 2, 3)]
    return final(sc, features, layer_scale[None, :], b_out[None, :], parts)


def solution(mesh):
    return jax.shard_map(
        on_device,
        mesh=mesh,
        in_specs=(
            P("hid", "row", "col"),
            P("hid", None, None),
            P("hid"),
            P("hid"),
            P("hid"),
            P("hid", None),
            P("hid"),
            P("hid", None),
            P("hid"),
            P("hid"),
        ),
        out_specs=P("hid", "row", "col"),
        check_vma=False,
    )
```

time: 258 us -> 98 us (0.38)
  waiting for transfers between devices: 122 us -> 18.4 us
  other arithmetic: 57.6 us -> 0.09 us
  Pallas kernels: 0 us -> 36.6 us
  matrix products: 28.6 us -> 0 us
  starting transfers between devices: 16.6 us -> 41.7 us
  blocking collectives: 13.4 us -> 0 us
  between operations: 13.6 us -> 0.29 us
  local copies, waits for them, and re-layouts: 5.77 us -> 0.8 us
    reduce_scatter x1 -> x0, waiting for transfers between devices: 51.4 us -> none  [on_device(): lax.psum_scatter(lax.dot_general(w_out, hidden, (((0,), (0,)), ((), ())),...]
    all_gather x1 -> x0, waiting for transfers between devices: 50.5 us -> none  [on_device(): gathered = lax.all_gather(normed, 'hid', axis=0, tiled=True)]
    reduce_sum x1 -> x0, other arithmetic: 48.6 us -> none  [on_device(): jnp.sum(mixed, axis=0)]
    pallas_call x0 -> x13, Pallas kernels: none -> 36.6 us  [the longest x4 16.9 us: mlp(): pl.pallas_call(kernel, out_shape=jax.ShapeDtypeStruct((4, rows, 256), out...]
    dot_general x1 -> x0, matrix products: 28.6 us -> none  [on_device(): lax.dot_general(w_out, hidden, (((0,), (0,)), ((), ())), preferred_elemen...]
    ppermute x4 -> x23, starting transfers between devices: 16.6 us -> 41.7 us  [the longest x9 12 us: to_hid(): return lax.ppermute(x, 'hid', [(i, (i + k) % 4) for i in range(4)])]
    psum x1 -> x0, blocking collectives: 13.4 us -> none  [on_device(): lax.psum((jnp.sum(mixed, axis=0), jnp.sum(mixed * mixed, axis=0)), 'hid')]
    convert_element_type x3 -> x0, other arithmetic: 8.05 us -> none  [the longest x1 3.28 us: on_device(): return result.astype(jnp.bfloat16)]
  transfers between devices with their start and end apart: 6 -> 23, of which waited for: 5 -> 6; matrix products, arithmetic and copies ran while one was open for 0% -> 0% of each run, Pallas kernels for 0% -> 28%
where the time goes in v2:
time: 98 us; the launch traced here: 97.9 us
  starting transfers between devices  41.7 us (43%)
  Pallas kernels  36.6 us (37%)
  waiting for transfers between devices  18.4 us (19%)
    pallas_call x4, Pallas kernels, mlp(): pl.pallas_call(kernel, out_shape=jax.ShapeDtypeStruct((4, rows, 256), out...  16.9 us
    ppermute x9, waiting for transfers between devices, to_hid(): return lax.ppermute(x, 'hid', [(i, (i + k) % 4) for i in range(4)])  15.8 us
    ppermute x9, starting transfers between devices, to_hid(): return lax.ppermute(x, 'hid', [(i, (i + k) % 4) for i in range(4)])  12 us
    ppermute x3, starting transfers between devices, from_core(): return lax.ppermute(v, 'col', [(0, 1), (1, 0), (2, 3), (3, 2)])  7.56 us
    ppermute x2, starting transfers between devices, around(): lax.ppermute(v, 'row', [(i, (i + (1 if up else -1)) % 16) for i in range(...  7.55 us
    ppermute x4, starting transfers between devices, from_hid(): return lax.ppermute(x, 'hid', [((i + k) % 4, i) for i in range(4)])  5.27 us
    ppermute x1, starting transfers between devices, from_chip(): return lax.ppermute(v, 'col', [(1, 2), (2, 1), (0, 3), (3, 0)])  5.16 us
    pallas_call x1, Pallas kernels, conv_edge(): pl.pallas_call(edge_kernel, out_shape=(o,) * 4, in_specs=[SM] + [VM] * 7,...  4.84 us
  transfers between devices with their start and end apart: 23, of which 6 were waited for; matrix products, arithmetic and copies ran while one was open for 0% of the time, Pallas kernels for 28%

profile of v2, /device:TPU:1, one launch (start us, length us, event | category | flops | bytes accessed | tf_op | source)
XLA Modules:
  0.0 97.9 jit_solution(11654363309995772246)
XLA Ops:
  0.0 0.6 stack.39.sc
  0.6 0.0 copy-start.9
  0.7 0.0 copy-start.10
  0.7 0.0 copy-start.6
  0.7 2.6 %cut.1 = bf16[256,1024]{1,0:T(8,128)(2,1)} custom-call(s32[9]{0:T(128)} %stack.39.sc, bf16[1024,1024]{1,0:T(8,128)(2,1)} %w_in.3, bf16[1024,1024]{1,0:T(8,128)(2,1)} %w_out.3), custom_call_target="tpu_custom_call" | custom-call | bytes 1048576 | tf_op jit(solution)/shard_map/cut/pallas_call | solution.py:90
  3.3 2.2 %collective-permute-start.6 = (bf16[256,1024]{1,0:T(8,128)(2,1)}, bf16[256,1024]{1,0:T(8,128)(2,1)S(1)}, u32[]{:S(2)}, u32[]{:S(2)}) collective-permute-start(bf16[256,1024]{1,0:T(8,128)(2,1)} %cut.1), channel_id=1, source_target_pairs={{3,0},{0,1},{1,2},{2,3},{7,4},{4,5},{5,6},{6,7},{11,8},{8,9},{9,10... | collective-permute-start | bytes 1572872 | tf_op jit(solution)/shard_map/ppermute | solution.py:387
  5.5 1.5 %collective-permute-start.5 = (bf16[256,1024]{1,0:T(8,128)(2,1)}, bf16[256,1024]{1,0:T(8,128)(2,1)S(1)}, u32[]{:S(2)}, u32[]{:S(2)}) collective-permute-start(bf16[256,1024]{1,0:T(8,128)(2,1)} %cut.1), channel_id=1, source_target_pairs={{1,0},{2,1},{3,2},{0,3},{5,4},{6,5},{7,6},{4,7},{9,8},{10,9},{11,1... | collective-permute-start | bytes 1572872 | tf_op jit(solution)/shard_map/ppermute | solution.py:387
  7.1 1.5 %turn.1 = (bf16[16,128,256]{2,1,0:T(8,128)(2,1)S(1)}, bf16[16,768]{1,0:T(8,128)(2,1)S(1)}, bf16[16,768]{1,0:T(8,128)(2,1)S(1)}) custom-call(s32[9]{0:T(128)S(1)} %copy-done.3, bf16[256,16,128]{2,1,0:T(8,128)(2,1)S(1)} %copy-done), custom_call_target="tpu_custom_call" | custom-call | bytes 4194304 | tf_op jit(solution)/shard_map/turn/pallas_call | solution.py:37
  8.5 2.9 %collective-permute-start = (bf16[16,768]{1,0:T(8,128)(2,1)S(1)}, bf16[16,768]{1,0:T(8,128)(2,1)S(1)}, u32[]{:S(2)}, u32[]{:S(2)}) collective-permute-start(bf16[16,768]{1,0:T(8,128)(2,1)S(1)} %get-tuple-element.42), channel_id=1, source_target_pairs={{0,4},{4,0},{8,12},{12,8},{1,5},{5,1},{9,13},{13,9},{2,6},{6,2},{1... | collective-permute-start | bytes 73736 | tf_op jit(solution)/shard_map/ppermute | solution.py:410
  11.4 5.2 %collective-permute-start.1 = (bf16[16,768]{1,0:T(8,128)(2,1)S(1)}, bf16[16,768]{1,0:T(8,128)(2,1)S(1)}, u32[]{:S(2)}, u32[]{:S(2)}) collective-permute-start(bf16[16,768]{1,0:T(8,128)(2,1)S(1)} %get-tuple-element.43), channel_id=1, source_target_pairs={{4,8},{8,4},{0,12},{12,0},{5,9},{9,5},{1,13},{13,1},{6,10},{10,6},... | collective-permute-start | bytes 73736 | tf_op jit(solution)/shard_map/ppermute | solution.py:418
  16.7 0.1 pad.8.clone
  16.7 0.1 maximum_maximum_fusion.p_ref
  16.9 1.8 %collective-permute-done.1.b_ref = bf16[16,768]{1,0:T(8,128)(2,1)S(1)} collective-permute-done((bf16[16,768]{1,0:T(8,128)(2,1)S(1)}, bf16[16,768]{1,0:T(8,128)(2,1)S(1)}, u32[]{:S(2)}, u32[]{:S(2)}) %collective-permute-start.1) | collective-permute-done | bytes 24608 | tf_op jit(solution)/shard_map/ppermute | solution.py:418
  18.6 0.1 pack.1
  18.7 1.4 %collective-permute-start.9 = (bf16[128,1024]{1,0:T(8,128)(2,1)S(1)}, bf16[128,1024]{1,0:T(8,128)(2,1)S(1)}, u32[]{:S(2)}, u32[]{:S(2)}) collective-permute-start(bf16[128,1024]{1,0:T(8,128)(2,1)S(1)} %get-tuple-element.52), channel_id=1, source_target_pairs={{1,0},{2,1},{3,2},{0,3},{5,4},{6,5},{7,6},{4,7},{9,8},{10,9},{11,1... | collective-permute-start | bytes 786440 | tf_op jit(solution)/shard_map/ppermute | solution.py:387
  20.1 0.1 collective-permute-start.10
  20.3 2.6 %collective-permute-start.7 = (bf16[416,256]{1,0:T(8,128)(2,1)S(1)}, bf16[416,256]{1,0:T(8,128)(2,1)S(1)}, u32[]{:S(2)}, u32[]{:S(2)}) collective-permute-start(bf16[416,256]{1,0:T(8,128)(2,1)S(1)} %get-tuple-element.50), channel_id=1, source_target_pairs={{0,16},{16,32},{32,48},{48,64},{64,80},{80,96},{96,112},{112,128},... | collective-permute-start | bytes 638984 | tf_op jit(solution)/shard_map/ppermute | solution.py:414
  22.9 4.9 %collective-permute-start.8 = (bf16[416,256]{1,0:T(8,128)(2,1)S(1)}, bf16[416,256]{1,0:T(8,128)(2,1)S(1)}, u32[]{:S(2)}, u32[]{:S(2)}) collective-permute-start(bf16[416,256]{1,0:T(8,128)(2,1)S(1)} %get-tuple-element.51), channel_id=1, source_target_pairs={{0,240},{16,0},{32,16},{48,32},{64,48},{80,64},{96,80},{112,96},{1... | collective-permute-start | bytes 638984 | tf_op jit(solution)/shard_map/ppermute | solution.py:414
  27.8 4.8 %conv_inner.1 = (bf16[256,256]{1,0:T(8,128)(2,1)S(1)}, bf16[256,256]{1,0:T(8,128)(2,1)S(1)}, bf16[256,256]{1,0:T(8,128)(2,1)S(1)}, bf16[256,256]{1,0:T(8,128)(2,1)S(1)}) custom-call(s32[9]{0:T(128)S(1)} %copy-done.3, bf16[16,128,256]{2,1,0:T(8,128)(2,1)S(1)} %get-tuple-element.41.xt_ref, bf16[16,768]{1,0:T(8,128)(2,1)S(1)} %collective-permute-done.a_ref, ...), custom_call_target="tpu_custom_call" | custom-call | flops 30000000 | bytes 4194304 | tf_op jit(solution)/shard_map/conv_inner/pallas_call | solution.py:177
  32.6 0.1 collective-permute-start.2
  32.7 3.8 %collective-permute-start.3 = (bf16[256,256]{1,0:T(8,128)(2,1)S(1)}, bf16[256,256]{1,0:T(8,128)(2,1)S(1)}, u32[]{:S(2)}, u32[]{:S(2)}) collective-permute-start(bf16[256,256]{1,0:T(8,128)(2,1)S(1)} %get-tuple-element.48), channel_id=1, source_target_pairs={{0,2},{1,3},{2,0},{3,1},{4,6},{5,7},{6,4},{7,5},{8,10},{9,11},{10,... | collective-permute-start | bytes 393224 | tf_op jit(solution)/shard_map/ppermute | solution.py:391
  36.6 0.4 join.1
  36.9 0.1 collective-permute-start.18
  37.0 2.7 %collective-permute-start.17 = (bf16[768,1024]{1,0:T(8,128)(2,1)S(1)}, bf16[768,1024]{1,0:T(8,128)(2,1)S(1)}, u32[]{:S(2)}, u32[]{:S(2)}) collective-permute-start(bf16[768,1024]{1,0:T(8,128)(2,1)S(1)} %get-tuple-element.54.held), channel_id=1, source_target_pairs={{64,0},{20,4},{80,16},{36,20},{96,32},{52,36},{112,48},{12,52},{72... | collective-permute-start | bytes 4718600 | tf_op jit(solution)/shard_map/ppermute | solution.py:406
  39.7 4.8 %conv_edge.1 = (bf16[288,256]{1,0:T(8,128)(2,1)S(1)}, bf16[288,256]{1,0:T(8,128)(2,1)S(1)}, bf16[288,256]{1,0:T(8,128)(2,1)S(1)}, bf16[288,256]{1,0:T(8,128)(2,1)S(1)}) custom-call(s32[9]{0:T(128)S(1)} %copy-done.3, bf16[16,128,256]{2,1,0:T(8,128)(2,1)S(1)} %get-tuple-element.41.xt_ref, bf16[16,768]{1,0:T(8,128)(2,1)S(1)} %collective-permute-done.a_ref, ...), custom_call_target="tpu_custom_call" | custom-call | flops 30000000 | bytes 4194304 | tf_op jit(solution)/shard_map/conv_edge/pallas_call | solution.py:191
  44.6 1.5 %collective-permute-start.11 = (bf16[288,256]{1,0:T(8,128)(2,1)S(1)}, bf16[288,256]{1,0:T(8,128)(2,1)S(1)}, u32[]{:S(2)}, u32[]{:S(2)}) collective-permute-start(bf16[288,256]{1,0:T(8,128)(2,1)S(1)} %get-tuple-element.59), channel_id=1, source_target_pairs={{0,1},{1,2},{2,3},{3,0},{4,5},{5,6},{6,7},{7,4},{8,9},{9,10},{10,1... | collective-permute-start | bytes 442376 | tf_op jit(solution)/shard_map/ppermute | solution.py:391
  46.1 2.0 %collective-permute-start.12 = (bf16[288,256]{1,0:T(8,128)(2,1)S(1)}, bf16[288,256]{1,0:T(8,128)(2,1)S(1)}, u32[]{:S(2)}, u32[]{:S(2)}) collective-permute-start(bf16[288,256]{1,0:T(8,128)(2,1)S(1)} %get-tuple-element.60), channel_id=1, source_target_pairs={{0,2},{1,3},{2,0},{3,1},{4,6},{5,7},{6,4},{7,5},{8,10},{9,11},{10,... | collective-permute-start | bytes 442376 | tf_op jit(solution)/shard_map/ppermute | solution.py:391
  48.1 0.5 collective-permute-start.13
  48.6 1.5 %collective-permute-done.11.e1 = bf16[288,256]{1,0:T(8,128)(2,1)S(1)} collective-permute-done((bf16[288,256]{1,0:T(8,128)(2,1)S(1)}, bf16[288,256]{1,0:T(8,128)(2,1)S(1)}, u32[]{:S(2)}, u32[]{:S(2)}) %collective-permute-start.11) | collective-permute-done | bytes 147488 | tf_op jit(solution)/shard_map/ppermute | solution.py:391
  50.1 2.9 %collective-permute-done.12.e2 = bf16[288,256]{1,0:T(8,128)(2,1)S(1)} collective-permute-done((bf16[288,256]{1,0:T(8,128)(2,1)S(1)}, bf16[288,256]{1,0:T(8,128)(2,1)S(1)}, u32[]{:S(2)}, u32[]{:S(2)}) %collective-permute-start.12) | collective-permute-done | bytes 147488 | tf_op jit(solution)/shard_map/ppermute | solution.py:391
  53.1 1.8 %norm.1 = (bf16[512,1024]{1,0:T(8,128)(2,1)S(1)}, f32[4,8,1,128]{3,2,1,0:T(1,128)S(1)}) custom-call(s32[9]{0:T(128)S(1)} %copy-done.3, bf16[256,256]{1,0:T(8,128)(2,1)S(1)} %get-tuple-element.46.i0, bf16[256,256]{1,0:T(8,128)(2,1)S(1)} %collective-permute-done.2.i1, bf16[256,256]{1,0:T(8,128)(2,1)S(1)} %collective-permute-done.3.i2, ...), custom_call_target="tpu_custom_call" | custom-call | flops 8388608 | bytes 2097152 | tf_op jit(solution)/shard_map/norm/pallas_call | solution.py:235
  54.9 4.1 %collective-permute-start.16 = (bf16[512,1024]{1,0:T(8,128)(2,1)S(1)}, bf16[512,1024]{1,0:T(8,128)(2,1)S(1)}, u32[]{:S(2)}, u32[]{:S(2)}) collective-permute-start(bf16[512,1024]{1,0:T(8,128)(2,1)S(1)} %get-tuple-element.62.n_ref), channel_id=1, source_target_pairs={{0,4},{4,0},{8,12},{12,8},{1,5},{5,1},{9,13},{13,9},{2,6},{6,2},{1... | collective-permute-start | bytes 3145736 | tf_op jit(solution)/shard_map/ppermute | solution.py:410
  59.0 0.0 collective-permute-start.14
  59.0 1.4 %collective-permute-start.15 = (bf16[384,1024]{1,0:T(8,128)(2,1)S(1)}, bf16[384,1024]{1,0:T(8,128)(2,1)S(1)}, u32[]{:S(2)}, u32[]{:S(2)}) collective-permute-start(bf16[384,1024]{1,0:T(8,128)(2,1)S(1)} %get-tuple-element.65), channel_id=1, source_target_pairs={{56,0},{196,4},{0,16},{212,20},{16,32},{228,36},{32,48},{244,52},{... | collective-permute-start | bytes 2359304 | tf_op jit(solution)/shard_map/ppermute | solution.py:406
  60.5 0.8 collective-permute-done.16.n_other.n_ref
  61.3 6.4 %mlp_first.1.acc = f32[4,1024,256]{2,1,0:T(8,128)S(1)} custom-call(s32[9]{0:T(128)S(1)} %copy-done.3, bf16[512,1024]{1,0:T(8,128)(2,1)S(1)} %get-tuple-element.62.n_ref, bf16[512,1024]{1,0:T(8,128)(2,1)S(1)} %collective-permute-done.16.n_other.n_ref, f32[4,8,1,128]{3,2,1,0:T(1,128)S(1)} %get-tuple-element.63.bias, bf16[1024,1024]{1,0:T(8,128)(2,1)S(1)} %copy-done.1, ...), custom_call_target="tpu_custom_call" | custom-call | flops 3670016000 | bytes 6291456 | tf_op jit(solution)/shard_map/mlp_first/pallas_call | solution.py:299
  67.7 6.0 %mlp_mid.1.acc = f32[4,1024,256]{2,1,0:T(8,128)S(1)} custom-call(s32[9]{0:T(128)S(1)} %copy-done.3, bf16[512,1024]{1,0:T(8,128)(2,1)S(1)} %get-tuple-element.62.n_ref, bf16[512,1024]{1,0:T(8,128)(2,1)S(1)} %collective-permute-done.16.n_other.n_ref, f32[4,8,1,128]{3,2,1,0:T(1,128)S(1)} %get-tuple-element.63.bias, f32[4,1024,256]{2,1,0:T(8,128)S(1)} %mlp_first.1.acc, ...), custom_call_target="tpu_custom_call" | custom-call | flops 3145728000 | bytes 6291456 | tf_op jit(solution)/shard_map/mlp_mid/pallas_call | solution.py:299
  73.7 2.3 %mlp_last_other.1 = bf16[4,512,256]{2,1,0:T(8,128)(2,1)S(1)} custom-call(s32[9]{0:T(128)S(1)} %copy-done.3, bf16[512,1024]{1,0:T(8,128)(2,1)S(1)} %collective-permute-done.16.n_other.n_ref, f32[4,8,1,128]{3,2,1,0:T(1,128)S(1)} %get-tuple-element.63.bias, f32[4,1024,256]{2,1,0:T(8,128)S(1)} %mlp_mid.1.acc, bf16[384,1024]{1,0:T(8,128)(2,1)S(1)} %collective-permute-done.14.low, ...), custom_call_target="tpu_custom_call" | custom-call | flops 786432000 | bytes 6291456 | tf_op jit(solution)/shard_map/mlp_last_other/pallas_call | solution.py:299
  76.0 0.6 collective-permute-start.19
  76.5 2.3 %mlp_last.1.acc = f32[4,512,256]{2,1,0:T(8,128)S(1)} custom-call(s32[9]{0:T(128)S(1)} %copy-done.3, bf16[512,1024]{1,0:T(8,128)(2,1)S(1)} %get-tuple-element.62.n_ref, f32[4,8,1,128]{3,2,1,0:T(1,128)S(1)} %get-tuple-element.63.bias, f32[4,1024,256]{2,1,0:T(8,128)S(1)} %mlp_mid.1.acc, bf16[384,1024]{1,0:T(8,128)(2,1)S(1)} %collective-permute-done.14.low, ...), custom_call_target="tpu_custom_call" | custom-call | flops 786432000 | bytes 6291456 | tf_op jit(solution)/shard_map/mlp_last/pallas_call | solution.py:299
  78.8 0.0 copy-start.4
  78.8 0.7 add.33
  79.6 1.3 %collective-permute-start.20 = (bf16[512,256]{1,0:T(8,128)(2,1)S(1)}, bf16[512,256]{1,0:T(8,128)(2,1)S(1)}, u32[]{:S(2)}, u32[]{:S(2)}) collective-permute-start(bf16[512,256]{1,0:T(8,128)(2,1)S(1)} %get-tuple-element.74), channel_id=1, source_target_pairs={{0,1},{1,2},{2,3},{3,0},{4,5},{5,6},{6,7},{7,4},{8,9},{9,10},{10,1... | collective-permute-start | bytes 786440 | tf_op jit(solution)/shard_map/ppermute | solution.py:391
  80.9 2.3 %collective-permute-start.21 = (bf16[512,256]{1,0:T(8,128)(2,1)S(1)}, bf16[512,256]{1,0:T(8,128)(2,1)S(1)}, u32[]{:S(2)}, u32[]{:S(2)}) collective-permute-start(bf16[512,256]{1,0:T(8,128)(2,1)S(1)} %get-tuple-element.75), channel_id=1, source_target_pairs={{0,2},{1,3},{2,0},{3,1},{4,6},{5,7},{6,4},{7,5},{8,10},{9,11},{10,... | collective-permute-start | bytes 786440 | tf_op jit(solution)/shard_map/ppermute | solution.py:391
  83.2 0.4 collective-permute-start.22
  83.6 4.8 %collective-permute-done.20.f1 = bf16[512,256]{1,0:T(8,128)(2,1)S(1)} collective-permute-done((bf16[512,256]{1,0:T(8,128)(2,1)S(1)}, bf16[512,256]{1,0:T(8,128)(2,1)S(1)}, u32[]{:S(2)}, u32[]{:S(2)}) %collective-permute-start.20) | collective-permute-done | bytes 262176 | tf_op jit(solution)/shard_map/ppermute | solution.py:391
  88.4 6.5 %collective-permute-done.21.f2 = bf16[512,256]{1,0:T(8,128)(2,1)S(1)} collective-permute-done((bf16[512,256]{1,0:T(8,128)(2,1)S(1)}, bf16[512,256]{1,0:T(8,128)(2,1)S(1)}, u32[]{:S(2)}, u32[]{:S(2)}) %collective-permute-start.21) | collective-permute-done | bytes 262176 | tf_op jit(solution)/shard_map/ppermute | solution.py:391
  94.9 3.0 %final.1 = bf16[256,16,128]{2,1,0:T(8,128)(2,1)} custom-call(s32[9]{0:T(128)S(1)} %copy-done.3, bf16[256,16,128]{2,1,0:T(8,128)(2,1)S(1)} %copy-done, f32[1,256]{1,0:T(1,128)S(1)} %bitcast.18, f32[1,256]{1,0:T(1,128)S(1)} %bitcast.19, bf16[512,256]{1,0:T(8,128)(2,1)S(1)} %get-tuple-element.73.f0, bf16[512,256]{1,0:T(8,128)(2,1)S(1)} %collective-permute-done.20.f1, ...), custom_call_target="tpu_custom_call" | custom-call | flops 1048576 | bytes 4194304 | tf_op jit(solution)/shard_map/final/pallas_call | solution.py:374
  (42 shorter events, 0.1 us)
Async XLA Ops:
  0.6 6.4 %copy-start = (bf16[256,16,128]{2,1,0:T(8,128)(2,1)S(1)}, bf16[256,16,128]{2,1,0:T(8,128)(2,1)}, u32[]{:S(2)}) copy-start(bf16[256,16,128]{2,1,0:T(8,128)(2,1)} %x_ref.3) | copy-start | bytes 3145732
  0.6 6.4 %copy-start.3 = (s32[9]{0:T(128)S(1)}, s32[9]{0:T(128)}, u32[]{:S(2)}) copy-start(s32[9]{0:T(128)} %stack.39.sc) | copy-start | bytes 112
  0.6 16.0 %copy-start.7 = (f32[1024]{0:T(1024)S(1)}, f32[1024]{0:T(1024)}, u32[]{:S(2)}) copy-start(f32[1024]{0:T(1024)} %param.16) | copy-start | bytes 12292
  0.6 16.0 %copy-start.8 = (f32[256]{0:T(256)S(1)}, f32[256]{0:T(256)}, u32[]{:S(2)}) copy-start(f32[256]{0:T(256)} %param.14) | copy-start | bytes 3076
  0.6 16.0 %copy-start.9 = (f32[256]{0:T(256)S(1)}, f32[256]{0:T(256)}, u32[]{:S(2)}) copy-start(f32[256]{0:T(256)} %param.13) | copy-start | bytes 3076
  0.7 16.0 %copy-start.10 = (f32[256]{0:T(256)S(1)}, f32[256]{0:T(256)}, u32[]{:S(2)}) copy-start(f32[256]{0:T(256)} %param.12) | copy-start | bytes 3076
  0.7 16.2 %copy-start.6 = (f32[256,7,7]{0,2,1:T(8,128)S(1)}, f32[256,7,7]{0,2,1:T(8,128)}, u32[]{:S(2)}) copy-start(f32[256,7,7]{0,2,1:T(8,128)} %param.11) | copy-start | bytes 150532
  3.3 15.3 %collective-permute-start.6 = (bf16[256,1024]{1,0:T(8,128)(2,1)}, bf16[256,1024]{1,0:T(8,128)(2,1)S(1)}, u32[]{:S(2)}, u32[]{:S(2)}) collective-permute-start(bf16[256,1024]{1,0:T(8,128)(2,1)} %cut.1), channel_id=1, source_target_pairs={{3,0},{0,1},{1,2},{2,3},{7,4},{4,5},{5,6},{6,7},{11,8},{8,9},{9,10... | collective-permute-start | bytes 1572872 | tf_op jit(solution)/shard_map/ppermute | solution.py:387
  5.5 13.1 %collective-permute-start.5 = (bf16[256,1024]{1,0:T(8,128)(2,1)}, bf16[256,1024]{1,0:T(8,128)(2,1)S(1)}, u32[]{:S(2)}, u32[]{:S(2)}) collective-permute-start(bf16[256,1024]{1,0:T(8,128)(2,1)} %cut.1), channel_id=1, source_target_pairs={{1,0},{2,1},{3,2},{0,3},{5,4},{6,5},{7,6},{4,7},{9,8},{10,9},{11,1... | collective-permute-start | bytes 1572872 | tf_op jit(solution)/shard_map/ppermute | solution.py:387
  8.5 10.1 %collective-permute-start = (bf16[16,768]{1,0:T(8,128)(2,1)S(1)}, bf16[16,768]{1,0:T(8,128)(2,1)S(1)}, u32[]{:S(2)}, u32[]{:S(2)}) collective-permute-start(bf16[16,768]{1,0:T(8,128)(2,1)S(1)} %get-tuple-element.42), channel_id=1, source_target_pairs={{0,4},{4,0},{8,12},{12,8},{1,5},{5,1},{9,13},{13,9},{2,6},{6,2},{1... | collective-permute-start | bytes 73736 | tf_op jit(solution)/shard_map/ppermute | solution.py:410
  11.4 7.2 %collective-permute-start.1 = (bf16[16,768]{1,0:T(8,128)(2,1)S(1)}, bf16[16,768]{1,0:T(8,128)(2,1)S(1)}, u32[]{:S(2)}, u32[]{:S(2)}) collective-permute-start(bf16[16,768]{1,0:T(8,128)(2,1)S(1)} %get-tuple-element.43), channel_id=1, source_target_pairs={{4,8},{8,4},{0,12},{12,0},{5,9},{9,5},{1,13},{13,1},{6,10},{10,6},... | collective-permute-start | bytes 73736 | tf_op jit(solution)/shard_map/ppermute | solution.py:418
  18.7 14.0 %collective-permute-start.9 = (bf16[128,1024]{1,0:T(8,128)(2,1)S(1)}, bf16[128,1024]{1,0:T(8,128)(2,1)S(1)}, u32[]{:S(2)}, u32[]{:S(2)}) collective-permute-start(bf16[128,1024]{1,0:T(8,128)(2,1)S(1)} %get-tuple-element.52), channel_id=1, source_target_pairs={{1,0},{2,1},{3,2},{0,3},{5,4},{6,5},{7,6},{4,7},{9,8},{10,9},{11,1... | collective-permute-start | bytes 786440 | tf_op jit(solution)/shard_map/ppermute | solution.py:387
  20.1 16.4 %collective-permute-start.10 = (bf16[128,1024]{1,0:T(8,128)(2,1)S(1)}, bf16[128,1024]{1,0:T(8,128)(2,1)S(1)}, u32[]{:S(2)}, u32[]{:S(2)}) collective-permute-start(bf16[128,1024]{1,0:T(8,128)(2,1)S(1)} %get-tuple-element.53), channel_id=1, source_target_pairs={{3,0},{0,1},{1,2},{2,3},{7,4},{4,5},{5,6},{6,7},{11,8},{8,9},{9,10... | collective-permute-start | bytes 786440 | tf_op jit(solution)/shard_map/ppermute | solution.py:387
  20.3 16.7 %collective-permute-start.7 = (bf16[416,256]{1,0:T(8,128)(2,1)S(1)}, bf16[416,256]{1,0:T(8,128)(2,1)S(1)}, u32[]{:S(2)}, u32[]{:S(2)}) collective-permute-start(bf16[416,256]{1,0:T(8,128)(2,1)S(1)} %get-tuple-element.50), channel_id=1, source_target_pairs={{0,16},{16,32},{32,48},{48,64},{64,80},{80,96},{96,112},{112,128},... | collective-permute-start | bytes 638984 | tf_op jit(solution)/shard_map/ppermute | solution.py:414
  22.9 14.1 %collective-permute-start.8 = (bf16[416,256]{1,0:T(8,128)(2,1)S(1)}, bf16[416,256]{1,0:T(8,128)(2,1)S(1)}, u32[]{:S(2)}, u32[]{:S(2)}) collective-permute-start(bf16[416,256]{1,0:T(8,128)(2,1)S(1)} %get-tuple-element.51), channel_id=1, source_target_pairs={{0,240},{16,0},{32,16},{48,32},{64,48},{80,64},{96,80},{112,96},{1... | collective-permute-start | bytes 638984 | tf_op jit(solution)/shard_map/ppermute | solution.py:414
  32.6 11.9 %collective-permute-start.2 = (bf16[256,256]{1,0:T(8,128)(2,1)S(1)}, bf16[256,256]{1,0:T(8,128)(2,1)S(1)}, u32[]{:S(2)}, u32[]{:S(2)}) collective-permute-start(bf16[256,256]{1,0:T(8,128)(2,1)S(1)} %get-tuple-element.47), channel_id=1, source_target_pairs={{0,1},{1,2},{2,3},{3,0},{4,5},{5,6},{6,7},{7,4},{8,9},{9,10},{10,1... | collective-permute-start | bytes 393224 | tf_op jit(solution)/shard_map/ppermute | solution.py:391
  32.7 13.4 %collective-permute-start.3 = (bf16[256,256]{1,0:T(8,128)(2,1)S(1)}, bf16[256,256]{1,0:T(8,128)(2,1)S(1)}, u32[]{:S(2)}, u32[]{:S(2)}) collective-permute-start(bf16[256,256]{1,0:T(8,128)(2,1)S(1)} %get-tuple-element.48), channel_id=1, source_target_pairs={{0,2},{1,3},{2,0},{3,1},{4,6},{5,7},{6,4},{7,5},{8,10},{9,11},{10,... | collective-permute-start | bytes 393224 | tf_op jit(solution)/shard_map/ppermute | solution.py:391
  36.6 24.7 %copy-start.1 = (bf16[1024,1024]{1,0:T(8,128)(2,1)S(1)}, bf16[1024,1024]{1,0:T(8,128)(2,1)}, u32[]{:S(2)}) copy-start(bf16[1024,1024]{1,0:T(8,128)(2,1)} %w_in.3) | copy-start | bytes 6291460
  36.6 24.7 %copy-start.2 = (bf16[1024,1024]{1,0:T(8,128)(2,1)S(1)}, bf16[1024,1024]{1,0:T(8,128)(2,1)}, u32[]{:S(2)}) copy-start(bf16[1024,1024]{1,0:T(8,128)(2,1)} %w_out.3) | copy-start | bytes 6291460
  36.6 11.5 %collective-permute-start.4 = (bf16[256,256]{1,0:T(8,128)(2,1)S(1)}, bf16[256,256]{1,0:T(8,128)(2,1)S(1)}, u32[]{:S(2)}, u32[]{:S(2)}) collective-permute-start(bf16[256,256]{1,0:T(8,128)(2,1)S(1)} %get-tuple-element.49), channel_id=1, source_target_pairs={{0,3},{1,0},{2,1},{3,2},{4,7},{5,4},{6,5},{7,6},{8,11},{9,8},{10,9... | collective-permute-start | bytes 393224 | tf_op jit(solution)/shard_map/ppermute | solution.py:391
  36.9 30.7 %collective-permute-start.18 = (bf16[768,1024]{1,0:T(8,128)(2,1)S(1)}, bf16[768,1024]{1,0:T(8,128)(2,1)S(1)}, u32[]{:S(2)}, u32[]{:S(2)}) collective-permute-start(bf16[768,1024]{1,0:T(8,128)(2,1)S(1)} %get-tuple-element.54.held), channel_id=1, source_target_pairs={{192,0},{60,4},{208,16},{4,20},{224,32},{20,36},{240,48},{36,52},{... | collective-permute-start | bytes 4718600 | tf_op jit(solution)/shard_map/ppermute | solution.py:406
  37.0 30.6 %collective-permute-start.17 = (bf16[768,1024]{1,0:T(8,128)(2,1)S(1)}, bf16[768,1024]{1,0:T(8,128)(2,1)S(1)}, u32[]{:S(2)}, u32[]{:S(2)}) collective-permute-start(bf16[768,1024]{1,0:T(8,128)(2,1)S(1)} %get-tuple-element.54.held), channel_id=1, source_target_pairs={{64,0},{20,4},{80,16},{36,20},{96,32},{52,36},{112,48},{12,52},{72... | collective-permute-start | bytes 4718600 | tf_op jit(solution)/shard_map/ppermute | solution.py:406
  44.6 5.6 %collective-permute-start.11 = (bf16[288,256]{1,0:T(8,128)(2,1)S(1)}, bf16[288,256]{1,0:T(8,128)(2,1)S(1)}, u32[]{:S(2)}, u32[]{:S(2)}) collective-permute-start(bf16[288,256]{1,0:T(8,128)(2,1)S(1)} %get-tuple-element.59), channel_id=1, source_target_pairs={{0,1},{1,2},{2,3},{3,0},{4,5},{5,6},{6,7},{7,4},{8,9},{9,10},{10,1... | collective-permute-start | bytes 442376 | tf_op jit(solution)/shard_map/ppermute | solution.py:391
  46.1 7.0 %collective-permute-start.12 = (bf16[288,256]{1,0:T(8,128)(2,1)S(1)}, bf16[288,256]{1,0:T(8,128)(2,1)S(1)}, u32[]{:S(2)}, u32[]{:S(2)}) collective-permute-start(bf16[288,256]{1,0:T(8,128)(2,1)S(1)} %get-tuple-element.60), channel_id=1, source_target_pairs={{0,2},{1,3},{2,0},{3,1},{4,6},{5,7},{6,4},{7,5},{8,10},{9,11},{10,... | collective-permute-start | bytes 442376 | tf_op jit(solution)/shard_map/ppermute | solution.py:391
  48.1 5.0 %collective-permute-start.13 = (bf16[288,256]{1,0:T(8,128)(2,1)S(1)}, bf16[288,256]{1,0:T(8,128)(2,1)S(1)}, u32[]{:S(2)}, u32[]{:S(2)}) collective-permute-start(bf16[288,256]{1,0:T(8,128)(2,1)S(1)} %get-tuple-element.61), channel_id=1, source_target_pairs={{0,3},{1,0},{2,1},{3,2},{4,7},{5,4},{6,5},{7,6},{8,11},{9,8},{10,9... | collective-permute-start | bytes 442376 | tf_op jit(solution)/shard_map/ppermute | solution.py:391
  54.9 6.4 %collective-permute-start.16 = (bf16[512,1024]{1,0:T(8,128)(2,1)S(1)}, bf16[512,1024]{1,0:T(8,128)(2,1)S(1)}, u32[]{:S(2)}, u32[]{:S(2)}) collective-permute-start(bf16[512,1024]{1,0:T(8,128)(2,1)S(1)} %get-tuple-element.62.n_ref), channel_id=1, source_target_pairs={{0,4},{4,0},{8,12},{12,8},{1,5},{5,1},{9,13},{13,9},{2,6},{6,2},{1... | collective-permute-start | bytes 3145736 | tf_op jit(solution)/shard_map/ppermute | solution.py:410
  59.0 14.7 %collective-permute-start.14 = (bf16[384,1024]{1,0:T(8,128)(2,1)S(1)}, bf16[384,1024]{1,0:T(8,128)(2,1)S(1)}, u32[]{:S(2)}, u32[]{:S(2)}) collective-permute-start(bf16[384,1024]{1,0:T(8,128)(2,1)S(1)} %get-tuple-element.64), channel_id=1, source_target_pairs={{16,0},{68,4},{32,16},{84,20},{48,32},{100,36},{8,48},{116,52},{24... | collective-permute-start | bytes 2359304 | tf_op jit(solution)/shard_map/ppermute | solution.py:406
  59.0 14.7 %collective-permute-start.15 = (bf16[384,1024]{1,0:T(8,128)(2,1)S(1)}, bf16[384,1024]{1,0:T(8,128)(2,1)S(1)}, u32[]{:S(2)}, u32[]{:S(2)}) collective-permute-start(bf16[384,1024]{1,0:T(8,128)(2,1)S(1)} %get-tuple-element.65), channel_id=1, source_target_pairs={{56,0},{196,4},{0,16},{212,20},{16,32},{228,36},{32,48},{244,52},{... | collective-permute-start | bytes 2359304 | tf_op jit(solution)/shard_map/ppermute | solution.py:406
  76.0 2.9 %collective-permute-start.19 = (bf16[4,512,256]{2,1,0:T(8,128)(2,1)S(1)}, bf16[4,512,256]{2,1,0:T(8,128)(2,1)S(1)}, u32[]{:S(2)}, u32[]{:S(2)}) collective-permute-start(bf16[4,512,256]{2,1,0:T(8,128)(2,1)S(1)} %mlp_last_other.1), channel_id=1, source_target_pairs={{0,4},{4,0},{8,12},{12,8},{1,5},{5,1},{9,13},{13,9},{2,6},{6,2},{1... | collective-permute-start | bytes 3145736 | tf_op jit(solution)/shard_map/ppermute | solution.py:410
  78.8 16.1 %copy-start.4 = (f32[256]{0:T(256)S(1)}, f32[256]{0:T(256)}, u32[]{:S(2)}) copy-start(f32[256]{0:T(256)} %param.19) | copy-start | bytes 3076
  78.8 16.1 %copy-start.5 = (f32[256]{0:T(256)S(1)}, f32[256]{0:T(256)}, u32[]{:S(2)}) copy-start(f32[256]{0:T(256)} %param.18) | copy-start | bytes 3076
  79.6 8.8 %collective-permute-start.20 = (bf16[512,256]{1,0:T(8,128)(2,1)S(1)}, bf16[512,256]{1,0:T(8,128)(2,1)S(1)}, u32[]{:S(2)}, u32[]{:S(2)}) collective-permute-start(bf16[512,256]{1,0:T(8,128)(2,1)S(1)} %get-tuple-element.74), channel_id=1, source_target_pairs={{0,1},{1,2},{2,3},{3,0},{4,5},{5,6},{6,7},{7,4},{8,9},{9,10},{10,1... | collective-permute-start | bytes 786440 | tf_op jit(solution)/shard_map/ppermute | solution.py:391
  80.9 14.0 %collective-permute-start.21 = (bf16[512,256]{1,0:T(8,128)(2,1)S(1)}, bf16[512,256]{1,0:T(8,128)(2,1)S(1)}, u32[]{:S(2)}, u32[]{:S(2)}) collective-permute-start(bf16[512,256]{1,0:T(8,128)(2,1)S(1)} %get-tuple-element.75), channel_id=1, source_target_pairs={{0,2},{1,3},{2,0},{3,1},{4,6},{5,7},{6,4},{7,5},{8,10},{9,11},{10,... | collective-permute-start | bytes 786440 | tf_op jit(solution)/shard_map/ppermute | solution.py:391
  83.2 11.7 %collective-permute-start.22 = (bf16[512,256]{1,0:T(8,128)(2,1)S(1)}, bf16[512,256]{1,0:T(8,128)(2,1)S(1)}, u32[]{:S(2)}, u32[]{:S(2)}) collective-permute-start(bf16[512,256]{1,0:T(8,128)(2,1)S(1)} %get-tuple-element.76), channel_id=1, source_target_pairs={{0,3},{1,0},{2,1},{3,2},{4,7},{5,4},{6,5},{7,6},{8,11},{9,8},{10,9... | collective-permute-start | bytes 786440 | tf_op jit(solution)/shard_map/ppermute | solution.py:391

commit v3 on v2

--- a/solution.py
+++ b/solution.py
@@ -20,10 +20,10 @@
 
 
 def turn_kernel(sc, x_ref, xt_ref, a_ref, b_ref, xf):
-    xf[...] = x_ref[...].astype(F32).reshape(4096, 128)
+    xf.reshape(256, 24, 128)[:, 0:16, :] = x_ref[...].astype(F32)
     for r in range(16):
         for h in range(2):
-            t = xf[pl.ds(h * 2048 + r, 128, stride=16), :]
+            t = xf[pl.ds(h * 3072 + r, 128, stride=24), :]
             xt_ref[r, :, h * 128 : (h + 1) * 128] = t.T.astype(BF)
     for j in range(3):
         js = slice(j * 256, (j + 1) * 256)
@@ -39,7 +39,7 @@
         out_shape=(jax.ShapeDtypeStruct((16, 128, 256), BF), edge, edge),
         in_specs=[SM, VM],
         out_specs=(VM, VM, VM),
-        scratch_shapes=[pltpu.VMEM((4096, 128), F32)],
+        scratch_shapes=[pltpu.VMEM((6144, 128), F32)],
         compiler_params=params(16),
         cost_estimate=pl.CostEstimate(flops=0, bytes_accessed=4 << 20, transcendentals=0),
         name="turn",
@@ -74,52 +74,28 @@
     )(xt, a, b, r1, r3)
 
 
-def cut_kernel(sc, w_in, w_out, piece, sems):
-    start = pl.multiple_of(sc[8], 128)
-    copies = [
-        pltpu.make_async_copy(w.at[pl.ds(start, 128)], piece.at[128 * i : 128 * i + 128], sems.at[i])
-        for i, w in enumerate((w_in, w_out))
-    ]
-    for copy in copies:
-        copy.start()
-    for copy in copies:
-        copy.wait()
-
-
-def cut(sc, w_in, w_out):
-    return pl.pallas_call(
-        cut_kernel,
-        out_shape=jax.ShapeDtypeStruct((256, 1024), BF),
-        in_specs=[SM, HB, HB],
-        out_specs=VM,
-        scratch_shapes=[pltpu.SemaphoreType.DMA((2,))],
-        compiler_params=params(60),
-        cost_estimate=pl.CostEstimate(flops=0, bytes_accessed=1 << 20, transcendentals=0),
-        name="cut",
-    )(sc, w_in, w_out)
-
-
 def taps(sc, xs, kw_ref, edge, sums, outs):
-    @pl.loop(0, 8)
+    @pl.loop(0, 4)
     def _(step):
-        h, k = lax.rem(step, 2), step // 2
-        q = lax.rem(sc[0] + k, 4)
-        row0 = 2 * q + 6 * (q // 2) if edge else 2 * q
+        h, g = lax.rem(step, 2), step // 2
+        row0 = (10 if edge else 4) * g
         for c0 in range(0, 128, CB):
-            acc = [jnp.zeros((CB, 128), F32) for _ in range(2)]
+            acc = [jnp.zeros((CB, 128), F32) for _ in range(4)]
             for b in range(7):
-                for ri in range(8):
+                for ri in range(10):
                     xv = xs[h, row0 + ri, c0 + 5 + b : c0 + 5 + b + CB, :]
-                    for ro in range(2):
+                    for ro in range(4):
                         a = ri - ro
                         if 0 <= a < 7:
                             acc[ro] = acc[ro] + kw_ref[h, a * 7 + b : a * 7 + b + 1, :] * xv
-            for ro in range(2):
-                sums[k, h, ro * 128 + c0 : ro * 128 + c0 + CB, :] = acc[ro].astype(BF)
+            for ro in range(4):
+                at = ro % 2 * 128 + c0
+                sums[2 * g + ro // 2, h, at : at + CB, :] = acc[ro].astype(BF)
 
     for k, o in enumerate(outs):
+        q = lax.rem(sc[0] + k, 4)
         for h in range(2):
-            o[0:256, h * 128 : (h + 1) * 128] = sums[k, h]
+            o[0:256, h * 128 : (h + 1) * 128] = sums[q, h]
 
 
 def columns(sc, a, b):
@@ -246,28 +222,10 @@
     )(sc, *inner, *edge)
 
 
-def blocks(pixels, acc, at, items, out):
-    items = [(win, wout, jnp.concatenate(bias, axis=1)) for win, wout, bias in items]
-
-    @pl.loop(0, 2 * len(pixels))
-    def _(step):
-        rows = pl.ds(pl.multiple_of(lax.rem(step, 2) * 256, 256), 256)
-        n = pixels[0][rows, :]
-        if len(pixels) > 1:
-            n = jnp.where(step < 2, n, pixels[1][rows, :])
-        total = None
-        for win, wout, bias in items:
-            pre = lax.dot_general(n, win[...], NT, preferred_element_type=F32)
-            h = gelu(pre + bias).astype(BF)
-            part = jnp.dot(h, wout[...], preferred_element_type=F32)
-            total = part if total is None else total + part
-        here = pl.ds(pl.multiple_of(step * 256, 256), 256)
-        there = pl.ds(pl.multiple_of(at + step * 256, 256), 256)
-        for q in range(4):
-            part = total[:, q * 256 : (q + 1) * 256]
-            if acc is not None:
-                part = part + acc[q, there, :]
-            out[q, here, :] = part.astype(out.dtype)
+def hidden_block(n, win, wout, bias):
+    pre = lax.dot_general(n, win, NT, preferred_element_type=F32)
+    h = gelu(pre + bias).astype(BF)
+    return jnp.dot(h, wout, preferred_element_type=F32)
 
 
 def shards_bias(sc, bias, shift):
@@ -275,32 +233,72 @@
     return [bias[k, sc[1] * 4 + lax.rem(color + shift, 4)] for k in (1, 2, 3)]
 
 
-def first_kernel(sc, n_ref, n_other, bias, w_in, w_out, held, out):
+def first_kernel(sc, n_ref, n_other, bias, w_in, w_out, out):
     own = pl.ds(pl.multiple_of(sc[1] * 512, 512), 512)
-    values = [bias[0, sc[1] * 4 + c] for c in range(4)]
-    items = [(w_in.at[own], w_out.at[own], values)]
-    items += [(held.at[0:384], held.at[384:768], shards_bias(sc, bias, 0))]
-    blocks((n_ref, n_other), None, 0, items, out)
-
-
-def middle_kernel(sc, n_ref, n_other, bias, acc, plus, minus, out):
-    items = [
-        (w.at[0:384], w.at[384:768], shards_bias(sc, bias, shift))
-        for w, shift in ((plus, 1), (minus, 3))
+    values = jnp.concatenate([bias[0, sc[1] * 4 + c] for c in range(4)], axis=1)
+
+    @pl.loop(0, 2)
+    def _(half):
+        n = jnp.where(half == 0, n_ref[...], n_other[...])
+        total = hidden_block(n, w_in[own, :], w_out[own, :], values)
+        here = pl.ds(pl.multiple_of(half * 512, 512), 512)
+        for q in range(4):
+            out[q, here, :] = total[:, q * 256 : (q + 1) * 256]
+
+
+def middle_kernel(
+    sc, n_ref, n_other, bias, acc, held, plus, minus, out, win, wout, bv, sems
+):
+    pairs = []
+    for at, size, w in ((0, 384, held), (384, 384, plus), (768, 256, minus)):
+        pairs.append((w.at[0:size], win.at[at : at + size]))
+        pairs.append((w.at[384 : 384 + size], wout.at[at : at + size]))
+    copies = [pltpu.make_async_copy(a, b, sems.at[i]) for i, (a, b) in enumerate(pairs)]
+    for copy in copies:
+        copy.start()
+    values = []
+    for shift in (0, 1, 3):
+        values += shards_bias(sc, bias, shift)
+    for i in range(8):
+        bv[i // 4, :, i % 4 * 128 : i % 4 * 128 + 128] = values[i]
+    for copy in copies:
+        copy.wait()
+
+    @pl.loop(0, 4)
+    def _(step):
+        half, chunk = lax.rem(step, 2), step // 2
+        rows = pl.ds(pl.multiple_of(chunk * 512, 512), 512)
+        n = jnp.where(half == 0, n_ref[...], n_other[...])
+        total = hidden_block(n, win[rows, :], wout[rows, :], bv[chunk])
+        here = pl.ds(pl.multiple_of(half * 512, 512), 512)
+        for q in range(4):
+            before = jnp.where(step < 2, acc[q, here, :], out[q, here, :])
+            out[q, here, :] = before + total[:, q * 256 : (q + 1) * 256]
+
+
+def last_kernel(at, sc, n_ref, bias, acc, minus, low, high, out):
+    win = jnp.concatenate([minus[256:384, :], low[...]])
+    wout = jnp.concatenate([minus[640:768, :], high[...]])
+    values = jnp.concatenate(shards_bias(sc, bias, 3)[2:] + shards_bias(sc, bias, 2), axis=1)
+    total = hidden_block(n_ref[...], win, wout, values)
+    for q in range(4):
+        part = acc[q, at : at + 512, :] + total[:, q * 256 : (q + 1) * 256]
+        out[q] = part.astype(out.dtype)
+
+
+def mlp(kernel, sc, arrays, size, rows, out, name):
+    middle = [
+        pltpu.VMEM((1024, 1024), BF),
+        pltpu.VMEM((1024, 1024), BF),
+        pltpu.VMEM((2, 1, 512), F32),
+        pltpu.SemaphoreType.DMA((6,)),
     ]
-    blocks((n_ref, n_other), acc, 0, items, out)
-
-
-def last_kernel(at, sc, n_ref, bias, acc, low, high, out):
-    blocks((n_ref,), acc, at, [(low, high, shards_bias(sc, bias, 2))], out)
-
-
-def mlp(kernel, sc, arrays, size, rows, out, name):
     return pl.pallas_call(
         kernel,
         out_shape=jax.ShapeDtypeStruct((4, rows, 256), out),
         in_specs=[SM] + [VM] * len(arrays),
         out_specs=VM,
+        scratch_shapes=middle if size == 1024 else [],
         compiler_params=params(20),
         cost_estimate=pl.CostEstimate(
             flops=4_000 * size * rows, bytes_accessed=6 << 20, transcendentals=size * rows
@@ -327,7 +325,7 @@
     )(sc, acc, other)
 
 
-def join_kernel(r1, ra, rb, r3, held, low, high, sems):
+def join_kernel(r1, ra, rb, r3, _, held, low, high, sems):
     moves = [(r1.at[0:128], 0), (ra, 128), (r3.at[0:128], 256)]
     moves += [(r1.at[128:256], 384), (rb, 512), (r3.at[128:256], 640)]
     copies = []
@@ -346,7 +344,7 @@
     return pl.pallas_call(
         join_kernel,
         out_shape=(jax.ShapeDtypeStruct((768, 1024), BF), half, half),
-        in_specs=[HB] * 4,
+        in_specs=[HB] * 5,
         out_specs=(HB,) * 3,
         scratch_shapes=[pltpu.SemaphoreType.DMA((12,))],
         compiler_params=params(16),
@@ -355,32 +353,46 @@
     )(*pieces)
 
 
-def final_kernel(sc, x_ref, ls_ref, bo_ref, f0, f1, f2, f3, o_ref, t):
-    for k, f in enumerate((f0, f1, f2, f3)):
-        q = lax.rem(sc[0] + 4 - k, 4)
-        inner, edge = 4 + 2 * q, 2 * q + 8 * (q // 2)
-        for i in range(4):
-            row = inner + i if i < 2 else edge + i - 2
-            v = f[i * 128 : (i + 1) * 128, :].astype(F32)
-            v = ls_ref[...] * (v + bo_ref[...])
-            for h in range(2):
-                t[pl.ds(h * 2048 + row, 128, stride=16), :] = v[
-                    :, h * 128 : (h + 1) * 128
-                ].T
-    o_ref[...] = (x_ref[...].astype(F32) + t[...].reshape(256, 16, 128)).astype(BF)
-
-
-def final(sc, x, ls, bo, parts):
+def spread_kernel(f, ls_ref, bo_ref, o_ref):
+    for i in range(4):
+        v = ls_ref[...] * (f[i * 128 : (i + 1) * 128, :].astype(F32) + bo_ref[...])
+        for h in range(2):
+            o_ref[i, h * 128 : (h + 1) * 128, :] = v[:, h * 128 : (h + 1) * 128].T
+
+
+def spread(f, ls, bo):
+    return pl.pallas_call(
+        spread_kernel,
+        out_shape=jax.ShapeDtypeStruct((4, 256, 128), F32),
+        in_specs=[VM] * 3,
+        out_specs=VM,
+        compiler_params=params(16),
+        cost_estimate=pl.CostEstimate(flops=1 << 18, bytes_accessed=1 << 20, transcendentals=0),
+        name="spread",
+    )(f, ls, bo)
+
+
+def final_kernel(sc, x_ref, s0, s1, s2, s3, o_ref, t):
+    for k, s in enumerate((s0, s1, s2, s3)):
+        t[lax.rem(sc[0] + 4 - k, 4)] = s[...]
+    order = ((0, 2), (1, 2), (0, 0), (1, 0), (2, 0), (3, 0), (2, 2), (3, 2))
+    for c in range(0, 256, 8):
+        v = jnp.concatenate([t[q, i : i + 2, c : c + 8, :] for q, i in order])
+        v = jnp.swapaxes(v, 0, 1)
+        o_ref[c : c + 8] = (x_ref[c : c + 8].astype(F32) + v).astype(BF)
+
+
+def final(sc, x, parts):
     return pl.pallas_call(
         final_kernel,
         out_shape=jax.ShapeDtypeStruct((256, 16, 128), BF),
-        in_specs=[SM] + [VM] * 7,
+        in_specs=[SM] + [VM] * 5,
         out_specs=VM,
-        scratch_shapes=[pltpu.VMEM((4096, 128), F32)],
+        scratch_shapes=[pltpu.VMEM((4, 4, 256, 128), F32)],
         compiler_params=params(16),
         cost_estimate=pl.CostEstimate(flops=1 << 20, bytes_accessed=4 << 20, transcendentals=0),
         name="final",
-    )(sc, x, ls, bo, *parts)
+    )(sc, x, *parts)
 
 
 def from_hid(x, k):
@@ -433,7 +445,12 @@
     start = 512 * core + 128 * color
     sc = jnp.stack([y, core, c0, c1, row, 15 - row, col, 3 - col, start]).astype(jnp.int32)
 
-    piece = cut(sc, w_in, w_out)
+    piece = jnp.concatenate(
+        [
+            lax.dynamic_slice_in_dim(w_in, start, 128, 0),
+            lax.dynamic_slice_in_dim(w_out, start, 128, 0),
+        ]
+    )
     r1, r3 = from_hid(piece, 1), from_hid(piece, 3)
 
     xt, send_a, send_b = turn(sc, features)
@@ -451,8 +468,9 @@
     ra, rb = from_hid(ra, 1), from_hid(rb, 3)
 
     inner = conv_inner(sc, xt, a, b, kw)
+    first = inner[0]
     inner = [inner[0]] + [to_hid(inner[k], k) for k in (1, 2, 3)]
-    held, low, high = join(r1, ra, rb, r3)
+    held, low, high = join(r1, ra, rb, r3, first)
     plane = [
         from_plane(held, 1, True),
         from_plane(held, -1, True),
@@ -466,19 +484,24 @@
     n, bias = norm(sc, inner, edge)
     n_other = from_core(n)
     plus, minus, low, high = plane
-    acc = mlp(first_kernel, sc, [n, n_other, bias, w_in, w_out, held], 896, 1024, F32, "mlp_first")
+    acc = mlp(first_kernel, sc, [n, n_other, bias, w_in, w_out], 512, 1024, F32, "mlp_first")
     plus, minus, acc = after([plus, minus, acc])
-    acc = mlp(middle_kernel, sc, [n, n_other, bias, acc, plus, minus], 768, 1024, F32, "mlp_mid")
+    arrays = [n, n_other, bias, acc, held, plus, minus]
+    acc = mlp(middle_kernel, sc, arrays, 1024, 1024, F32, "mlp_mid")
     low, high, acc = after([low, high, acc])
     last = functools.partial(last_kernel, 512)
-    other = mlp(last, sc, [n_other, bias, acc, low, high], 384, 512, BF, "mlp_last_other")
+    arrays = [bias, acc, minus, low, high]
+    other = mlp(last, sc, [n_other] + arrays, 512, 512, BF, "mlp_last_other")
     back = from_core(other)
     (acc,) = after([acc], other)
     last = functools.partial(last_kernel, 0)
-    acc = mlp(last, sc, [n, bias, acc, low, high], 384, 512, F32, "mlp_last")
+    arrays = [bias, acc, minus, low, high]
+    acc = mlp(last, sc, [n] + arrays, 512, 512, F32, "mlp_last")
     parts = add(sc, acc, back)
-    parts = [parts[0]] + [to_hid(parts[k], k) for k in (1, 2, 3)]
-    return final(sc, features, layer_scale[None, :], b_out[None, :], parts)
+    two, one, three = (to_hid(parts[k], k) for k in (2, 1, 3))
+    ls, bo = layer_scale[None, :], b_out[None, :]
+    parts = [spread(f, ls, bo) for f in (parts[0], one, two, three)]
+    return final(sc, features, parts)
 
 
 def solution(mesh):

time: 98 us -> 96.1 us (0.981)
  Pallas kernels: 36.6 us -> 30.2 us
  starting transfers between devices: 41.7 us -> 45.1 us
    ppermute x3, starting transfers between devices: 7.56 us -> 11.6 us  [from_core(): return lax.ppermute(v, 'col', [(0, 1), (1, 0), (2, 3), (3, 2)])]
    pallas_call x4, Pallas kernels: 16.9 us -> 13.8 us  [mlp(): pl.pallas_call(kernel, out_shape=jax.ShapeDtypeStruct((4, rows, 256), out...]
    pallas_call x1 -> x4, Pallas kernels: 2.64 us -> 0.78 us  [spread(): pl.pallas_call(spread_kernel, out_shape=jax.ShapeDtypeStruct((4, 256, 128...]
    dynamic_slice x0 -> x1, local copies, waits for them, and re-layouts: none -> 1.14 us  [on_device(): lax.dynamic_slice_in_dim(w_out, start, 128, 0)]
  transfers between devices with their start and end apart: 23 -> 23, of which waited for: 6 -> 9; matrix products, arithmetic and copies ran while one was open for 0% -> 0% of each run, Pallas kernels for 28% -> 26%
where the time goes in v3:
time: 96.1 us; the launch traced here: 96 us
  starting transfers between devices  45.1 us (47%)
  Pallas kernels  30.2 us (31%)
  waiting for transfers between devices  17.9 us (19%)
  local copies, waits for them, and re-layouts  1.39 us (1%)
    ppermute x9, waiting for transfers between devices, to_hid(): return lax.ppermute(x, 'hid', [(i, (i + k) % 4) for i in range(4)])  15 us
    pallas_call x4, Pallas kernels, mlp(): pl.pallas_call(kernel, out_shape=jax.ShapeDtypeStruct((4, rows, 256), out...  13.8 us
    ppermute x3, starting transfers between devices, from_core(): return lax.ppermute(v, 'col', [(0, 1), (1, 0), (2, 3), (3, 2)])  11.6 us
    ppermute x9, starting transfers between devices, to_hid(): return lax.ppermute(x, 'hid', [(i, (i + k) % 4) for i in range(4)])  11.5 us
    ppermute x2, starting transfers between devices, around(): lax.ppermute(v, 'row', [(i, (i + (1 if up else -1)) % 16) for i in range(...  7.5 us
    ppermute x1, starting transfers between devices, from_chip(): return lax.ppermute(v, 'col', [(1, 2), (2, 1), (0, 3), (3, 0)])  5.17 us
    ppermute x4, starting transfers between devices, from_hid(): return lax.ppermute(x, 'hid', [((i + k) % 4, i) for i in range(4)])  5.13 us
    pallas_call x1, Pallas kernels, conv_edge(): pl.pallas_call(edge_kernel, out_shape=(o,) * 4, in_specs=[SM] + [VM] * 7,...  4.65 us
  transfers between devices with their start and end apart: 23, of which 9 were waited for; matrix products, arithmetic and copies ran while one was open for 0% of the time, Pallas kernels for 26%

profile of v3, /device:TPU:1, one launch (start us, length us, event | category | flops | bytes accessed | tf_op | source)
XLA Modules:
  0.0 96.0 jit_solution(1804934844556076211)
XLA Ops:
  0.1 1.1 %constant_dynamic-slice_fusion = (bf16[128,1024]{1,0:T(8,128)(2,1)S(1)}, bf16[128,1024]{1,0:T(8,128)(2,1)S(1)}) fusion(bf16[1024,1024]{1,0:T(8,128)(2,1)} %w_out.1, s32[]{:T(128)S(6)} %select_n.36, bf16[1024,1024]{1,0:T(8,128)(2,1)} %w_in.1), kind=kLoop, calls=%fused_computation.9 | loop fusion | bytes 1048580 | tf_op jit(solution)/shard_map/dynamic_slice | solution.py:451
  1.3 0.8 pad_maximum_fusion
  2.1 2.1 %collective-permute-start.6 = (bf16[256,1024]{1,0:T(8,128)(2,1)}, bf16[256,1024]{1,0:T(8,128)(2,1)S(1)}, u32[]{:S(2)}, u32[]{:S(2)}) collective-permute-start(bf16[256,1024]{1,0:T(8,128)(2,1)} %pad_maximum_fusion), channel_id=1, source_target_pairs={{3,0},{0,1},{1,2},{2,3},{7,4},{4,5},{5,6},{6,7},{11,8},{8,9},{9,10... | collective-permute-start | bytes 1572872 | tf_op jit(solution)/shard_map/ppermute | solution.py:399
  4.2 1.4 %collective-permute-start.5 = (bf16[256,1024]{1,0:T(8,128)(2,1)}, bf16[256,1024]{1,0:T(8,128)(2,1)S(1)}, u32[]{:S(2)}, u32[]{:S(2)}) collective-permute-start(bf16[256,1024]{1,0:T(8,128)(2,1)} %pad_maximum_fusion), channel_id=1, source_target_pairs={{1,0},{2,1},{3,2},{0,3},{5,4},{6,5},{7,6},{4,7},{9,8},{10,9},{11,1... | collective-permute-start | bytes 1572872 | tf_op jit(solution)/shard_map/ppermute | solution.py:399
  5.7 0.1 stack.39.sc
  5.7 1.2 %turn.1 = (bf16[16,128,256]{2,1,0:T(8,128)(2,1)S(1)}, bf16[16,768]{1,0:T(8,128)(2,1)S(1)}, bf16[16,768]{1,0:T(8,128)(2,1)S(1)}) custom-call(s32[9]{0:T(128)S(1)} %stack.39.sc, bf16[256,16,128]{2,1,0:T(8,128)(2,1)S(1)} %copy-done), custom_call_target="tpu_custom_call" | custom-call | bytes 4194304 | tf_op jit(solution)/shard_map/turn/pallas_call | solution.py:37
  7.0 3.0 %collective-permute-start = (bf16[16,768]{1,0:T(8,128)(2,1)S(1)}, bf16[16,768]{1,0:T(8,128)(2,1)S(1)}, u32[]{:S(2)}, u32[]{:S(2)}) collective-permute-start(bf16[16,768]{1,0:T(8,128)(2,1)S(1)} %get-tuple-element.42), channel_id=1, source_target_pairs={{0,4},{4,0},{8,12},{12,8},{1,5},{5,1},{9,13},{13,9},{2,6},{6,2},{1... | collective-permute-start | bytes 73736 | tf_op jit(solution)/shard_map/ppermute | solution.py:422
  10.0 5.2 %collective-permute-start.1 = (bf16[16,768]{1,0:T(8,128)(2,1)S(1)}, bf16[16,768]{1,0:T(8,128)(2,1)S(1)}, u32[]{:S(2)}, u32[]{:S(2)}) collective-permute-start(bf16[16,768]{1,0:T(8,128)(2,1)S(1)} %get-tuple-element.43), channel_id=1, source_target_pairs={{4,8},{8,4},{0,12},{12,0},{5,9},{9,5},{1,13},{13,1},{6,10},{10,6},... | collective-permute-start | bytes 73736 | tf_op jit(solution)/shard_map/ppermute | solution.py:430
  15.2 0.1 pad.10.clone
  15.3 0.1 maximum_maximum_fusion.p_ref
  15.4 1.7 %collective-permute-done.1.b_ref = bf16[16,768]{1,0:T(8,128)(2,1)S(1)} collective-permute-done((bf16[16,768]{1,0:T(8,128)(2,1)S(1)}, bf16[16,768]{1,0:T(8,128)(2,1)S(1)}, u32[]{:S(2)}, u32[]{:S(2)}) %collective-permute-start.1) | collective-permute-done | bytes 24608 | tf_op jit(solution)/shard_map/ppermute | solution.py:430
  17.2 0.1 pack.1
  17.2 1.6 %collective-permute-start.9 = (bf16[128,1024]{1,0:T(8,128)(2,1)S(1)}, bf16[128,1024]{1,0:T(8,128)(2,1)S(1)}, u32[]{:S(2)}, u32[]{:S(2)}) collective-permute-start(bf16[128,1024]{1,0:T(8,128)(2,1)S(1)} %get-tuple-element.52), channel_id=1, source_target_pairs={{1,0},{2,1},{3,2},{0,3},{5,4},{6,5},{7,6},{4,7},{9,8},{10,9},{11,1... | collective-permute-start | bytes 786440 | tf_op jit(solution)/shard_map/ppermute | solution.py:399
  18.8 2.6 %collective-permute-start.7 = (bf16[416,256]{1,0:T(8,128)(2,1)S(1)}, bf16[416,256]{1,0:T(8,128)(2,1)S(1)}, u32[]{:S(2)}, u32[]{:S(2)}) collective-permute-start(bf16[416,256]{1,0:T(8,128)(2,1)S(1)} %get-tuple-element.50), channel_id=1, source_target_pairs={{0,16},{16,32},{32,48},{48,64},{64,80},{80,96},{96,112},{112,128},... | collective-permute-start | bytes 638984 | tf_op jit(solution)/shard_map/ppermute | solution.py:426
  21.4 4.9 %collective-permute-start.8 = (bf16[416,256]{1,0:T(8,128)(2,1)S(1)}, bf16[416,256]{1,0:T(8,128)(2,1)S(1)}, u32[]{:S(2)}, u32[]{:S(2)}) collective-permute-start(bf16[416,256]{1,0:T(8,128)(2,1)S(1)} %get-tuple-element.51), channel_id=1, source_target_pairs={{0,240},{16,0},{32,16},{48,32},{64,48},{80,64},{96,80},{112,96},{1... | collective-permute-start | bytes 638984 | tf_op jit(solution)/shard_map/ppermute | solution.py:426
  26.3 4.6 %conv_inner.1 = (bf16[256,256]{1,0:T(8,128)(2,1)S(1)}, bf16[256,256]{1,0:T(8,128)(2,1)S(1)}, bf16[256,256]{1,0:T(8,128)(2,1)S(1)}, bf16[256,256]{1,0:T(8,128)(2,1)S(1)}) custom-call(s32[9]{0:T(128)S(1)} %stack.39.sc, bf16[16,128,256]{2,1,0:T(8,128)(2,1)S(1)} %get-tuple-element.41.xt_ref, bf16[16,768]{1,0:T(8,128)(2,1)S(1)} %collective-permute-done.a_ref, ...), custom_call_target="tpu_custom_call" | custom-call | flops 30000000 | bytes 4194304 | tf_op jit(solution)/shard_map/conv_inner/pallas_call | solution.py:153
  30.9 0.4 join.1
  31.3 0.1 collective-permute-start.18
  31.4 2.7 %collective-permute-start.17 = (bf16[768,1024]{1,0:T(8,128)(2,1)S(1)}, bf16[768,1024]{1,0:T(8,128)(2,1)S(1)}, u32[]{:S(2)}, u32[]{:S(2)}) collective-permute-start(bf16[768,1024]{1,0:T(8,128)(2,1)S(1)} %get-tuple-element.54.held), channel_id=1, source_target_pairs={{64,0},{20,4},{80,16},{36,20},{96,32},{52,36},{112,48},{12,52},{72... | collective-permute-start | bytes 4718600 | tf_op jit(solution)/shard_map/ppermute | solution.py:418
  34.1 3.8 %collective-permute-start.3 = (bf16[256,256]{1,0:T(8,128)(2,1)S(1)}, bf16[256,256]{1,0:T(8,128)(2,1)S(1)}, u32[]{:S(2)}, u32[]{:S(2)}) collective-permute-start(bf16[256,256]{1,0:T(8,128)(2,1)S(1)} %get-tuple-element.48), channel_id=1, source_target_pairs={{0,2},{1,3},{2,0},{3,1},{4,6},{5,7},{6,4},{7,5},{8,10},{9,11},{10,... | collective-permute-start | bytes 393224 | tf_op jit(solution)/shard_map/ppermute | solution.py:403
  37.9 4.7 %conv_edge.1 = (bf16[288,256]{1,0:T(8,128)(2,1)S(1)}, bf16[288,256]{1,0:T(8,128)(2,1)S(1)}, bf16[288,256]{1,0:T(8,128)(2,1)S(1)}, bf16[288,256]{1,0:T(8,128)(2,1)S(1)}) custom-call(s32[9]{0:T(128)S(1)} %stack.39.sc, bf16[16,128,256]{2,1,0:T(8,128)(2,1)S(1)} %get-tuple-element.41.xt_ref, bf16[16,768]{1,0:T(8,128)(2,1)S(1)} %collective-permute-done.a_ref, ...), custom_call_target="tpu_custom_call" | custom-call | flops 30000000 | bytes 4194304 | tf_op jit(solution)/shard_map/conv_edge/pallas_call | solution.py:167
  42.6 1.5 %collective-permute-start.11 = (bf16[288,256]{1,0:T(8,128)(2,1)S(1)}, bf16[288,256]{1,0:T(8,128)(2,1)S(1)}, u32[]{:S(2)}, u32[]{:S(2)}) collective-permute-start(bf16[288,256]{1,0:T(8,128)(2,1)S(1)} %get-tuple-element.59), channel_id=1, source_target_pairs={{0,1},{1,2},{2,3},{3,0},{4,5},{5,6},{6,7},{7,4},{8,9},{9,10},{10,1... | collective-permute-start | bytes 442376 | tf_op jit(solution)/shard_map/ppermute | solution.py:403
  44.1 0.7 collective-permute-start.12
  44.8 1.8 %collective-permute-start.13 = (bf16[288,256]{1,0:T(8,128)(2,1)S(1)}, bf16[288,256]{1,0:T(8,128)(2,1)S(1)}, u32[]{:S(2)}, u32[]{:S(2)}) collective-permute-start(bf16[288,256]{1,0:T(8,128)(2,1)S(1)} %get-tuple-element.61), channel_id=1, source_target_pairs={{0,3},{1,0},{2,1},{3,2},{4,7},{5,4},{6,5},{7,6},{8,11},{9,8},{10,9... | collective-permute-start | bytes 442376 | tf_op jit(solution)/shard_map/ppermute | solution.py:403
  46.6 1.5 %collective-permute-done.11.e1 = bf16[288,256]{1,0:T(8,128)(2,1)S(1)} collective-permute-done((bf16[288,256]{1,0:T(8,128)(2,1)S(1)}, bf16[288,256]{1,0:T(8,128)(2,1)S(1)}, u32[]{:S(2)}, u32[]{:S(2)}) %collective-permute-start.11) | collective-permute-done | bytes 147488 | tf_op jit(solution)/shard_map/ppermute | solution.py:403
  48.2 1.5 %collective-permute-done.12.e2 = bf16[288,256]{1,0:T(8,128)(2,1)S(1)} collective-permute-done((bf16[288,256]{1,0:T(8,128)(2,1)S(1)}, bf16[288,256]{1,0:T(8,128)(2,1)S(1)}, u32[]{:S(2)}, u32[]{:S(2)}) %collective-permute-start.12) | collective-permute-done | bytes 147488 | tf_op jit(solution)/shard_map/ppermute | solution.py:403
  49.6 0.7 collective-permute-done.13.e3
  50.3 1.8 %norm.1 = (bf16[512,1024]{1,0:T(8,128)(2,1)S(1)}, f32[4,8,1,128]{3,2,1,0:T(1,128)S(1)}) custom-call(s32[9]{0:T(128)S(1)} %stack.39.sc, bf16[256,256]{1,0:T(8,128)(2,1)S(1)} %get-tuple-element.46._.i0, bf16[256,256]{1,0:T(8,128)(2,1)S(1)} %collective-permute-done.2.i1, bf16[256,256]{1,0:T(8,128)(2,1)S(1)} %collective-permute-done.3.i2, ...), custom_call_target="tpu_custom_call" | custom-call | flops 8388608 | bytes 2097152 | tf_op jit(solution)/shard_map/norm/pallas_call | solution.py:211
  52.1 5.0 %collective-permute-start.16 = (bf16[512,1024]{1,0:T(8,128)(2,1)S(1)}, bf16[512,1024]{1,0:T(8,128)(2,1)S(1)}, u32[]{:S(2)}, u32[]{:S(2)}) collective-permute-start(bf16[512,1024]{1,0:T(8,128)(2,1)S(1)} %get-tuple-element.62.n_ref), channel_id=1, source_target_pairs={{0,4},{4,0},{8,12},{12,8},{1,5},{5,1},{9,13},{13,9},{2,6},{6,2},{1... | collective-permute-start | bytes 3145736 | tf_op jit(solution)/shard_map/ppermute | solution.py:422
  57.1 1.5 %collective-permute-start.15 = (bf16[384,1024]{1,0:T(8,128)(2,1)S(1)}, bf16[384,1024]{1,0:T(8,128)(2,1)S(1)}, u32[]{:S(2)}, u32[]{:S(2)}) collective-permute-start(bf16[384,1024]{1,0:T(8,128)(2,1)S(1)} %get-tuple-element.65), channel_id=1, source_target_pairs={{56,0},{196,4},{0,16},{212,20},{16,32},{228,36},{32,48},{244,52},{... | collective-permute-start | bytes 2359304 | tf_op jit(solution)/shard_map/ppermute | solution.py:418
  58.6 0.8 collective-permute-done.16.n_other.n_ref
  59.4 3.3 %mlp_first.1.acc = f32[4,1024,256]{2,1,0:T(8,128)S(1)} custom-call(s32[9]{0:T(128)S(1)} %stack.39.sc, bf16[512,1024]{1,0:T(8,128)(2,1)S(1)} %get-tuple-element.62.n_ref, bf16[512,1024]{1,0:T(8,128)(2,1)S(1)} %collective-permute-done.16.n_other.n_ref, f32[4,8,1,128]{3,2,1,0:T(1,128)S(1)} %get-tuple-element.63.bias, bf16[1024,1024]{1,0:T(8,128)(2,1)S(1)} %copy-done.2, ...), custom_call_target="tpu_custom_call" | custom-call | flops 2097152000 | bytes 6291456 | tf_op jit(solution)/shard_map/mlp_first/pallas_call | solution.py:296
  62.8 6.6 %mlp_mid.1.acc = f32[4,1024,256]{2,1,0:T(8,128)S(1)} custom-call(s32[9]{0:T(128)S(1)} %stack.39.sc, bf16[512,1024]{1,0:T(8,128)(2,1)S(1)} %get-tuple-element.62.n_ref, bf16[512,1024]{1,0:T(8,128)(2,1)S(1)} %collective-permute-done.16.n_other.n_ref, f32[4,8,1,128]{3,2,1,0:T(1,128)S(1)} %get-tuple-element.63.bias, f32[4,1024,256]{2,1,0:T(8,128)S(1)} %mlp_first.1.acc, ...), custom_call_target="tpu_custom_call" | custom-call | flops 4194304000 | bytes 6291456 | tf_op jit(solution)/shard_map/mlp_mid/pallas_call | solution.py:296
  69.4 0.1 collective-permute-done.15.high
  69.5 1.9 %mlp_last_other.1 = bf16[4,512,256]{2,1,0:T(8,128)(2,1)S(1)} custom-call(s32[9]{0:T(128)S(1)} %stack.39.sc, bf16[512,1024]{1,0:T(8,128)(2,1)S(1)} %collective-permute-done.16.n_other.n_ref, f32[4,8,1,128]{3,2,1,0:T(1,128)S(1)} %get-tuple-element.63.bias, f32[4,1024,256]{2,1,0:T(8,128)S(1)} %mlp_mid.1.acc, ...), custom_call_target="tpu_custom_call" | custom-call | flops 1048576000 | bytes 6291456 | tf_op jit(solution)/shard_map/mlp_last_other/pallas_call | solution.py:296
  71.4 3.6 %collective-permute-start.19 = (bf16[4,512,256]{2,1,0:T(8,128)(2,1)S(1)}, bf16[4,512,256]{2,1,0:T(8,128)(2,1)S(1)}, u32[]{:S(2)}, u32[]{:S(2)}) collective-permute-start(bf16[4,512,256]{2,1,0:T(8,128)(2,1)S(1)} %mlp_last_other.1), channel_id=1, source_target_pairs={{0,4},{4,0},{8,12},{12,8},{1,5},{5,1},{9,13},{13,9},{2,6},{6,2},{1... | collective-permute-start | bytes 3145736 | tf_op jit(solution)/shard_map/ppermute | solution.py:422
  75.1 1.9 %mlp_last.1.acc = f32[4,512,256]{2,1,0:T(8,128)S(1)} custom-call(s32[9]{0:T(128)S(1)} %stack.39.sc, bf16[512,1024]{1,0:T(8,128)(2,1)S(1)} %get-tuple-element.62.n_ref, f32[4,8,1,128]{3,2,1,0:T(1,128)S(1)} %get-tuple-element.63.bias, f32[4,1024,256]{2,1,0:T(8,128)S(1)} %mlp_mid.1.acc, bf16[768,1024]{1,0:T(8,128)(2,1)S(1)} %collective-permute-done.18.minus, ...), custom_call_target="tpu_custom_call" | custom-call | flops 1048576000 | bytes 6291456 | tf_op jit(solution)/shard_map/mlp_last/pallas_call | solution.py:296
  77.0 0.3 collective-permute-done.19.other
  77.3 0.7 add.38
  78.1 0.6 collective-permute-start.20
  78.7 3.0 %collective-permute-start.21 = (bf16[512,256]{1,0:T(8,128)(2,1)S(1)}, bf16[512,256]{1,0:T(8,128)(2,1)S(1)}, u32[]{:S(2)}, u32[]{:S(2)}) collective-permute-start(bf16[512,256]{1,0:T(8,128)(2,1)S(1)} %get-tuple-element.75), channel_id=1, source_target_pairs={{0,2},{1,3},{2,0},{3,1},{4,6},{5,7},{6,4},{7,5},{8,10},{9,11},{10,... | collective-permute-start | bytes 786440 | tf_op jit(solution)/shard_map/ppermute | solution.py:403
  81.7 0.2 spread.4.s0
  81.9 5.0 %collective-permute-done.20.f = bf16[512,256]{1,0:T(8,128)(2,1)S(1)} collective-permute-done((bf16[512,256]{1,0:T(8,128)(2,1)S(1)}, bf16[512,256]{1,0:T(8,128)(2,1)S(1)}, u32[]{:S(2)}, u32[]{:S(2)}) %collective-permute-start.20) | collective-permute-done | bytes 262176 | tf_op jit(solution)/shard_map/ppermute | solution.py:403
  86.9 0.2 spread.5.s1
  87.1 6.3 %collective-permute-done.21.f = bf16[512,256]{1,0:T(8,128)(2,1)S(1)} collective-permute-done((bf16[512,256]{1,0:T(8,128)(2,1)S(1)}, bf16[512,256]{1,0:T(8,128)(2,1)S(1)}, u32[]{:S(2)}, u32[]{:S(2)}) %collective-permute-start.21) | collective-permute-done | bytes 262176 | tf_op jit(solution)/shard_map/ppermute | solution.py:403
  93.4 0.2 spread.6.s2
  93.6 0.2 spread.7.s3
  93.8 2.2 %final.1 = bf16[256,16,128]{2,1,0:T(8,128)(2,1)} custom-call(s32[9]{0:T(128)S(1)} %stack.39.sc, bf16[256,16,128]{2,1,0:T(8,128)(2,1)S(1)} %copy-done, f32[4,256,128]{2,1,0:T(8,128)S(1)} %spread.4.s0, f32[4,256,128]{2,1,0:T(8,128)S(1)} %spread.5.s1, f32[4,256,128]{2,1,0:T(8,128)S(1)} %spread.6.s2, f32[4,256,128]{2,1,0:T(8,128)S(1)} %spread.7.s3), custom_call_target="tpu_custom_call" | custom-call | flops 1048576 | bytes 4194304 | tf_op jit(solution)/shard_map/final/pallas_call | solution.py:386
  (45 shorter events, 0.2 us)
Async XLA Ops:
  0.0 5.7 %copy-start = (bf16[256,16,128]{2,1,0:T(8,128)(2,1)S(1)}, bf16[256,16,128]{2,1,0:T(8,128)(2,1)}, u32[]{:S(2)}) copy-start(bf16[256,16,128]{2,1,0:T(8,128)(2,1)} %x_ref.3) | copy-start | bytes 3145732
  0.0 15.1 %copy-start.6 = (f32[1024]{0:T(1024)S(1)}, f32[1024]{0:T(1024)}, u32[]{:S(2)}) copy-start(f32[1024]{0:T(1024)} %param.16) | copy-start | bytes 12292
  0.0 15.1 %copy-start.7 = (f32[256]{0:T(256)S(1)}, f32[256]{0:T(256)}, u32[]{:S(2)}) copy-start(f32[256]{0:T(256)} %param.14) | copy-start | bytes 3076
  0.0 15.1 %copy-start.8 = (f32[256]{0:T(256)S(1)}, f32[256]{0:T(256)}, u32[]{:S(2)}) copy-start(f32[256]{0:T(256)} %param.13) | copy-start | bytes 3076
  0.0 15.1 %copy-start.9 = (f32[256]{0:T(256)S(1)}, f32[256]{0:T(256)}, u32[]{:S(2)}) copy-start(f32[256]{0:T(256)} %param.12) | copy-start | bytes 3076
  0.0 15.3 %copy-start.5 = (f32[256,7,7]{0,2,1:T(8,128)S(1)}, f32[256,7,7]{0,2,1:T(8,128)}, u32[]{:S(2)}) copy-start(f32[256,7,7]{0,2,1:T(8,128)} %param.11) | copy-start | bytes 150532
  2.1 15.1 %collective-permute-start.6 = (bf16[256,1024]{1,0:T(8,128)(2,1)}, bf16[256,1024]{1,0:T(8,128)(2,1)S(1)}, u32[]{:S(2)}, u32[]{:S(2)}) collective-permute-start(bf16[256,1024]{1,0:T(8,128)(2,1)} %pad_maximum_fusion), channel_id=1, source_target_pairs={{3,0},{0,1},{1,2},{2,3},{7,4},{4,5},{5,6},{6,7},{11,8},{8,9},{9,10... | collective-permute-start | bytes 1572872 | tf_op jit(solution)/shard_map/ppermute | solution.py:399
  4.2 13.0 %collective-permute-start.5 = (bf16[256,1024]{1,0:T(8,128)(2,1)}, bf16[256,1024]{1,0:T(8,128)(2,1)S(1)}, u32[]{:S(2)}, u32[]{:S(2)}) collective-permute-start(bf16[256,1024]{1,0:T(8,128)(2,1)} %pad_maximum_fusion), channel_id=1, source_target_pairs={{1,0},{2,1},{3,2},{0,3},{5,4},{6,5},{7,6},{4,7},{9,8},{10,9},{11,1... | collective-permute-start | bytes 1572872 | tf_op jit(solution)/shard_map/ppermute | solution.py:399
  7.0 10.2 %collective-permute-start = (bf16[16,768]{1,0:T(8,128)(2,1)S(1)}, bf16[16,768]{1,0:T(8,128)(2,1)S(1)}, u32[]{:S(2)}, u32[]{:S(2)}) collective-permute-start(bf16[16,768]{1,0:T(8,128)(2,1)S(1)} %get-tuple-element.42), channel_id=1, source_target_pairs={{0,4},{4,0},{8,12},{12,8},{1,5},{5,1},{9,13},{13,9},{2,6},{6,2},{1... | collective-permute-start | bytes 73736 | tf_op jit(solution)/shard_map/ppermute | solution.py:422
  10.0 7.2 %collective-permute-start.1 = (bf16[16,768]{1,0:T(8,128)(2,1)S(1)}, bf16[16,768]{1,0:T(8,128)(2,1)S(1)}, u32[]{:S(2)}, u32[]{:S(2)}) collective-permute-start(bf16[16,768]{1,0:T(8,128)(2,1)S(1)} %get-tuple-element.43), channel_id=1, source_target_pairs={{4,8},{8,4},{0,12},{12,0},{5,9},{9,5},{1,13},{13,1},{6,10},{10,6},... | collective-permute-start | bytes 73736 | tf_op jit(solution)/shard_map/ppermute | solution.py:430
  17.2 13.6 %collective-permute-start.9 = (bf16[128,1024]{1,0:T(8,128)(2,1)S(1)}, bf16[128,1024]{1,0:T(8,128)(2,1)S(1)}, u32[]{:S(2)}, u32[]{:S(2)}) collective-permute-start(bf16[128,1024]{1,0:T(8,128)(2,1)S(1)} %get-tuple-element.52), channel_id=1, source_target_pairs={{1,0},{2,1},{3,2},{0,3},{5,4},{6,5},{7,6},{4,7},{9,8},{10,9},{11,1... | collective-permute-start | bytes 786440 | tf_op jit(solution)/shard_map/ppermute | solution.py:399
  18.8 12.1 %collective-permute-start.10 = (bf16[128,1024]{1,0:T(8,128)(2,1)S(1)}, bf16[128,1024]{1,0:T(8,128)(2,1)S(1)}, u32[]{:S(2)}, u32[]{:S(2)}) collective-permute-start(bf16[128,1024]{1,0:T(8,128)(2,1)S(1)} %get-tuple-element.53), channel_id=1, source_target_pairs={{3,0},{0,1},{1,2},{2,3},{7,4},{4,5},{5,6},{6,7},{11,8},{8,9},{9,10... | collective-permute-start | bytes 786440 | tf_op jit(solution)/shard_map/ppermute | solution.py:399
  18.8 15.3 %collective-permute-start.7 = (bf16[416,256]{1,0:T(8,128)(2,1)S(1)}, bf16[416,256]{1,0:T(8,128)(2,1)S(1)}, u32[]{:S(2)}, u32[]{:S(2)}) collective-permute-start(bf16[416,256]{1,0:T(8,128)(2,1)S(1)} %get-tuple-element.50), channel_id=1, source_target_pairs={{0,16},{16,32},{32,48},{48,64},{64,80},{80,96},{96,112},{112,128},... | collective-permute-start | bytes 638984 | tf_op jit(solution)/shard_map/ppermute | solution.py:426
  21.4 16.5 %collective-permute-start.8 = (bf16[416,256]{1,0:T(8,128)(2,1)S(1)}, bf16[416,256]{1,0:T(8,128)(2,1)S(1)}, u32[]{:S(2)}, u32[]{:S(2)}) collective-permute-start(bf16[416,256]{1,0:T(8,128)(2,1)S(1)} %get-tuple-element.51), channel_id=1, source_target_pairs={{0,240},{16,0},{32,16},{48,32},{64,48},{80,64},{96,80},{112,96},{1... | collective-permute-start | bytes 638984 | tf_op jit(solution)/shard_map/ppermute | solution.py:426
  30.9 28.5 %copy-start.1 = (bf16[1024,1024]{1,0:T(8,128)(2,1)S(1)}, bf16[1024,1024]{1,0:T(8,128)(2,1)}, u32[]{:S(2)}) copy-start(bf16[1024,1024]{1,0:T(8,128)(2,1)} %w_out.1) | copy-start | bytes 6291460
  30.9 28.5 %copy-start.2 = (bf16[1024,1024]{1,0:T(8,128)(2,1)S(1)}, bf16[1024,1024]{1,0:T(8,128)(2,1)}, u32[]{:S(2)}) copy-start(bf16[1024,1024]{1,0:T(8,128)(2,1)} %w_in.1) | copy-start | bytes 6291460
  31.3 31.5 %collective-permute-start.18 = (bf16[768,1024]{1,0:T(8,128)(2,1)S(1)}, bf16[768,1024]{1,0:T(8,128)(2,1)S(1)}, u32[]{:S(2)}, u32[]{:S(2)}) collective-permute-start(bf16[768,1024]{1,0:T(8,128)(2,1)S(1)} %get-tuple-element.54.held), channel_id=1, source_target_pairs={{192,0},{60,4},{208,16},{4,20},{224,32},{20,36},{240,48},{36,52},{... | collective-permute-start | bytes 4718600 | tf_op jit(solution)/shard_map/ppermute | solution.py:418
  31.4 31.4 %collective-permute-start.17 = (bf16[768,1024]{1,0:T(8,128)(2,1)S(1)}, bf16[768,1024]{1,0:T(8,128)(2,1)S(1)}, u32[]{:S(2)}, u32[]{:S(2)}) collective-permute-start(bf16[768,1024]{1,0:T(8,128)(2,1)S(1)} %get-tuple-element.54.held), channel_id=1, source_target_pairs={{64,0},{20,4},{80,16},{36,20},{96,32},{52,36},{112,48},{12,52},{72... | collective-permute-start | bytes 4718600 | tf_op jit(solution)/shard_map/ppermute | solution.py:418
  34.0 8.5 %collective-permute-start.2 = (bf16[256,256]{1,0:T(8,128)(2,1)S(1)}, bf16[256,256]{1,0:T(8,128)(2,1)S(1)}, u32[]{:S(2)}, u32[]{:S(2)}) collective-permute-start(bf16[256,256]{1,0:T(8,128)(2,1)S(1)} %get-tuple-element.47), channel_id=1, source_target_pairs={{0,1},{1,2},{2,3},{3,0},{4,5},{5,6},{6,7},{7,4},{8,9},{9,10},{10,1... | collective-permute-start | bytes 393224 | tf_op jit(solution)/shard_map/ppermute | solution.py:403
  34.1 10.0 %collective-permute-start.3 = (bf16[256,256]{1,0:T(8,128)(2,1)S(1)}, bf16[256,256]{1,0:T(8,128)(2,1)S(1)}, u32[]{:S(2)}, u32[]{:S(2)}) collective-permute-start(bf16[256,256]{1,0:T(8,128)(2,1)S(1)} %get-tuple-element.48), channel_id=1, source_target_pairs={{0,2},{1,3},{2,0},{3,1},{4,6},{5,7},{6,4},{7,5},{8,10},{9,11},{10,... | collective-permute-start | bytes 393224 | tf_op jit(solution)/shard_map/ppermute | solution.py:403
  37.9 6.9 %collective-permute-start.4 = (bf16[256,256]{1,0:T(8,128)(2,1)S(1)}, bf16[256,256]{1,0:T(8,128)(2,1)S(1)}, u32[]{:S(2)}, u32[]{:S(2)}) collective-permute-start(bf16[256,256]{1,0:T(8,128)(2,1)S(1)} %get-tuple-element.49), channel_id=1, source_target_pairs={{0,3},{1,0},{2,1},{3,2},{4,7},{5,4},{6,5},{7,6},{8,11},{9,8},{10,9... | collective-permute-start | bytes 393224 | tf_op jit(solution)/shard_map/ppermute | solution.py:403
  42.6 5.6 %collective-permute-start.11 = (bf16[288,256]{1,0:T(8,128)(2,1)S(1)}, bf16[288,256]{1,0:T(8,128)(2,1)S(1)}, u32[]{:S(2)}, u32[]{:S(2)}) collective-permute-start(bf16[288,256]{1,0:T(8,128)(2,1)S(1)} %get-tuple-element.59), channel_id=1, source_target_pairs={{0,1},{1,2},{2,3},{3,0},{4,5},{5,6},{6,7},{7,4},{8,9},{9,10},{10,1... | collective-permute-start | bytes 442376 | tf_op jit(solution)/shard_map/ppermute | solution.py:403
  44.1 5.5 %collective-permute-start.12 = (bf16[288,256]{1,0:T(8,128)(2,1)S(1)}, bf16[288,256]{1,0:T(8,128)(2,1)S(1)}, u32[]{:S(2)}, u32[]{:S(2)}) collective-permute-start(bf16[288,256]{1,0:T(8,128)(2,1)S(1)} %get-tuple-element.60), channel_id=1, source_target_pairs={{0,2},{1,3},{2,0},{3,1},{4,6},{5,7},{6,4},{7,5},{8,10},{9,11},{10,... | collective-permute-start | bytes 442376 | tf_op jit(solution)/shard_map/ppermute | solution.py:403
  44.8 5.5 %collective-permute-start.13 = (bf16[288,256]{1,0:T(8,128)(2,1)S(1)}, bf16[288,256]{1,0:T(8,128)(2,1)S(1)}, u32[]{:S(2)}, u32[]{:S(2)}) collective-permute-start(bf16[288,256]{1,0:T(8,128)(2,1)S(1)} %get-tuple-element.61), channel_id=1, source_target_pairs={{0,3},{1,0},{2,1},{3,2},{4,7},{5,4},{6,5},{7,6},{8,11},{9,8},{10,9... | collective-permute-start | bytes 442376 | tf_op jit(solution)/shard_map/ppermute | solution.py:403
  52.1 7.3 %collective-permute-start.16 = (bf16[512,1024]{1,0:T(8,128)(2,1)S(1)}, bf16[512,1024]{1,0:T(8,128)(2,1)S(1)}, u32[]{:S(2)}, u32[]{:S(2)}) collective-permute-start(bf16[512,1024]{1,0:T(8,128)(2,1)S(1)} %get-tuple-element.62.n_ref), channel_id=1, source_target_pairs={{0,4},{4,0},{8,12},{12,8},{1,5},{5,1},{9,13},{13,9},{2,6},{6,2},{1... | collective-permute-start | bytes 3145736 | tf_op jit(solution)/shard_map/ppermute | solution.py:422
  57.1 12.3 %collective-permute-start.14 = (bf16[384,1024]{1,0:T(8,128)(2,1)S(1)}, bf16[384,1024]{1,0:T(8,128)(2,1)S(1)}, u32[]{:S(2)}, u32[]{:S(2)}) collective-permute-start(bf16[384,1024]{1,0:T(8,128)(2,1)S(1)} %get-tuple-element.64), channel_id=1, source_target_pairs={{16,0},{68,4},{32,16},{84,20},{48,32},{100,36},{8,48},{116,52},{24... | collective-permute-start | bytes 2359304 | tf_op jit(solution)/shard_map/ppermute | solution.py:418
  57.1 12.3 %collective-permute-start.15 = (bf16[384,1024]{1,0:T(8,128)(2,1)S(1)}, bf16[384,1024]{1,0:T(8,128)(2,1)S(1)}, u32[]{:S(2)}, u32[]{:S(2)}) collective-permute-start(bf16[384,1024]{1,0:T(8,128)(2,1)S(1)} %get-tuple-element.65), channel_id=1, source_target_pairs={{56,0},{196,4},{0,16},{212,20},{16,32},{228,36},{32,48},{244,52},{... | collective-permute-start | bytes 2359304 | tf_op jit(solution)/shard_map/ppermute | solution.py:418
  71.4 5.9 %collective-permute-start.19 = (bf16[4,512,256]{2,1,0:T(8,128)(2,1)S(1)}, bf16[4,512,256]{2,1,0:T(8,128)(2,1)S(1)}, u32[]{:S(2)}, u32[]{:S(2)}) collective-permute-start(bf16[4,512,256]{2,1,0:T(8,128)(2,1)S(1)} %mlp_last_other.1), channel_id=1, source_target_pairs={{0,4},{4,0},{8,12},{12,8},{1,5},{5,1},{9,13},{13,9},{2,6},{6,2},{1... | collective-permute-start | bytes 3145736 | tf_op jit(solution)/shard_map/ppermute | solution.py:422
  77.0 4.7 %copy-start.3 = (f32[256]{0:T(256)S(1)}, f32[256]{0:T(256)}, u32[]{:S(2)}) copy-start(f32[256]{0:T(256)} %param.19) | copy-start | bytes 3076
  77.0 4.7 %copy-start.4 = (f32[256]{0:T(256)S(1)}, f32[256]{0:T(256)}, u32[]{:S(2)}) copy-start(f32[256]{0:T(256)} %param.18) | copy-start | bytes 3076
  78.1 8.8 %collective-permute-start.20 = (bf16[512,256]{1,0:T(8,128)(2,1)S(1)}, bf16[512,256]{1,0:T(8,128)(2,1)S(1)}, u32[]{:S(2)}, u32[]{:S(2)}) collective-permute-start(bf16[512,256]{1,0:T(8,128)(2,1)S(1)} %get-tuple-element.74), channel_id=1, source_target_pairs={{0,1},{1,2},{2,3},{3,0},{4,5},{5,6},{6,7},{7,4},{8,9},{9,10},{10,1... | collective-permute-start | bytes 786440 | tf_op jit(solution)/shard_map/ppermute | solution.py:403
  78.7 14.7 %collective-permute-start.21 = (bf16[512,256]{1,0:T(8,128)(2,1)S(1)}, bf16[512,256]{1,0:T(8,128)(2,1)S(1)}, u32[]{:S(2)}, u32[]{:S(2)}) collective-permute-start(bf16[512,256]{1,0:T(8,128)(2,1)S(1)} %get-tuple-element.75), channel_id=1, source_target_pairs={{0,2},{1,3},{2,0},{3,1},{4,6},{5,7},{6,4},{7,5},{8,10},{9,11},{10,... | collective-permute-start | bytes 786440 | tf_op jit(solution)/shard_map/ppermute | solution.py:403
  81.7 11.9 %collective-permute-start.22 = (bf16[512,256]{1,0:T(8,128)(2,1)S(1)}, bf16[512,256]{1,0:T(8,128)(2,1)S(1)}, u32[]{:S(2)}, u32[]{:S(2)}) collective-permute-start(bf16[512,256]{1,0:T(8,128)(2,1)S(1)} %get-tuple-element.76), channel_id=1, source_target_pairs={{0,3},{1,0},{2,1},{3,2},{4,7},{5,4},{6,5},{7,6},{8,11},{9,8},{10,9... | collective-permute-start | bytes 786440 | tf_op jit(solution)/shard_map/ppermute | solution.py:403

commit v4 on v3

--- a/solution.py
+++ b/solution.py
@@ -12,7 +12,7 @@
 SM = pl.BlockSpec(memory_space=pltpu.SMEM)
 HB = pl.BlockSpec(memory_space=pl.ANY)
 NT = (((1,), (1,)), ((), ()))
-CB = 32
+CB = 64
 
 
 def params(mib):
@@ -261,11 +261,16 @@
         values += shards_bias(sc, bias, shift)
     for i in range(8):
         bv[i // 4, :, i % 4 * 128 : i % 4 * 128 + 128] = values[i]
-    for copy in copies:
+    for copy in copies[:4]:
         copy.wait()
 
     @pl.loop(0, 4)
     def _(step):
+        @pl.when(step == 2)
+        def _():
+            for copy in copies[4:]:
+                copy.wait()
+
         half, chunk = lax.rem(step, 2), step // 2
         rows = pl.ds(pl.multiple_of(chunk * 512, 512), 512)
         n = jnp.where(half == 0, n_ref[...], n_other[...])

time: 96.1 us -> 96.1 us (level)
  no operation moved by 1% of the time
where the time goes in v4:
time: 96.1 us; the launch traced here: 96 us
  starting transfers between devices  45.3 us (47%)
  Pallas kernels  30.1 us (31%)
  waiting for transfers between devices  17.9 us (19%)
  local copies, waits for them, and re-layouts  1.39 us (1%)
    ppermute x9, waiting for transfers between devices, to_hid(): return lax.ppermute(x, 'hid', [(i, (i + k) % 4) for i in range(4)])  15 us
    pallas_call x4, Pallas kernels, mlp(): pl.pallas_call(kernel, out_shape=jax.ShapeDtypeStruct((4, rows, 256), out...  13.8 us
    ppermute x3, starting transfers between devices, from_core(): return lax.ppermute(v, 'col', [(0, 1), (1, 0), (2, 3), (3, 2)])  11.7 us
    ppermute x9, starting transfers between devices, to_hid(): return lax.ppermute(x, 'hid', [(i, (i + k) % 4) for i in range(4)])  11.6 us
    ppermute x2, starting transfers between devices, around(): lax.ppermute(v, 'row', [(i, (i + (1 if up else -1)) % 16) for i in range(...  7.5 us
    ppermute x1, starting transfers between devices, from_chip(): return lax.ppermute(v, 'col', [(1, 2), (2, 1), (0, 3), (3, 0)])  5.17 us
    ppermute x4, starting transfers between devices, from_hid(): return lax.ppermute(x, 'hid', [((i + k) % 4, i) for i in range(4)])  5.13 us
    pallas_call x1, Pallas kernels, conv_edge(): pl.pallas_call(edge_kernel, out_shape=(o,) * 4, in_specs=[SM] + [VM] * 7,...  4.59 us
  transfers between devices with their start and end apart: 23, of which 9 were waited for; matrix products, arithmetic and copies ran while one was open for 0% of the time, Pallas kernels for 26%

profile of v4, /device:TPU:1, one launch (start us, length us, event | category | flops | bytes accessed | tf_op | source)
XLA Modules:
  0.0 96.0 jit_solution(5258573106065341031)
XLA Ops:
  0.1 1.1 %constant_dynamic-slice_fusion = (bf16[128,1024]{1,0:T(8,128)(2,1)S(1)}, bf16[128,1024]{1,0:T(8,128)(2,1)S(1)}) fusion(bf16[1024,1024]{1,0:T(8,128)(2,1)} %w_out.1, s32[]{:T(128)S(6)} %select_n.36, bf16[1024,1024]{1,0:T(8,128)(2,1)} %w_in.1), kind=kLoop, calls=%fused_computation.9 | loop fusion | bytes 1048580 | tf_op jit(solution)/shard_map/dynamic_slice | solution.py:456
  1.3 0.8 pad_maximum_fusion
  2.1 2.1 %collective-permute-start.6 = (bf16[256,1024]{1,0:T(8,128)(2,1)}, bf16[256,1024]{1,0:T(8,128)(2,1)S(1)}, u32[]{:S(2)}, u32[]{:S(2)}) collective-permute-start(bf16[256,1024]{1,0:T(8,128)(2,1)} %pad_maximum_fusion), channel_id=1, source_target_pairs={{3,0},{0,1},{1,2},{2,3},{7,4},{4,5},{5,6},{6,7},{11,8},{8,9},{9,10... | collective-permute-start | bytes 1572872 | tf_op jit(solution)/shard_map/ppermute | solution.py:404
  4.2 1.4 %collective-permute-start.5 = (bf16[256,1024]{1,0:T(8,128)(2,1)}, bf16[256,1024]{1,0:T(8,128)(2,1)S(1)}, u32[]{:S(2)}, u32[]{:S(2)}) collective-permute-start(bf16[256,1024]{1,0:T(8,128)(2,1)} %pad_maximum_fusion), channel_id=1, source_target_pairs={{1,0},{2,1},{3,2},{0,3},{5,4},{6,5},{7,6},{4,7},{9,8},{10,9},{11,1... | collective-permute-start | bytes 1572872 | tf_op jit(solution)/shard_map/ppermute | solution.py:404
  5.7 0.1 stack.39.sc
  5.7 1.2 %turn.1 = (bf16[16,128,256]{2,1,0:T(8,128)(2,1)S(1)}, bf16[16,768]{1,0:T(8,128)(2,1)S(1)}, bf16[16,768]{1,0:T(8,128)(2,1)S(1)}) custom-call(s32[9]{0:T(128)S(1)} %stack.39.sc, bf16[256,16,128]{2,1,0:T(8,128)(2,1)S(1)} %copy-done), custom_call_target="tpu_custom_call" | custom-call | bytes 4194304 | tf_op jit(solution)/shard_map/turn/pallas_call | solution.py:37
  7.0 3.0 %collective-permute-start = (bf16[16,768]{1,0:T(8,128)(2,1)S(1)}, bf16[16,768]{1,0:T(8,128)(2,1)S(1)}, u32[]{:S(2)}, u32[]{:S(2)}) collective-permute-start(bf16[16,768]{1,0:T(8,128)(2,1)S(1)} %get-tuple-element.42), channel_id=1, source_target_pairs={{0,4},{4,0},{8,12},{12,8},{1,5},{5,1},{9,13},{13,9},{2,6},{6,2},{1... | collective-permute-start | bytes 73736 | tf_op jit(solution)/shard_map/ppermute | solution.py:427
  10.0 5.2 %collective-permute-start.1 = (bf16[16,768]{1,0:T(8,128)(2,1)S(1)}, bf16[16,768]{1,0:T(8,128)(2,1)S(1)}, u32[]{:S(2)}, u32[]{:S(2)}) collective-permute-start(bf16[16,768]{1,0:T(8,128)(2,1)S(1)} %get-tuple-element.43), channel_id=1, source_target_pairs={{4,8},{8,4},{0,12},{12,0},{5,9},{9,5},{1,13},{13,1},{6,10},{10,6},... | collective-permute-start | bytes 73736 | tf_op jit(solution)/shard_map/ppermute | solution.py:435
  15.2 0.1 pad.10.clone
  15.3 0.1 maximum_maximum_fusion.p_ref
  15.4 1.7 %collective-permute-done.1.b_ref = bf16[16,768]{1,0:T(8,128)(2,1)S(1)} collective-permute-done((bf16[16,768]{1,0:T(8,128)(2,1)S(1)}, bf16[16,768]{1,0:T(8,128)(2,1)S(1)}, u32[]{:S(2)}, u32[]{:S(2)}) %collective-permute-start.1) | collective-permute-done | bytes 24608 | tf_op jit(solution)/shard_map/ppermute | solution.py:435
  17.2 0.1 pack.1
  17.2 1.6 %collective-permute-start.9 = (bf16[128,1024]{1,0:T(8,128)(2,1)S(1)}, bf16[128,1024]{1,0:T(8,128)(2,1)S(1)}, u32[]{:S(2)}, u32[]{:S(2)}) collective-permute-start(bf16[128,1024]{1,0:T(8,128)(2,1)S(1)} %get-tuple-element.52), channel_id=1, source_target_pairs={{1,0},{2,1},{3,2},{0,3},{5,4},{6,5},{7,6},{4,7},{9,8},{10,9},{11,1... | collective-permute-start | bytes 786440 | tf_op jit(solution)/shard_map/ppermute | solution.py:404
  18.8 2.6 %collective-permute-start.7 = (bf16[416,256]{1,0:T(8,128)(2,1)S(1)}, bf16[416,256]{1,0:T(8,128)(2,1)S(1)}, u32[]{:S(2)}, u32[]{:S(2)}) collective-permute-start(bf16[416,256]{1,0:T(8,128)(2,1)S(1)} %get-tuple-element.50), channel_id=1, source_target_pairs={{0,16},{16,32},{32,48},{48,64},{64,80},{80,96},{96,112},{112,128},... | collective-permute-start | bytes 638984 | tf_op jit(solution)/shard_map/ppermute | solution.py:431
  21.4 4.9 %collective-permute-start.8 = (bf16[416,256]{1,0:T(8,128)(2,1)S(1)}, bf16[416,256]{1,0:T(8,128)(2,1)S(1)}, u32[]{:S(2)}, u32[]{:S(2)}) collective-permute-start(bf16[416,256]{1,0:T(8,128)(2,1)S(1)} %get-tuple-element.51), channel_id=1, source_target_pairs={{0,240},{16,0},{32,16},{48,32},{64,48},{80,64},{96,80},{112,96},{1... | collective-permute-start | bytes 638984 | tf_op jit(solution)/shard_map/ppermute | solution.py:431
  26.3 4.5 %conv_inner.1 = (bf16[256,256]{1,0:T(8,128)(2,1)S(1)}, bf16[256,256]{1,0:T(8,128)(2,1)S(1)}, bf16[256,256]{1,0:T(8,128)(2,1)S(1)}, bf16[256,256]{1,0:T(8,128)(2,1)S(1)}) custom-call(s32[9]{0:T(128)S(1)} %stack.39.sc, bf16[16,128,256]{2,1,0:T(8,128)(2,1)S(1)} %get-tuple-element.41.xt_ref, bf16[16,768]{1,0:T(8,128)(2,1)S(1)} %collective-permute-done.a_ref, ...), custom_call_target="tpu_custom_call" | custom-call | flops 30000000 | bytes 4194304 | tf_op jit(solution)/shard_map/conv_inner/pallas_call | solution.py:153
  30.9 0.4 join.1
  31.2 0.1 collective-permute-start.18
  31.3 2.7 %collective-permute-start.17 = (bf16[768,1024]{1,0:T(8,128)(2,1)S(1)}, bf16[768,1024]{1,0:T(8,128)(2,1)S(1)}, u32[]{:S(2)}, u32[]{:S(2)}) collective-permute-start(bf16[768,1024]{1,0:T(8,128)(2,1)S(1)} %get-tuple-element.54.held), channel_id=1, source_target_pairs={{64,0},{20,4},{80,16},{36,20},{96,32},{52,36},{112,48},{12,52},{72... | collective-permute-start | bytes 4718600 | tf_op jit(solution)/shard_map/ppermute | solution.py:423
  34.0 3.8 %collective-permute-start.3 = (bf16[256,256]{1,0:T(8,128)(2,1)S(1)}, bf16[256,256]{1,0:T(8,128)(2,1)S(1)}, u32[]{:S(2)}, u32[]{:S(2)}) collective-permute-start(bf16[256,256]{1,0:T(8,128)(2,1)S(1)} %get-tuple-element.48), channel_id=1, source_target_pairs={{0,2},{1,3},{2,0},{3,1},{4,6},{5,7},{6,4},{7,5},{8,10},{9,11},{10,... | collective-permute-start | bytes 393224 | tf_op jit(solution)/shard_map/ppermute | solution.py:408
  37.8 4.6 %conv_edge.1 = (bf16[288,256]{1,0:T(8,128)(2,1)S(1)}, bf16[288,256]{1,0:T(8,128)(2,1)S(1)}, bf16[288,256]{1,0:T(8,128)(2,1)S(1)}, bf16[288,256]{1,0:T(8,128)(2,1)S(1)}) custom-call(s32[9]{0:T(128)S(1)} %stack.39.sc, bf16[16,128,256]{2,1,0:T(8,128)(2,1)S(1)} %get-tuple-element.41.xt_ref, bf16[16,768]{1,0:T(8,128)(2,1)S(1)} %collective-permute-done.a_ref, ...), custom_call_target="tpu_custom_call" | custom-call | flops 30000000 | bytes 4194304 | tf_op jit(solution)/shard_map/conv_edge/pallas_call | solution.py:167
  42.4 1.5 %collective-permute-start.11 = (bf16[288,256]{1,0:T(8,128)(2,1)S(1)}, bf16[288,256]{1,0:T(8,128)(2,1)S(1)}, u32[]{:S(2)}, u32[]{:S(2)}) collective-permute-start(bf16[288,256]{1,0:T(8,128)(2,1)S(1)} %get-tuple-element.59), channel_id=1, source_target_pairs={{0,1},{1,2},{2,3},{3,0},{4,5},{5,6},{6,7},{7,4},{8,9},{9,10},{10,1... | collective-permute-start | bytes 442376 | tf_op jit(solution)/shard_map/ppermute | solution.py:408
  44.0 0.8 collective-permute-start.12
  44.8 1.7 %collective-permute-start.13 = (bf16[288,256]{1,0:T(8,128)(2,1)S(1)}, bf16[288,256]{1,0:T(8,128)(2,1)S(1)}, u32[]{:S(2)}, u32[]{:S(2)}) collective-permute-start(bf16[288,256]{1,0:T(8,128)(2,1)S(1)} %get-tuple-element.61), channel_id=1, source_target_pairs={{0,3},{1,0},{2,1},{3,2},{4,7},{5,4},{6,5},{7,6},{8,11},{9,8},{10,9... | collective-permute-start | bytes 442376 | tf_op jit(solution)/shard_map/ppermute | solution.py:408
  46.5 1.5 %collective-permute-done.11.e1 = bf16[288,256]{1,0:T(8,128)(2,1)S(1)} collective-permute-done((bf16[288,256]{1,0:T(8,128)(2,1)S(1)}, bf16[288,256]{1,0:T(8,128)(2,1)S(1)}, u32[]{:S(2)}, u32[]{:S(2)}) %collective-permute-start.11) | collective-permute-done | bytes 147488 | tf_op jit(solution)/shard_map/ppermute | solution.py:408
  48.0 1.5 %collective-permute-done.12.e2 = bf16[288,256]{1,0:T(8,128)(2,1)S(1)} collective-permute-done((bf16[288,256]{1,0:T(8,128)(2,1)S(1)}, bf16[288,256]{1,0:T(8,128)(2,1)S(1)}, u32[]{:S(2)}, u32[]{:S(2)}) %collective-permute-start.12) | collective-permute-done | bytes 147488 | tf_op jit(solution)/shard_map/ppermute | solution.py:408
  49.5 0.7 collective-permute-done.13.e3
  50.2 1.8 %norm.1 = (bf16[512,1024]{1,0:T(8,128)(2,1)S(1)}, f32[4,8,1,128]{3,2,1,0:T(1,128)S(1)}) custom-call(s32[9]{0:T(128)S(1)} %stack.39.sc, bf16[256,256]{1,0:T(8,128)(2,1)S(1)} %get-tuple-element.46._.i0, bf16[256,256]{1,0:T(8,128)(2,1)S(1)} %collective-permute-done.2.i1, bf16[256,256]{1,0:T(8,128)(2,1)S(1)} %collective-permute-done.3.i2, ...), custom_call_target="tpu_custom_call" | custom-call | flops 8388608 | bytes 2097152 | tf_op jit(solution)/shard_map/norm/pallas_call | solution.py:211
  52.0 5.0 %collective-permute-start.16 = (bf16[512,1024]{1,0:T(8,128)(2,1)S(1)}, bf16[512,1024]{1,0:T(8,128)(2,1)S(1)}, u32[]{:S(2)}, u32[]{:S(2)}) collective-permute-start(bf16[512,1024]{1,0:T(8,128)(2,1)S(1)} %get-tuple-element.62.n_ref), channel_id=1, source_target_pairs={{0,4},{4,0},{8,12},{12,8},{1,5},{5,1},{9,13},{13,9},{2,6},{6,2},{1... | collective-permute-start | bytes 3145736 | tf_op jit(solution)/shard_map/ppermute | solution.py:427
  57.0 1.5 %collective-permute-start.15 = (bf16[384,1024]{1,0:T(8,128)(2,1)S(1)}, bf16[384,1024]{1,0:T(8,128)(2,1)S(1)}, u32[]{:S(2)}, u32[]{:S(2)}) collective-permute-start(bf16[384,1024]{1,0:T(8,128)(2,1)S(1)} %get-tuple-element.65), channel_id=1, source_target_pairs={{56,0},{196,4},{0,16},{212,20},{16,32},{228,36},{32,48},{244,52},{... | collective-permute-start | bytes 2359304 | tf_op jit(solution)/shard_map/ppermute | solution.py:423
  58.5 0.8 collective-permute-done.16.n_other.n_ref
  59.3 3.4 %mlp_first.1.acc = f32[4,1024,256]{2,1,0:T(8,128)S(1)} custom-call(s32[9]{0:T(128)S(1)} %stack.39.sc, bf16[512,1024]{1,0:T(8,128)(2,1)S(1)} %get-tuple-element.62.n_ref, bf16[512,1024]{1,0:T(8,128)(2,1)S(1)} %collective-permute-done.16.n_other.n_ref, f32[4,8,1,128]{3,2,1,0:T(1,128)S(1)} %get-tuple-element.63.bias, bf16[1024,1024]{1,0:T(8,128)(2,1)S(1)} %copy-done.2, ...), custom_call_target="tpu_custom_call" | custom-call | flops 2097152000 | bytes 6291456 | tf_op jit(solution)/shard_map/mlp_first/pallas_call | solution.py:301
  62.7 6.6 %mlp_mid.1.acc = f32[4,1024,256]{2,1,0:T(8,128)S(1)} custom-call(s32[9]{0:T(128)S(1)} %stack.39.sc, bf16[512,1024]{1,0:T(8,128)(2,1)S(1)} %get-tuple-element.62.n_ref, bf16[512,1024]{1,0:T(8,128)(2,1)S(1)} %collective-permute-done.16.n_other.n_ref, f32[4,8,1,128]{3,2,1,0:T(1,128)S(1)} %get-tuple-element.63.bias, f32[4,1024,256]{2,1,0:T(8,128)S(1)} %mlp_first.1.acc, ...), custom_call_target="tpu_custom_call" | custom-call | flops 4194304000 | bytes 6291456 | tf_op jit(solution)/shard_map/mlp_mid/pallas_call | solution.py:301
  69.3 0.1 collective-permute-done.15.high
  69.3 1.9 %mlp_last_other.1 = bf16[4,512,256]{2,1,0:T(8,128)(2,1)S(1)} custom-call(s32[9]{0:T(128)S(1)} %stack.39.sc, bf16[512,1024]{1,0:T(8,128)(2,1)S(1)} %collective-permute-done.16.n_other.n_ref, f32[4,8,1,128]{3,2,1,0:T(1,128)S(1)} %get-tuple-element.63.bias, f32[4,1024,256]{2,1,0:T(8,128)S(1)} %mlp_mid.1.acc, ...), custom_call_target="tpu_custom_call" | custom-call | flops 1048576000 | bytes 6291456 | tf_op jit(solution)/shard_map/mlp_last_other/pallas_call | solution.py:301
  71.3 3.8 %collective-permute-start.19 = (bf16[4,512,256]{2,1,0:T(8,128)(2,1)S(1)}, bf16[4,512,256]{2,1,0:T(8,128)(2,1)S(1)}, u32[]{:S(2)}, u32[]{:S(2)}) collective-permute-start(bf16[4,512,256]{2,1,0:T(8,128)(2,1)S(1)} %mlp_last_other.1), channel_id=1, source_target_pairs={{0,4},{4,0},{8,12},{12,8},{1,5},{5,1},{9,13},{13,9},{2,6},{6,2},{1... | collective-permute-start | bytes 3145736 | tf_op jit(solution)/shard_map/ppermute | solution.py:427
  75.1 1.9 %mlp_last.1.acc = f32[4,512,256]{2,1,0:T(8,128)S(1)} custom-call(s32[9]{0:T(128)S(1)} %stack.39.sc, bf16[512,1024]{1,0:T(8,128)(2,1)S(1)} %get-tuple-element.62.n_ref, f32[4,8,1,128]{3,2,1,0:T(1,128)S(1)} %get-tuple-element.63.bias, f32[4,1024,256]{2,1,0:T(8,128)S(1)} %mlp_mid.1.acc, bf16[768,1024]{1,0:T(8,128)(2,1)S(1)} %collective-permute-done.18.minus, ...), custom_call_target="tpu_custom_call" | custom-call | flops 1048576000 | bytes 6291456 | tf_op jit(solution)/shard_map/mlp_last/pallas_call | solution.py:301
  77.0 0.3 collective-permute-done.19.other
  77.4 0.7 add.38
  78.1 0.5 collective-permute-start.20
  78.6 3.2 %collective-permute-start.21 = (bf16[512,256]{1,0:T(8,128)(2,1)S(1)}, bf16[512,256]{1,0:T(8,128)(2,1)S(1)}, u32[]{:S(2)}, u32[]{:S(2)}) collective-permute-start(bf16[512,256]{1,0:T(8,128)(2,1)S(1)} %get-tuple-element.75), channel_id=1, source_target_pairs={{0,2},{1,3},{2,0},{3,1},{4,6},{5,7},{6,4},{7,5},{8,10},{9,11},{10,... | collective-permute-start | bytes 786440 | tf_op jit(solution)/shard_map/ppermute | solution.py:408
  81.7 0.2 spread.4.s0
  81.9 4.9 %collective-permute-done.20.f = bf16[512,256]{1,0:T(8,128)(2,1)S(1)} collective-permute-done((bf16[512,256]{1,0:T(8,128)(2,1)S(1)}, bf16[512,256]{1,0:T(8,128)(2,1)S(1)}, u32[]{:S(2)}, u32[]{:S(2)}) %collective-permute-start.20) | collective-permute-done | bytes 262176 | tf_op jit(solution)/shard_map/ppermute | solution.py:408
  86.9 0.2 spread.5.s1
  87.1 6.3 %collective-permute-done.21.f = bf16[512,256]{1,0:T(8,128)(2,1)S(1)} collective-permute-done((bf16[512,256]{1,0:T(8,128)(2,1)S(1)}, bf16[512,256]{1,0:T(8,128)(2,1)S(1)}, u32[]{:S(2)}, u32[]{:S(2)}) %collective-permute-start.21) | collective-permute-done | bytes 262176 | tf_op jit(solution)/shard_map/ppermute | solution.py:408
  93.4 0.2 spread.6.s2
  93.6 0.2 spread.7.s3
  93.8 2.2 %final.1 = bf16[256,16,128]{2,1,0:T(8,128)(2,1)} custom-call(s32[9]{0:T(128)S(1)} %stack.39.sc, bf16[256,16,128]{2,1,0:T(8,128)(2,1)S(1)} %copy-done, f32[4,256,128]{2,1,0:T(8,128)S(1)} %spread.4.s0, f32[4,256,128]{2,1,0:T(8,128)S(1)} %spread.5.s1, f32[4,256,128]{2,1,0:T(8,128)S(1)} %spread.6.s2, f32[4,256,128]{2,1,0:T(8,128)S(1)} %spread.7.s3), custom_call_target="tpu_custom_call" | custom-call | flops 1048576 | bytes 4194304 | tf_op jit(solution)/shard_map/final/pallas_call | solution.py:391
  (45 shorter events, 0.2 us)
Async XLA Ops:
  0.0 5.7 %copy-start = (bf16[256,16,128]{2,1,0:T(8,128)(2,1)S(1)}, bf16[256,16,128]{2,1,0:T(8,128)(2,1)}, u32[]{:S(2)}) copy-start(bf16[256,16,128]{2,1,0:T(8,128)(2,1)} %x_ref.3) | copy-start | bytes 3145732
  0.0 15.1 %copy-start.6 = (f32[1024]{0:T(1024)S(1)}, f32[1024]{0:T(1024)}, u32[]{:S(2)}) copy-start(f32[1024]{0:T(1024)} %param.16) | copy-start | bytes 12292
  0.0 15.1 %copy-start.7 = (f32[256]{0:T(256)S(1)}, f32[256]{0:T(256)}, u32[]{:S(2)}) copy-start(f32[256]{0:T(256)} %param.14) | copy-start | bytes 3076
  0.0 15.1 %copy-start.8 = (f32[256]{0:T(256)S(1)}, f32[256]{0:T(256)}, u32[]{:S(2)}) copy-start(f32[256]{0:T(256)} %param.13) | copy-start | bytes 3076
  0.0 15.1 %copy-start.9 = (f32[256]{0:T(256)S(1)}, f32[256]{0:T(256)}, u32[]{:S(2)}) copy-start(f32[256]{0:T(256)} %param.12) | copy-start | bytes 3076
  0.0 15.3 %copy-start.5 = (f32[256,7,7]{0,2,1:T(8,128)S(1)}, f32[256,7,7]{0,2,1:T(8,128)}, u32[]{:S(2)}) copy-start(f32[256,7,7]{0,2,1:T(8,128)} %param.11) | copy-start | bytes 150532
  2.1 15.1 %collective-permute-start.6 = (bf16[256,1024]{1,0:T(8,128)(2,1)}, bf16[256,1024]{1,0:T(8,128)(2,1)S(1)}, u32[]{:S(2)}, u32[]{:S(2)}) collective-permute-start(bf16[256,1024]{1,0:T(8,128)(2,1)} %pad_maximum_fusion), channel_id=1, source_target_pairs={{3,0},{0,1},{1,2},{2,3},{7,4},{4,5},{5,6},{6,7},{11,8},{8,9},{9,10... | collective-permute-start | bytes 1572872 | tf_op jit(solution)/shard_map/ppermute | solution.py:404
  4.2 13.0 %collective-permute-start.5 = (bf16[256,1024]{1,0:T(8,128)(2,1)}, bf16[256,1024]{1,0:T(8,128)(2,1)S(1)}, u32[]{:S(2)}, u32[]{:S(2)}) collective-permute-start(bf16[256,1024]{1,0:T(8,128)(2,1)} %pad_maximum_fusion), channel_id=1, source_target_pairs={{1,0},{2,1},{3,2},{0,3},{5,4},{6,5},{7,6},{4,7},{9,8},{10,9},{11,1... | collective-permute-start | bytes 1572872 | tf_op jit(solution)/shard_map/ppermute | solution.py:404
  7.0 10.2 %collective-permute-start = (bf16[16,768]{1,0:T(8,128)(2,1)S(1)}, bf16[16,768]{1,0:T(8,128)(2,1)S(1)}, u32[]{:S(2)}, u32[]{:S(2)}) collective-permute-start(bf16[16,768]{1,0:T(8,128)(2,1)S(1)} %get-tuple-element.42), channel_id=1, source_target_pairs={{0,4},{4,0},{8,12},{12,8},{1,5},{5,1},{9,13},{13,9},{2,6},{6,2},{1... | collective-permute-start | bytes 73736 | tf_op jit(solution)/shard_map/ppermute | solution.py:427
  10.0 7.2 %collective-permute-start.1 = (bf16[16,768]{1,0:T(8,128)(2,1)S(1)}, bf16[16,768]{1,0:T(8,128)(2,1)S(1)}, u32[]{:S(2)}, u32[]{:S(2)}) collective-permute-start(bf16[16,768]{1,0:T(8,128)(2,1)S(1)} %get-tuple-element.43), channel_id=1, source_target_pairs={{4,8},{8,4},{0,12},{12,0},{5,9},{9,5},{1,13},{13,1},{6,10},{10,6},... | collective-permute-start | bytes 73736 | tf_op jit(solution)/shard_map/ppermute | solution.py:435
  17.2 13.6 %collective-permute-start.9 = (bf16[128,1024]{1,0:T(8,128)(2,1)S(1)}, bf16[128,1024]{1,0:T(8,128)(2,1)S(1)}, u32[]{:S(2)}, u32[]{:S(2)}) collective-permute-start(bf16[128,1024]{1,0:T(8,128)(2,1)S(1)} %get-tuple-element.52), channel_id=1, source_target_pairs={{1,0},{2,1},{3,2},{0,3},{5,4},{6,5},{7,6},{4,7},{9,8},{10,9},{11,1... | collective-permute-start | bytes 786440 | tf_op jit(solution)/shard_map/ppermute | solution.py:404
  18.8 12.0 %collective-permute-start.10 = (bf16[128,1024]{1,0:T(8,128)(2,1)S(1)}, bf16[128,1024]{1,0:T(8,128)(2,1)S(1)}, u32[]{:S(2)}, u32[]{:S(2)}) collective-permute-start(bf16[128,1024]{1,0:T(8,128)(2,1)S(1)} %get-tuple-element.53), channel_id=1, source_target_pairs={{3,0},{0,1},{1,2},{2,3},{7,4},{4,5},{5,6},{6,7},{11,8},{8,9},{9,10... | collective-permute-start | bytes 786440 | tf_op jit(solution)/shard_map/ppermute | solution.py:404
  18.8 15.2 %collective-permute-start.7 = (bf16[416,256]{1,0:T(8,128)(2,1)S(1)}, bf16[416,256]{1,0:T(8,128)(2,1)S(1)}, u32[]{:S(2)}, u32[]{:S(2)}) collective-permute-start(bf16[416,256]{1,0:T(8,128)(2,1)S(1)} %get-tuple-element.50), channel_id=1, source_target_pairs={{0,16},{16,32},{32,48},{48,64},{64,80},{80,96},{96,112},{112,128},... | collective-permute-start | bytes 638984 | tf_op jit(solution)/shard_map/ppermute | solution.py:431
  21.4 16.4 %collective-permute-start.8 = (bf16[416,256]{1,0:T(8,128)(2,1)S(1)}, bf16[416,256]{1,0:T(8,128)(2,1)S(1)}, u32[]{:S(2)}, u32[]{:S(2)}) collective-permute-start(bf16[416,256]{1,0:T(8,128)(2,1)S(1)} %get-tuple-element.51), channel_id=1, source_target_pairs={{0,240},{16,0},{32,16},{48,32},{64,48},{80,64},{96,80},{112,96},{1... | collective-permute-start | bytes 638984 | tf_op jit(solution)/shard_map/ppermute | solution.py:431
  30.8 28.5 %copy-start.1 = (bf16[1024,1024]{1,0:T(8,128)(2,1)S(1)}, bf16[1024,1024]{1,0:T(8,128)(2,1)}, u32[]{:S(2)}) copy-start(bf16[1024,1024]{1,0:T(8,128)(2,1)} %w_out.1) | copy-start | bytes 6291460
  30.8 28.4 %copy-start.2 = (bf16[1024,1024]{1,0:T(8,128)(2,1)S(1)}, bf16[1024,1024]{1,0:T(8,128)(2,1)}, u32[]{:S(2)}) copy-start(bf16[1024,1024]{1,0:T(8,128)(2,1)} %w_in.1) | copy-start | bytes 6291460
  31.2 31.4 %collective-permute-start.18 = (bf16[768,1024]{1,0:T(8,128)(2,1)S(1)}, bf16[768,1024]{1,0:T(8,128)(2,1)S(1)}, u32[]{:S(2)}, u32[]{:S(2)}) collective-permute-start(bf16[768,1024]{1,0:T(8,128)(2,1)S(1)} %get-tuple-element.54.held), channel_id=1, source_target_pairs={{192,0},{60,4},{208,16},{4,20},{224,32},{20,36},{240,48},{36,52},{... | collective-permute-start | bytes 4718600 | tf_op jit(solution)/shard_map/ppermute | solution.py:423
  31.3 31.4 %collective-permute-start.17 = (bf16[768,1024]{1,0:T(8,128)(2,1)S(1)}, bf16[768,1024]{1,0:T(8,128)(2,1)S(1)}, u32[]{:S(2)}, u32[]{:S(2)}) collective-permute-start(bf16[768,1024]{1,0:T(8,128)(2,1)S(1)} %get-tuple-element.54.held), channel_id=1, source_target_pairs={{64,0},{20,4},{80,16},{36,20},{96,32},{52,36},{112,48},{12,52},{72... | collective-permute-start | bytes 4718600 | tf_op jit(solution)/shard_map/ppermute | solution.py:423
  34.0 8.5 %collective-permute-start.2 = (bf16[256,256]{1,0:T(8,128)(2,1)S(1)}, bf16[256,256]{1,0:T(8,128)(2,1)S(1)}, u32[]{:S(2)}, u32[]{:S(2)}) collective-permute-start(bf16[256,256]{1,0:T(8,128)(2,1)S(1)} %get-tuple-element.47), channel_id=1, source_target_pairs={{0,1},{1,2},{2,3},{3,0},{4,5},{5,6},{6,7},{7,4},{8,9},{9,10},{10,1... | collective-permute-start | bytes 393224 | tf_op jit(solution)/shard_map/ppermute | solution.py:408
  34.0 10.0 %collective-permute-start.3 = (bf16[256,256]{1,0:T(8,128)(2,1)S(1)}, bf16[256,256]{1,0:T(8,128)(2,1)S(1)}, u32[]{:S(2)}, u32[]{:S(2)}) collective-permute-start(bf16[256,256]{1,0:T(8,128)(2,1)S(1)} %get-tuple-element.48), channel_id=1, source_target_pairs={{0,2},{1,3},{2,0},{3,1},{4,6},{5,7},{6,4},{7,5},{8,10},{9,11},{10,... | collective-permute-start | bytes 393224 | tf_op jit(solution)/shard_map/ppermute | solution.py:408
  37.8 6.9 %collective-permute-start.4 = (bf16[256,256]{1,0:T(8,128)(2,1)S(1)}, bf16[256,256]{1,0:T(8,128)(2,1)S(1)}, u32[]{:S(2)}, u32[]{:S(2)}) collective-permute-start(bf16[256,256]{1,0:T(8,128)(2,1)S(1)} %get-tuple-element.49), channel_id=1, source_target_pairs={{0,3},{1,0},{2,1},{3,2},{4,7},{5,4},{6,5},{7,6},{8,11},{9,8},{10,9... | collective-permute-start | bytes 393224 | tf_op jit(solution)/shard_map/ppermute | solution.py:408
  42.4 5.6 %collective-permute-start.11 = (bf16[288,256]{1,0:T(8,128)(2,1)S(1)}, bf16[288,256]{1,0:T(8,128)(2,1)S(1)}, u32[]{:S(2)}, u32[]{:S(2)}) collective-permute-start(bf16[288,256]{1,0:T(8,128)(2,1)S(1)} %get-tuple-element.59), channel_id=1, source_target_pairs={{0,1},{1,2},{2,3},{3,0},{4,5},{5,6},{6,7},{7,4},{8,9},{9,10},{10,1... | collective-permute-start | bytes 442376 | tf_op jit(solution)/shard_map/ppermute | solution.py:408
  44.0 5.5 %collective-permute-start.12 = (bf16[288,256]{1,0:T(8,128)(2,1)S(1)}, bf16[288,256]{1,0:T(8,128)(2,1)S(1)}, u32[]{:S(2)}, u32[]{:S(2)}) collective-permute-start(bf16[288,256]{1,0:T(8,128)(2,1)S(1)} %get-tuple-element.60), channel_id=1, source_target_pairs={{0,2},{1,3},{2,0},{3,1},{4,6},{5,7},{6,4},{7,5},{8,10},{9,11},{10,... | collective-permute-start | bytes 442376 | tf_op jit(solution)/shard_map/ppermute | solution.py:408
  44.8 5.4 %collective-permute-start.13 = (bf16[288,256]{1,0:T(8,128)(2,1)S(1)}, bf16[288,256]{1,0:T(8,128)(2,1)S(1)}, u32[]{:S(2)}, u32[]{:S(2)}) collective-permute-start(bf16[288,256]{1,0:T(8,128)(2,1)S(1)} %get-tuple-element.61), channel_id=1, source_target_pairs={{0,3},{1,0},{2,1},{3,2},{4,7},{5,4},{6,5},{7,6},{8,11},{9,8},{10,9... | collective-permute-start | bytes 442376 | tf_op jit(solution)/shard_map/ppermute | solution.py:408
  52.0 7.3 %collective-permute-start.16 = (bf16[512,1024]{1,0:T(8,128)(2,1)S(1)}, bf16[512,1024]{1,0:T(8,128)(2,1)S(1)}, u32[]{:S(2)}, u32[]{:S(2)}) collective-permute-start(bf16[512,1024]{1,0:T(8,128)(2,1)S(1)} %get-tuple-element.62.n_ref), channel_id=1, source_target_pairs={{0,4},{4,0},{8,12},{12,8},{1,5},{5,1},{9,13},{13,9},{2,6},{6,2},{1... | collective-permute-start | bytes 3145736 | tf_op jit(solution)/shard_map/ppermute | solution.py:427
  57.0 12.3 %collective-permute-start.14 = (bf16[384,1024]{1,0:T(8,128)(2,1)S(1)}, bf16[384,1024]{1,0:T(8,128)(2,1)S(1)}, u32[]{:S(2)}, u32[]{:S(2)}) collective-permute-start(bf16[384,1024]{1,0:T(8,128)(2,1)S(1)} %get-tuple-element.64), channel_id=1, source_target_pairs={{16,0},{68,4},{32,16},{84,20},{48,32},{100,36},{8,48},{116,52},{24... | collective-permute-start | bytes 2359304 | tf_op jit(solution)/shard_map/ppermute | solution.py:423
  57.0 12.3 %collective-permute-start.15 = (bf16[384,1024]{1,0:T(8,128)(2,1)S(1)}, bf16[384,1024]{1,0:T(8,128)(2,1)S(1)}, u32[]{:S(2)}, u32[]{:S(2)}) collective-permute-start(bf16[384,1024]{1,0:T(8,128)(2,1)S(1)} %get-tuple-element.65), channel_id=1, source_target_pairs={{56,0},{196,4},{0,16},{212,20},{16,32},{228,36},{32,48},{244,52},{... | collective-permute-start | bytes 2359304 | tf_op jit(solution)/shard_map/ppermute | solution.py:423
  71.3 6.0 %collective-permute-start.19 = (bf16[4,512,256]{2,1,0:T(8,128)(2,1)S(1)}, bf16[4,512,256]{2,1,0:T(8,128)(2,1)S(1)}, u32[]{:S(2)}, u32[]{:S(2)}) collective-permute-start(bf16[4,512,256]{2,1,0:T(8,128)(2,1)S(1)} %mlp_last_other.1), channel_id=1, source_target_pairs={{0,4},{4,0},{8,12},{12,8},{1,5},{5,1},{9,13},{13,9},{2,6},{6,2},{1... | collective-permute-start | bytes 3145736 | tf_op jit(solution)/shard_map/ppermute | solution.py:427
  77.0 4.7 %copy-start.3 = (f32[256]{0:T(256)S(1)}, f32[256]{0:T(256)}, u32[]{:S(2)}) copy-start(f32[256]{0:T(256)} %param.19) | copy-start | bytes 3076
  77.0 4.7 %copy-start.4 = (f32[256]{0:T(256)S(1)}, f32[256]{0:T(256)}, u32[]{:S(2)}) copy-start(f32[256]{0:T(256)} %param.18) | copy-start | bytes 3076
  78.1 8.8 %collective-permute-start.20 = (bf16[512,256]{1,0:T(8,128)(2,1)S(1)}, bf16[512,256]{1,0:T(8,128)(2,1)S(1)}, u32[]{:S(2)}, u32[]{:S(2)}) collective-permute-start(bf16[512,256]{1,0:T(8,128)(2,1)S(1)} %get-tuple-element.74), channel_id=1, source_target_pairs={{0,1},{1,2},{2,3},{3,0},{4,5},{5,6},{6,7},{7,4},{8,9},{9,10},{10,1... | collective-permute-start | bytes 786440 | tf_op jit(solution)/shard_map/ppermute | solution.py:408
  78.6 14.8 %collective-permute-start.21 = (bf16[512,256]{1,0:T(8,128)(2,1)S(1)}, bf16[512,256]{1,0:T(8,128)(2,1)S(1)}, u32[]{:S(2)}, u32[]{:S(2)}) collective-permute-start(bf16[512,256]{1,0:T(8,128)(2,1)S(1)} %get-tuple-element.75), channel_id=1, source_target_pairs={{0,2},{1,3},{2,0},{3,1},{4,6},{5,7},{6,4},{7,5},{8,10},{9,11},{10,... | collective-permute-start | bytes 786440 | tf_op jit(solution)/shard_map/ppermute | solution.py:408
  81.7 11.9 %collective-permute-start.22 = (bf16[512,256]{1,0:T(8,128)(2,1)S(1)}, bf16[512,256]{1,0:T(8,128)(2,1)S(1)}, u32[]{:S(2)}, u32[]{:S(2)}) collective-permute-start(bf16[512,256]{1,0:T(8,128)(2,1)S(1)} %get-tuple-element.76), channel_id=1, source_target_pairs={{0,3},{1,0},{2,1},{3,2},{4,7},{5,4},{6,5},{7,6},{8,11},{9,8},{10,9... | collective-permute-start | bytes 786440 | tf_op jit(solution)/shard_map/ppermute | solution.py:408
